TPU v7x, 32 devices: a whole 2x2x4 slice. The times are simulated.
32 devices in a mesh: dp: 16 (over z, x, core), fsdp: 2 (over y).
Axes of the slice: x: 2, y: 2, z: 4, core: 2. Of those that a mesh axis runs over, the one named last changes fastest.
Arguments:
- tokens: bfloat16 [16, 1024, 1536], P('dp', 'fsdp'), may hold values from -6 to 6
- caption: bfloat16 [16, 256, 4096], P('dp', None, 'fsdp'), may hold values from -6 to 6
- modulation: bfloat16 [16, 6, 1536], P('dp', None, 'fsdp'), may hold values from -4 to 4
- caption_mask: int32 [16, 256], P('dp'), may hold values from 0 to 1, as said below
- positions: int32 [16, 2, 1024], P('dp', None, 'fsdp'), may hold values from 0 to 63, as said below
- w_qkv: bfloat16 [1536, 4608], P('fsdp'), may hold values from -0.15625 to 0.15625
- w_out: bfloat16 [1536, 1536], P('fsdp'), may hold values from -0.15625 to 0.15625
- w_caption_kv: bfloat16 [4096, 3072], P('fsdp'), may hold values from -0.09375 to 0.09375
- w_gate_up: bfloat16 [1536, 8192], P('fsdp'), may hold values from -0.15625 to 0.15625
- w_down: bfloat16 [4096, 1536], P('fsdp'), may hold values from -0.09375 to 0.09375
- norm_gains: bfloat16 [6, 1536], P(None, 'fsdp'), may hold values from 0.099609375 to 1.8984375
- caption_gain: bfloat16 [1536], P('fsdp'), may hold values from 0.099609375 to 1.8984375
- cross_gate: bfloat16 [24], P('fsdp'), may hold values from -1.5 to 1.5
- cotangent: bfloat16 [16, 1024, 1536], P('dp', 'fsdp'), may hold values from -6 to 6
Outputs:
- block_out: bfloat16 [16, 1024, 1536], P('dp', 'fsdp')
- grad_tokens: bfloat16 [16, 1024, 1536], P('dp', 'fsdp')
- grad_caption: bfloat16 [16, 256, 4096], P('dp', None, 'fsdp')
- grad_modulation: float32 [16, 6, 1536], P('dp', None, 'fsdp')
- grad_w_qkv: float32 [1536, 4608], P('fsdp', 'dp')
- grad_w_out: float32 [1536, 1536], P('fsdp', 'dp')
- grad_w_caption_kv: float32 [4096, 3072], P('fsdp', 'dp')
- grad_w_gate_up: float32 [1536, 8192], P('fsdp', 'dp')
- grad_w_down: float32 [4096, 1536], P('fsdp', 'dp')
- grad_norm_gains: float32 [6, 1536], P(None, 'fsdp')
- grad_caption_gain: float32 [1536], P('fsdp')
- grad_cross_gate: float32 [24], P('fsdp')
Inputs may be any that keep to these rules, and one draw needn't show every extreme that they name: `caption_mask`: each image's row holds ones for its first n slots and zeros after them, with 8 <= n <= 256; some image has n = 256 and some has n = 8. Image i lies on a grid of W_i columns, W_i one of 16, 32, 64: positions[i,0,t] = t // W_i and positions[i,1,t] = t % W_i; both 16 and 64 occur.
All inputs are finite; a program needn't handle non-finite values.
Results may differ from a plain program's by a relative error of at most 0.029.
Values may be sent and summed in bfloat16 or wider, within the bound.
No kernel may reach another device: no remote copies, remote signals or barrier semaphores. Data moves between devices by JAX's collectives and lax.ppermute only.
A program may use at most 512 MiB of HBM per device.

v0:
```python
import jax
import jax.numpy as jnp
from jax import lax
from jax.sharding import PartitionSpec as P

D = 1536
HEADS = 24
HEAD_DIM = 64
FF = 4096


EPS = 1e-05


def rms_scale(values):
    return lax.rsqrt(jnp.mean(values * values, axis=-1, keepdims=True) + EPS)


def norm_back(grad_normed, values, inv_rms, gain_row):
    scaled_grad = grad_normed * gain_row
    grad_values = inv_rms * scaled_grad - values * inv_rms**3 * jnp.mean(
        scaled_grad * values, axis=-1, keepdims=True
    )
    return (grad_values, grad_normed * values * inv_rms)


def rope_tables(positions):
    quarter = HEAD_DIM // 4
    frequency = 10000.0 ** (-jnp.arange(quarter, dtype=jnp.float32) / quarter)
    row_angles = positions[..., 0, :].astype(jnp.float32)[..., None] * frequency
    col_angles = positions[..., 1, :].astype(jnp.float32)[..., None] * frequency
    angles = jnp.concatenate([row_angles, col_angles], axis=-1)[..., None, :]
    return (jnp.cos(angles), jnp.sin(angles))


def rotate(values, cosine, sine_table):
    quarter = HEAD_DIM // 4
    shaped = values.reshape(values.shape[:-1] + (HEADS, HEAD_DIM))
    front_part = jnp.concatenate(
        [shaped[..., :quarter], shaped[..., 2 * quarter : 3 * quarter]], axis=-1
    )
    back_part = jnp.concatenate(
        [shaped[..., quarter : 2 * quarter], shaped[..., 3 * quarter :]], axis=-1
    )
    new_front = front_part * cosine - back_part * sine_table
    new_back = front_part * sine_table + back_part * cosine
    joined = jnp.concatenate(
        [
            new_front[..., :quarter],
            new_back[..., :quarter],
            new_front[..., quarter:],
            new_back[..., quarter:],
        ],
        axis=-1,
    )
    return joined.reshape(values.shape)


def project_tokens(inputs, full_qkv, gain_rows, mod_rows, cosine, sine_table):
    input_scale = rms_scale(inputs)
    hidden = inputs * input_scale * gain_rows[0]
    modulated = (hidden * (1.0 + mod_rows[:, 1][:, None, :]) + mod_rows[:, 0][:, None, :]).astype(
        jnp.bfloat16
    )
    mixed = jnp.einsum("brd,de->bre", modulated, full_qkv, preferred_element_type=jnp.float32)
    query_pre = mixed[..., :D]
    key_pre = mixed[..., D : 2 * D]
    query_scale = rms_scale(query_pre)
    key_scale = rms_scale(key_pre)
    query_b = rotate(query_pre * query_scale * gain_rows[1], cosine, sine_table).astype(
        jnp.bfloat16
    )
    key_b = rotate(key_pre * key_scale * gain_rows[2], cosine, sine_table).astype(jnp.bfloat16)
    value_b = mixed[..., 2 * D :].astype(jnp.bfloat16)
    own_kv = jnp.concatenate([key_b, value_b], axis=-1)
    return (
        hidden,
        input_scale,
        modulated,
        query_pre,
        query_scale,
        key_pre,
        key_scale,
        query_b,
        own_kv,
    )


def ffn_front(middle, full_gate_up, gain_rows, mod_rows):
    ffn_scale = rms_scale(middle)
    ffn_hidden = middle * ffn_scale * gain_rows[4]
    ffn_in = (ffn_hidden * (1.0 + mod_rows[:, 4][:, None, :]) + mod_rows[:, 3][:, None, :]).astype(
        jnp.bfloat16
    )
    gate_up = jnp.einsum("brd,de->bre", ffn_in, full_gate_up, preferred_element_type=jnp.float32)
    gate_part = gate_up[..., :FF]
    up_part = gate_up[..., FF:]
    ffn_inner = (jax.nn.silu(gate_part) * up_part).astype(jnp.bfloat16)
    return (ffn_hidden, ffn_scale, ffn_in, gate_part, up_part, ffn_inner)


def cross_weights(query_h, caption_keys, mask_row):
    ckey_h = caption_keys[:, :D].reshape(-1, HEADS, HEAD_DIM)
    scores = jnp.einsum(
        "qhd,khd->hqk", query_h, ckey_h, preferred_element_type=jnp.float32
    ) * HEAD_DIM ** (-0.5)
    scores = jnp.where(mask_row[None, None, :] > 0, scores, -1e30)
    return jax.nn.softmax(scores, axis=-1)


def attend_image(image_items):
    query_b, key_value, caption_keys, mask_row = image_items
    row_count = query_b.shape[0]
    query_h = query_b.reshape(row_count, HEADS, HEAD_DIM)
    key_h = key_value[:, :D].reshape(-1, HEADS, HEAD_DIM)
    value_h = key_value[:, D:].reshape(-1, HEADS, HEAD_DIM)
    scores = jnp.einsum(
        "qhd,khd->hqk", query_h, key_h, preferred_element_type=jnp.float32
    ) * HEAD_DIM ** (-0.5)
    row_top = jnp.max(scores, axis=-1, keepdims=True)
    exponent = jnp.exp(scores - row_top)
    totals = jnp.sum(exponent, axis=-1, keepdims=True)
    weights_self = (exponent / totals).astype(jnp.bfloat16)
    self_out = jnp.einsum("hqk,khd->qhd", weights_self, value_h, preferred_element_type=jnp.float32)
    cross_probs = cross_weights(query_h, caption_keys, mask_row)
    cvalue_h = caption_keys[:, D:].reshape(-1, HEADS, HEAD_DIM)
    cross_out = jnp.einsum(
        "hqk,khd->qhd",
        cross_probs.astype(jnp.bfloat16),
        cvalue_h,
        preferred_element_type=jnp.float32,
    )
    log_totals = (row_top + jnp.log(totals))[..., 0]
    return (self_out.reshape(row_count, D), log_totals, cross_out.reshape(row_count, D))


def attend_back(image_items):
    query_b, key_value, log_totals, grad_self, caption_keys, mask_row, grad_cross = image_items
    row_count = query_b.shape[0]
    attn_scale = HEAD_DIM ** (-0.5)
    query_h = query_b.reshape(row_count, HEADS, HEAD_DIM)
    key_h = key_value[:, :D].reshape(-1, HEADS, HEAD_DIM)
    value_h = key_value[:, D:].reshape(-1, HEADS, HEAD_DIM)
    scores = (
        jnp.einsum("qhd,khd->hqk", query_h, key_h, preferred_element_type=jnp.float32) * attn_scale
    )
    weights_self = jnp.exp(scores - log_totals[..., None])
    weights_low = weights_self.astype(jnp.bfloat16)
    grad_self_h = grad_self.reshape(row_count, HEADS, HEAD_DIM)
    grad_weights = jnp.einsum(
        "qhd,khd->hqk", grad_self_h, value_h, preferred_element_type=jnp.float32
    )
    grad_scores = (
        weights_self * (grad_weights - jnp.sum(weights_self * grad_weights, axis=-1, keepdims=True))
    ).astype(jnp.bfloat16)
    grad_query = (
        jnp.einsum("hqk,khd->qhd", grad_scores, key_h, preferred_element_type=jnp.float32)
        * attn_scale
    )
    grad_keys = (
        jnp.einsum("hqk,qhd->khd", grad_scores, query_h, preferred_element_type=jnp.float32)
        * attn_scale
    )
    grad_values = jnp.einsum(
        "hqk,qhd->khd", weights_low, grad_self_h, preferred_element_type=jnp.float32
    )
    cross_probs = cross_weights(query_h, caption_keys, mask_row)
    ckey_h = caption_keys[:, :D].reshape(-1, HEADS, HEAD_DIM)
    cvalue_h = caption_keys[:, D:].reshape(-1, HEADS, HEAD_DIM)
    grad_cross_h = grad_cross.reshape(row_count, HEADS, HEAD_DIM)
    grad_cross_weights = jnp.einsum(
        "qhd,khd->hqk", grad_cross_h, cvalue_h, preferred_element_type=jnp.float32
    )
    grad_cross_scores = (
        cross_probs
        * (grad_cross_weights - jnp.sum(cross_probs * grad_cross_weights, axis=-1, keepdims=True))
    ).astype(jnp.bfloat16)
    grad_query = (
        grad_query
        + jnp.einsum("hqk,khd->qhd", grad_cross_scores, ckey_h, preferred_element_type=jnp.float32)
        * attn_scale
    )
    grad_ckeys = (
        jnp.einsum("hqk,qhd->khd", grad_cross_scores, query_h, preferred_element_type=jnp.float32)
        * attn_scale
    )
    grad_cvalues = jnp.einsum(
        "hqk,qhd->khd",
        cross_probs.astype(jnp.bfloat16),
        grad_cross_h,
        preferred_element_type=jnp.float32,
    )
    key_count = key_value.shape[0]
    slot_count = caption_keys.shape[0]
    key_terms = jnp.concatenate(
        [grad_keys.reshape(key_count, D), grad_values.reshape(key_count, D)], axis=-1
    )
    caption_terms = jnp.concatenate(
        [grad_ckeys.reshape(slot_count, D), grad_cvalues.reshape(slot_count, D)], axis=-1
    )
    return (grad_query.reshape(row_count, D), key_terms, caption_terms)


def per_device(
    tokens,
    caption,
    modulation,
    caption_mask,
    positions,
    w_qkv,
    w_out,
    w_caption_kv,
    w_gate_up,
    w_down,
    norm_gains,
    caption_gain,
    cross_gate,
    cotangent,
):
    cosine, sine_table = rope_tables(positions)
    gathered = (
        lax.all_gather(w_qkv, "fsdp", axis=0, tiled=True),
        lax.all_gather(w_out, "fsdp", axis=0, tiled=True),
        lax.all_gather(w_gate_up, "fsdp", axis=0, tiled=True),
        lax.all_gather(w_down, "fsdp", axis=0, tiled=True),
        lax.all_gather(norm_gains, "fsdp", axis=1, tiled=True),
        lax.all_gather(caption_gain, "fsdp", axis=0, tiled=True),
        lax.all_gather(cross_gate, "fsdp", axis=0, tiled=True),
        lax.all_gather(modulation, "fsdp", axis=2, tiled=True),
    )
    gain_rows = gathered[4].astype(jnp.float32)
    cap_gain = gathered[5].astype(jnp.float32)
    gate_heads = jnp.tanh(gathered[6].astype(jnp.float32))
    gate_tanh = jnp.repeat(gate_heads, HEAD_DIM)
    mod_rows = gathered[7].astype(jnp.float32)
    inputs = tokens.astype(jnp.float32)
    prepared = project_tokens(inputs, gathered[0], gain_rows, mod_rows, cosine, sine_table)
    partial_kv = jnp.einsum(
        "blc,ce->ble", caption, w_caption_kv, preferred_element_type=jnp.float32
    )
    cap_rows = lax.psum_scatter(
        partial_kv.astype(jnp.bfloat16), "fsdp", scatter_dimension=1, tiled=True
    ).astype(jnp.float32)
    ckey_pre = cap_rows[..., :D]
    ckey_scale = rms_scale(ckey_pre)
    cap_local = jnp.concatenate(
        [
            (ckey_pre * ckey_scale * cap_gain).astype(jnp.bfloat16),
            cap_rows[..., D:].astype(jnp.bfloat16),
        ],
        axis=-1,
    )
    caption_keys = lax.all_gather(cap_local, "fsdp", axis=1, tiled=True)
    image_kv = lax.all_gather(prepared[8], "fsdp", axis=1, tiled=True)
    self_out, log_totals, cross_out = lax.map(
        attend_image, (prepared[7], image_kv, caption_keys, caption_mask)
    )
    combined = (self_out + gate_tanh * cross_out).astype(jnp.bfloat16)
    projected = jnp.einsum("brd,de->bre", combined, gathered[1], preferred_element_type=jnp.float32)
    out_scale = rms_scale(projected)
    normed = projected * out_scale * gain_rows[3]
    gate_mod = jnp.tanh(mod_rows[:, 2])[:, None, :]
    middle = inputs + gate_mod * normed
    ffn_state = ffn_front(middle, gathered[2], gain_rows, mod_rows)
    down_proj = jnp.einsum(
        "brf,fd->brd", ffn_state[5], gathered[3], preferred_element_type=jnp.float32
    )
    down_scale = rms_scale(down_proj)
    down_normed = down_proj * down_scale * gain_rows[5]
    ffn_gate = jnp.tanh(mod_rows[:, 5])[:, None, :]
    block_out = (middle + ffn_gate * down_normed).astype(jnp.bfloat16)
    back_qkv = gathered[0]
    back_out = gathered[1]
    back_gate_up = gathered[2]
    back_down = gathered[3]
    grad_y = cotangent.astype(jnp.float32)
    grad_down_normed = grad_y * ffn_gate
    ffn_gate_rows = jnp.sum(grad_y * down_normed, axis=1) * (1.0 - ffn_gate[:, 0, :] ** 2)
    grad_down, down_gain_terms = norm_back(grad_down_normed, down_proj, down_scale, gain_rows[5])
    grad_down_low = grad_down.astype(jnp.bfloat16)
    grad_w_down = jnp.einsum(
        "brf,brd->fd", ffn_state[5], grad_down_low, preferred_element_type=jnp.float32
    )
    grad_inner = jnp.einsum(
        "brd,fd->brf", grad_down_low, back_down, preferred_element_type=jnp.float32
    )
    gate_part = ffn_state[3]
    up_part = ffn_state[4]
    sigmoid_gate = jax.nn.sigmoid(gate_part)
    grad_gate_part = (
        grad_inner * up_part * (sigmoid_gate * (1.0 + gate_part * (1.0 - sigmoid_gate)))
    )
    grad_up_part = grad_inner * (gate_part * sigmoid_gate)
    grad_gate_up = jnp.concatenate([grad_gate_part, grad_up_part], axis=-1).astype(jnp.bfloat16)
    grad_w_gate_up = jnp.einsum(
        "brd,bre->de", ffn_state[2], grad_gate_up, preferred_element_type=jnp.float32
    )
    grad_ffn_in = jnp.einsum(
        "bre,de->brd", grad_gate_up, back_gate_up, preferred_element_type=jnp.float32
    )
    ffn_shift = jnp.sum(grad_ffn_in, axis=1)
    ffn_scale_rows = jnp.sum(grad_ffn_in * ffn_state[0], axis=1)
    grad_ffn_hidden = grad_ffn_in * (1.0 + mod_rows[:, 4][:, None, :])
    grad_from_ffn, ffn_gain_terms = norm_back(grad_ffn_hidden, middle, ffn_state[1], gain_rows[4])
    grad_mid = grad_y + grad_from_ffn
    ffn_shards = (
        lax.psum_scatter(
            grad_w_gate_up.astype(jnp.bfloat16), "fsdp", scatter_dimension=0, tiled=True
        ).astype(jnp.float32),
        lax.psum_scatter(
            grad_w_down.astype(jnp.bfloat16), "fsdp", scatter_dimension=0, tiled=True
        ).astype(jnp.float32),
    )
    grad_normed = grad_mid * gate_mod
    grad_gate_rows = jnp.sum(grad_mid * normed, axis=1) * (1.0 - gate_mod[:, 0, :] ** 2)
    grad_proj, out_gain_terms = norm_back(grad_normed, projected, out_scale, gain_rows[3])
    grad_proj_low = grad_proj.astype(jnp.bfloat16)
    grad_w_out = jnp.einsum(
        "brd,bre->de", combined, grad_proj_low, preferred_element_type=jnp.float32
    )
    grad_comb = jnp.einsum(
        "bre,de->brd", grad_proj_low, back_out, preferred_element_type=jnp.float32
    ).astype(jnp.bfloat16)
    grad_comb_wide = grad_comb.astype(jnp.float32)
    grad_cross = (gate_tanh * grad_comb_wide).astype(jnp.bfloat16)
    gate_terms = jnp.sum(grad_comb_wide * cross_out, axis=(0, 1)).reshape(HEADS, HEAD_DIM).sum(
        axis=-1
    ) * (1.0 - gate_heads**2)
    grad_query, key_terms, caption_terms = lax.map(
        attend_back,
        (prepared[7], image_kv, log_totals, grad_comb, caption_keys, caption_mask, grad_cross),
    )
    own_kv_grads = lax.psum_scatter(
        key_terms.astype(jnp.bfloat16), "fsdp", scatter_dimension=1, tiled=True
    ).astype(jnp.float32)
    grad_qn = rotate(grad_query, cosine, -sine_table)
    grad_kn = rotate(own_kv_grads[..., :D], cosine, -sine_table)
    grad_qpre, query_gain_terms = norm_back(grad_qn, prepared[3], prepared[4], gain_rows[1])
    grad_kpre, key_gain_terms = norm_back(grad_kn, prepared[5], prepared[6], gain_rows[2])
    grad_mixed = jnp.concatenate([grad_qpre, grad_kpre, own_kv_grads[..., D:]], axis=-1).astype(
        jnp.bfloat16
    )
    grad_w_qkv = jnp.einsum(
        "brd,bre->de", prepared[2], grad_mixed, preferred_element_type=jnp.float32
    )
    grad_mod_in = jnp.einsum(
        "bre,de->brd", grad_mixed, back_qkv, preferred_element_type=jnp.float32
    )
    grad_shift = jnp.sum(grad_mod_in, axis=1)
    grad_scale_rows = jnp.sum(grad_mod_in * prepared[0], axis=1)
    grad_hidden = grad_mod_in * (1.0 + mod_rows[:, 1][:, None, :])
    grad_inputs, input_gain_terms = norm_back(grad_hidden, inputs, prepared[1], gain_rows[0])
    grad_tokens = (grad_mid + grad_inputs).astype(jnp.bfloat16)
    cap_grad_rows = lax.psum_scatter(
        caption_terms.astype(jnp.bfloat16), "fsdp", scatter_dimension=1, tiled=True
    ).astype(jnp.float32)
    grad_ckey_pre, cap_gain_terms = norm_back(
        cap_grad_rows[..., :D], ckey_pre, ckey_scale, cap_gain
    )
    cap_grad_local = jnp.concatenate([grad_ckey_pre, cap_grad_rows[..., D:]], axis=-1).astype(
        jnp.bfloat16
    )
    cap_gain_grad = jnp.sum(cap_gain_terms, axis=(0, 1))
    grad_cap_kv = lax.all_gather(cap_grad_local, "fsdp", axis=1, tiled=True)
    grad_w_caption_kv = jnp.einsum(
        "blc,ble->ce", caption, grad_cap_kv, preferred_element_type=jnp.float32
    )
    grad_caption = jnp.einsum(
        "ble,ce->blc", grad_cap_kv, w_caption_kv, preferred_element_type=jnp.float32
    ).astype(jnp.bfloat16)
    gain_grads = jnp.stack(
        [
            jnp.sum(input_gain_terms, axis=(0, 1)),
            jnp.sum(query_gain_terms, axis=(0, 1)),
            jnp.sum(key_gain_terms, axis=(0, 1)),
            jnp.sum(out_gain_terms, axis=(0, 1)),
            jnp.sum(ffn_gain_terms, axis=(0, 1)),
            jnp.sum(down_gain_terms, axis=(0, 1)),
        ]
    )
    mod_grads = jnp.stack(
        [grad_shift, grad_scale_rows, grad_gate_rows, ffn_shift, ffn_scale_rows, ffn_gate_rows],
        axis=1,
    )
    shard_grads = (
        lax.psum_scatter(
            grad_w_qkv.astype(jnp.bfloat16), "fsdp", scatter_dimension=0, tiled=True
        ).astype(jnp.float32),
        lax.psum_scatter(
            grad_w_out.astype(jnp.bfloat16), "fsdp", scatter_dimension=0, tiled=True
        ).astype(jnp.float32),
        lax.psum_scatter(
            gain_grads.astype(jnp.bfloat16), "fsdp", scatter_dimension=1, tiled=True
        ).astype(jnp.float32),
        lax.psum_scatter(
            gate_terms.astype(jnp.bfloat16), "fsdp", scatter_dimension=0, tiled=True
        ).astype(jnp.float32),
        lax.psum_scatter(
            mod_grads.astype(jnp.bfloat16), "fsdp", scatter_dimension=2, tiled=True
        ).astype(jnp.float32),
        lax.psum_scatter(
            cap_gain_grad.astype(jnp.bfloat16), "fsdp", scatter_dimension=0, tiled=True
        ).astype(jnp.float32),
    )
    wide_grads = (
        lax.psum_scatter(
            shard_grads[0].astype(jnp.bfloat16), "dp", scatter_dimension=1, tiled=True
        ).astype(jnp.float32),
        lax.psum_scatter(
            shard_grads[1].astype(jnp.bfloat16), "dp", scatter_dimension=1, tiled=True
        ).astype(jnp.float32),
        lax.psum_scatter(
            grad_w_caption_kv.astype(jnp.bfloat16), "dp", scatter_dimension=1, tiled=True
        ).astype(jnp.float32),
        lax.psum_scatter(
            ffn_shards[0].astype(jnp.bfloat16), "dp", scatter_dimension=1, tiled=True
        ).astype(jnp.float32),
        lax.psum_scatter(
            ffn_shards[1].astype(jnp.bfloat16), "dp", scatter_dimension=1, tiled=True
        ).astype(jnp.float32),
    )
    small_sums = lax.psum((shard_grads[2], shard_grads[3], shard_grads[5]), "dp")
    return (
        block_out,
        grad_tokens,
        grad_caption,
        shard_grads[4],
        wide_grads[0],
        wide_grads[1],
        wide_grads[2],
        wide_grads[3],
        wide_grads[4],
        small_sums[0],
        small_sums[2],
        small_sums[1],
    )


def solution(mesh):
    placed = (
        P("dp", "fsdp", None),
        P("dp", None, "fsdp"),
        P("dp", None, "fsdp"),
        P("dp", None),
        P("dp", None, "fsdp"),
        P("fsdp", None),
        P("fsdp", None),
        P("fsdp", None),
        P("fsdp", None),
        P("fsdp", None),
        P(None, "fsdp"),
        P("fsdp"),
        P("fsdp"),
        P("dp", "fsdp", None),
    )
    return jax.shard_map(
        per_device,
        mesh=mesh,
        in_specs=placed,
        out_specs=(
            P("dp", "fsdp", None),
            P("dp", "fsdp", None),
            P("dp", None, "fsdp"),
            P("dp", None, "fsdp"),
            P("fsdp", "dp"),
            P("fsdp", "dp"),
            P("fsdp", "dp"),
            P("fsdp", "dp"),
            P("fsdp", "dp"),
            P(None, "fsdp"),
            P("fsdp"),
            P("fsdp"),
        ),
        check_vma=False,
    )
```

profile of v0, /device:TPU:0, one launch (start us, length us, event | category | flops | bytes accessed | tf_op | source)
XLA Modules:
  0.0 2412.7 jit_solution(13094956979278001249)
XLA Ops:
  51.7 166.6 %all-gather.9.cloned.1.call-done = bf16[1536,4608]{1,0:T(8,128)(2,1)} async-done(((bf16[768,4608]{1,0:T(8,128)(2,1)}), bf16[1536,4608]{1,0:T(8,128)(2,1)}) %all-gather.9.cloned.1.call-update) | async-done | bytes 14155792 | tf_op jit(solution)/shard_map/all_gather | solution.py:222
  282.6 56.0 %all-gather.11.cloned.1.call-done = bf16[1,1024,3072]{2,1,0:T(8,128)(2,1)} async-done(((bf16[1,512,3072]{2,1,0:T(8,128)(2,1)}), bf16[1,1024,3072]{2,1,0:T(8,128)(2,1)}) %all-gather.11.cloned.1.call-update) | async-done | bytes 6291472 | tf_op jit(solution)/shard_map/all_gather | solution.py:254
  354.0 21.3 multiply_reduce_fusion.1
  375.4 20.9 fusion.1
  396.3 22.5 fusion.7
  448.6 249.4 %all-gather.17.cloned.1.call-done = bf16[1536,8192]{1,0:T(8,128)(2,1)} async-done(((bf16[768,8192]{1,0:T(8,128)(2,1)}), bf16[1536,8192]{1,0:T(8,128)(2,1)}) %all-gather.17.cloned.1.call-update) | async-done | bytes 25165840 | tf_op jit(solution)/shard_map/all_gather | solution.py:224
  698.0 22.8 convolution_bitcast_fusion
  730.2 121.9 %all-gather.19.cloned.1.call-done = bf16[4096,1536]{1,0:T(8,128)(2,1)} async-done(((bf16[2048,1536]{1,0:T(8,128)(2,1)}), bf16[4096,1536]{1,0:T(8,128)(2,1)}) %all-gather.19.cloned.1.call-update) | async-done | bytes 12582928 | tf_op jit(solution)/shard_map/all_gather | solution.py:225
  867.3 18.8 fusion.19
  886.1 22.2 fusion.48
  963.7 34.7 %multiply_reduce_fusion = (f32[24,512]{1,0:T(8,128)S(1)}, f32[24,512,1024]{2,1,0:T(8,128)}) fusion(f32[24,512,1024]{2,1,0:T(8,128)} %get-tuple-element.241, f32[24,512]{1,0:T(8,128)S(1)} %copy-done.43, bf16[512,24,64]{0,2,1:T(8,128)(2,1)S(1)} %bitcast.242, bf16[1024,24,64]{0,2,1:T(8,128)(2,1)} %bitcast.246), kind=kOutput, calls=%fused_computation.2 | convolution fusion | flops 1660932096 | bytes 105480192 | tf_op jit(solution)/shard_map/while/body/eval_jaxpr/qhd,khd->hqk/dot_general | solution.py:150
  998.3 40.4 %multiply_convert_fusion = bf16[24,512,1024]{2,1,0:T(8,128)(2,1)} fusion(f32[24,512,1024]{2,1,0:T(8,128)} %get-tuple-element.250, f32[24,512,1024]{2,1,0:T(8,128)} %get-tuple-element.241, f32[24,512]{1,0:T(8,128)S(1)} %get-tuple-element.249, f32[24,512]{1,0:T(8,128)S(1)} %copy-done.43), kind=kLoop, calls=%fused_computation.1 | loop fusion | flops 62914560 | bytes 125927424 | tf_op jit(solution)/shard_map/while/body/eval_jaxpr/convert_element_type | solution.py:155
  1038.7 20.5 fusion.64
  1137.6 28.9 %reduce-scatter.25.cloned.1.call-done = bf16[1,512,3072]{2,1,0:T(8,128)(2,1)} async-done(((bf16[1,1024,3072]{2,1,0:T(8,128)(2,1)}), bf16[1,512,3072]{2,1,0:T(8,128)(2,1)}) %reduce-scatter.25.cloned.1.call-update) | async-done | bytes 3145744 | tf_op jit(solution)/shard_map/reduce_scatter | solution.py:333
  1217.6 21.3 convolution_convert_fusion
  1241.1 15.5 fusion.46
  1281.7 122.5 %reduce-scatter.39.cloned.1.call-done = bf16[2048,1536]{1,0:T(8,128)(2,1)} async-done(((bf16[4096,1536]{1,0:T(8,128)(2,1)}), bf16[2048,1536]{1,0:T(8,128)(2,1)}) %reduce-scatter.39.cloned.1.call-update) | async-done | bytes 6291472 | tf_op jit(solution)/shard_map/reduce_scatter | solution.py:310
  1413.0 155.0 %reduce-scatter.29.cloned.1.call-done = bf16[768,4608]{1,0:T(8,128)(2,1)} async-done(((bf16[1536,4608]{1,0:T(8,128)(2,1)}), bf16[768,4608]{1,0:T(8,128)(2,1)}) %reduce-scatter.29.cloned.1.call-update) | async-done | bytes 7077904 | tf_op jit(solution)/shard_map/reduce_scatter | solution.py:386
  1578.1 271.3 %reduce-scatter.35.cloned.1.call-done = bf16[768,8192]{1,0:T(8,128)(2,1)} async-done(((bf16[1536,8192]{1,0:T(8,128)(2,1)}), bf16[768,8192]{1,0:T(8,128)(2,1)}) %reduce-scatter.35.cloned.1.call-update) | async-done | bytes 12582928 | tf_op jit(solution)/shard_map/reduce_scatter | solution.py:307
  1877.8 61.7 %all-reduce.3 = (f32[6,768]{1,0:T(8,128)}, f32[768]{0:T(1024)}, f32[12]{0:T(128)}) all-reduce(bf16[6,768]{1,0:T(8,128)(2,1)} %reduce-scatter.41.cloned.1.call-done, f32[768]{0:T(1024)S(1)} %dynamic-slice_convert_fusion, f32[12]{0:T(128)S(1)} %dynamic-slice_convert_fusion.1), channel_id=1, replica_groups=mesh['dp'=16,'fsdp'=2] {'dp'}, use_global_device_ids=true, to_apply=%region_46.47 | all-reduce | flops 5388 | bytes 33888 | tf_op jit(solution)/shard_map/psum | solution.py:422
  1946.9 135.8 %reduce-scatter.33.cloned.1.call-done = bf16[2048,192]{0,1:T(8,128)(2,1)} async-done(((bf16[2048,3072]{0,1:T(8,128)(2,1)}), bf16[2048,192]{0,1:T(8,128)(2,1)}) %reduce-scatter.33.cloned.1.call-update) | async-done | bytes 786448 | tf_op jit(solution)/shard_map/reduce_scatter | solution.py:412
  2085.2 85.9 %reduce-scatter.49.cloned.1.call-done = bf16[96,2048]{1,0:T(8,128)(2,1)} async-done(((bf16[1536,2048]{1,0:T(8,128)(2,1)}), bf16[96,2048]{1,0:T(8,128)(2,1)}) %reduce-scatter.49.cloned.1.call-update) | async-done | bytes 393232
  2173.5 91.2 %reduce-scatter.45.cloned.1.call-done = bf16[288,768]{1,0:T(8,128)(2,1)} async-done(((bf16[4608,768]{1,0:T(8,128)(2,1)}), bf16[288,768]{1,0:T(8,128)(2,1)}) %reduce-scatter.45.cloned.1.call-update) | async-done | bytes 442384
  2267.2 135.9 %reduce-scatter.37.cloned.1.call-done = bf16[768,512]{1,0:T(8,128)(2,1)} async-done(((bf16[768,8192]{1,0:T(8,128)(2,1)}), bf16[768,512]{1,0:T(8,128)(2,1)}) %reduce-scatter.37.cloned.1.call-update) | async-done | bytes 786448 | tf_op jit(solution)/shard_map/reduce_scatter | solution.py:415
  (438 shorter events, 451.5 us)
Async XLA Ops:
  7.2 39.5 %reduce-scatter.23.cloned.1.call-start = ((), (), s32[]{:S(2)}) async-start(), calls=%async_computation.16 | async-start | bytes 2359296 | tf_op jit(solution)/shard_map/reduce_scatter | solution.py:241
  17.6 200.8 %all-gather.9.cloned.1.call-start = ((), (), s32[]{:S(2)}) async-start(), calls=%async_computation.14 | async-start | bytes 21233664 | tf_op jit(solution)/shard_map/all_gather | solution.py:222
  18.3 249.1 %all-gather.13.cloned.1.call-start = ((), (), s32[]{:S(2)}) async-start(), calls=%async_computation.17 | async-start | bytes 2359296 | tf_op jit(solution)/shard_map/all_gather | solution.py:253
  51.6 286.9 %all-gather.11.cloned.1.call-start = ((), (), s32[]{:S(2)}) async-start(), calls=%async_computation.15 | async-start | bytes 9437184 | tf_op jit(solution)/shard_map/all_gather | solution.py:254
  258.0 180.2 %all-gather.15.cloned.1.call-start = ((), (), s32[]{:S(2)}) async-start(), calls=%async_computation.18 | async-start | bytes 7077888 | tf_op jit(solution)/shard_map/all_gather | solution.py:223
  258.6 439.3 %all-gather.17.cloned.1.call-start = ((), (), s32[]{:S(2)}) async-start(), calls=%async_computation.19 | async-start | bytes 37748736 | tf_op jit(solution)/shard_map/all_gather | solution.py:224
  259.2 592.9 %all-gather.19.cloned.1.call-start = ((), (), s32[]{:S(2)}) async-start(), calls=%async_computation.20 | async-start | bytes 18874368 | tf_op jit(solution)/shard_map/all_gather | solution.py:225
  260.0 836.9 %reduce-scatter.27.cloned.1.call-start = ((), (), s32[]{:S(2)}) async-start(), calls=%async_computation.22 | async-start | bytes 2359296 | tf_op jit(solution)/shard_map/reduce_scatter | solution.py:354
  445.4 252.6 %copy-start.67 = (f32[1536]{0:T(1024)S(1)}, f32[1536]{0:T(1024)}, u32[]{:S(2)}) copy-start(f32[1536]{0:T(1024)} %get-tuple-element.147) | copy-start | bytes 18436
  445.4 252.6 %copy-start.69 = (f32[1536]{0:T(1024)S(1)}, f32[1536]{0:T(1024)}, u32[]{:S(2)}) copy-start(f32[1536]{0:T(1024)} %get-tuple-element.140) | copy-start | bytes 18436
  447.9 460.4 %copy-start.90 = (f32[512]{0:T(512)}, f32[512]{0:T(512)S(1)}, u32[]{:S(2)}) copy-start(f32[512]{0:T(512)S(1)} %get-tuple-element.231) | copy-start | bytes 6148
  963.6 202.9 %reduce-scatter.25.cloned.1.call-start = ((), (), s32[]{:S(2)}) async-start(), calls=%async_computation.21 | async-start | bytes 9437184 | tf_op jit(solution)/shard_map/reduce_scatter | solution.py:333
  1089.2 180.1 %reduce-scatter.31.cloned.1.call-start = ((), (), s32[]{:S(2)}) async-start(), calls=%async_computation.25 | async-start | bytes 7077888 | tf_op jit(solution)/shard_map/reduce_scatter | solution.py:389
  1096.8 177.0 %all-gather.21.cloned.1.call-start = ((), (), s32[]{:S(2)}) async-start(), calls=%async_computation.23 | async-start | bytes 2359296 | tf_op jit(solution)/shard_map/all_gather | solution.py:364
  1102.3 301.9 %reduce-scatter.39.cloned.1.call-start = ((), (), s32[]{:S(2)}) async-start(), calls=%async_computation.29 | async-start | bytes 18874368 | tf_op jit(solution)/shard_map/reduce_scatter | solution.py:310
  1115.1 452.9 %reduce-scatter.29.cloned.1.call-start = ((), (), s32[]{:S(2)}) async-start(), calls=%async_computation.24 | async-start | bytes 21233664 | tf_op jit(solution)/shard_map/reduce_scatter | solution.py:386
  1216.9 632.5 %reduce-scatter.35.cloned.1.call-start = ((), (), s32[]{:S(2)}) async-start(), calls=%async_computation.27 | async-start | bytes 37748736 | tf_op jit(solution)/shard_map/reduce_scatter | solution.py:307
  1239.0 629.3 %reduce-scatter.43.cloned.1.call-start = ((), (), s32[]{:S(2)}) async-start(), calls=%async_computation.31 | async-start | bytes 589824
  1268.4 609.4 %reduce-scatter.41.cloned.1.call-start = ((), (), s32[]{:S(2)}) async-start(), calls=%async_computation.30 | async-start | bytes 36864 | tf_op jit(solution)/shard_map/reduce_scatter | solution.py:392
  1269.3 675.7 %reduce-scatter.47.cloned.1.call-start = ((), (), s32[]{:S(2)}) async-start(), calls=%async_computation.33 | async-start | bytes 2506752
  1273.7 809.1 %reduce-scatter.33.cloned.1.call-start = ((), (), s32[]{:S(2)}) async-start(), calls=%async_computation.26 | async-start | bytes 13369344 | tf_op jit(solution)/shard_map/reduce_scatter | solution.py:412
  1281.7 889.4 %reduce-scatter.49.cloned.1.call-start = ((), (), s32[]{:S(2)}) async-start(), calls=%async_computation.34 | async-start | bytes 6684672
  1413.0 851.8 %reduce-scatter.45.cloned.1.call-start = ((), (), s32[]{:S(2)}) async-start(), calls=%async_computation.32 | async-start | bytes 7520256
  1578.1 825.0 %reduce-scatter.37.cloned.1.call-start = ((), (), s32[]{:S(2)}) async-start(), calls=%async_computation.28 | async-start | bytes 13369344 | tf_op jit(solution)/shard_map/reduce_scatter | solution.py:415
  (113 other events, 3023.0 us)
Sparse Core Ops, SparseCore 0:
  17.6 29.0 reduce-scatter.22
  48.3 169.9 all-gather.8
  220.5 27.2 all-gather.12
  258.2 80.3 all-gather.10
  340.0 62.6 all-gather.14
  404.2 293.7 all-gather.16
  699.6 152.5 all-gather.18
  963.7 26.0 reduce-scatter.26
  1089.4 77.0 reduce-scatter.24
  1168.7 59.9 reduce-scatter.30
  1230.3 27.2 all-gather.20
  1259.7 144.4 reduce-scatter.38
  1406.5 161.4 reduce-scatter.28
  1570.1 279.2 reduce-scatter.34
  1852.1 13.1 reduce-scatter.42
  1868.0 9.7 reduce-scatter.40
  1881.9 63.0 reduce-scatter.46
  1948.9 133.8 reduce-scatter.32
  2086.7 84.3 reduce-scatter.48
  2175.5 89.1 reduce-scatter.44
  2268.8 134.2 reduce-scatter.36
where the time goes:
time: 2420 us; the launch traced here: 2410 us
  waiting for transfers between devices  1650 us (68%)
  matrix products  365 us (15%)
  other arithmetic  160 us (7%)
  local copies, waits for them, and re-layouts  137 us (6%)
  blocking collectives  86.5 us (4%)
    reduce_scatter x1, waiting for transfers between devices, per_device(): lax.psum_scatter(grad_w_gate_up.astype(jnp.bfloat16), 'fsdp', scatter_dim...  271 us
    all_gather x1, waiting for transfers between devices, per_device(): lax.all_gather(w_gate_up, 'fsdp', axis=0, tiled=True)  249 us
    unnamed x25, waiting for transfers between devices  185 us
    all_gather x1, waiting for transfers between devices, per_device(): lax.all_gather(w_qkv, 'fsdp', axis=0, tiled=True)  167 us
    reduce_scatter x1, waiting for transfers between devices, per_device(): lax.psum_scatter(grad_w_qkv.astype(jnp.bfloat16), 'fsdp', scatter_dimensi...  155 us
    reduce_scatter x1, waiting for transfers between devices, per_device(): lax.psum_scatter(ffn_shards[0].astype(jnp.bfloat16), 'dp', scatter_dimens...  136 us
    reduce_scatter x1, waiting for transfers between devices, per_device(): lax.psum_scatter(grad_w_caption_kv.astype(jnp.bfloat16), 'dp', scatter_di...  136 us
    reduce_scatter x1, waiting for transfers between devices, per_device(): lax.psum_scatter(grad_w_down.astype(jnp.bfloat16), 'fsdp', scatter_dimens...  122 us
  transfers between devices with their start and end apart: 21, of which 15 were waited for; matrix products, arithmetic and copies ran while one was open for 22% of the time, Pallas kernels for 0%

commit v1 on v0

v1 whole, which is shorter than its diff:
```python
import functools

import jax
import jax.numpy as jnp
from jax import lax
from jax.experimental import pallas as pl
from jax.experimental.pallas import tpu as pltpu
from jax.sharding import PartitionSpec as P

D = 1536
HEADS = 24
HEAD_DIM = 64
FF = 4096
EPS = 1e-05


def rms_scale(values):
    return lax.rsqrt(jnp.mean(values * values, axis=-1, keepdims=True) + EPS)


def norm_back(grad_normed, values, inv_rms, gain_row):
    scaled_grad = grad_normed * gain_row
    grad_values = inv_rms * scaled_grad - values * inv_rms**3 * jnp.mean(
        scaled_grad * values, axis=-1, keepdims=True
    )
    return (grad_values, grad_normed * values * inv_rms)


def rope_tables(positions):
    lane = jnp.arange(PAIR)
    frequency = 10000.0 ** (-(lane % 16).astype(jnp.float32) / 16)
    places = positions.astype(jnp.float32)
    angles = jnp.where((lane % 64 < 32)[None], places[:, :1], places[:, 1:]) * frequency
    sign = jnp.where(lane % 32 < 16, -1.0, 1.0).astype(jnp.float32)
    return jnp.cos(angles), jnp.sin(angles) * sign


PAIR = 2 * HEAD_DIM
NT = (((1,), (1,)), ((), ()))
TN = (((0,), (0,)), ((), ()))


def head_masks(dtype):
    lane = lax.broadcasted_iota(jnp.int32, (1, PAIR), 1)
    return [(lane < HEAD_DIM).astype(dtype), (lane >= HEAD_DIM).astype(dtype)]


def attend_kernel(q_ref, k_ref, v_ref, ck_ref, cv_ref, bias_ref, gate_ref, a_ref, o_ref, oy_ref, stat_ref):
    masks = head_masks(jnp.float32)
    rows = q_ref.shape[0]
    step = min(rows, 256)
    gate = gate_ref[...]
    for start in range(0, rows, step):
        where = pl.ds(start, step)
        q = q_ref[where, :].astype(jnp.float32) * HEAD_DIM**-0.5
        own, cross, stats = [], [], []
        for mask in masks:
            qm = (q * mask).astype(jnp.bfloat16)
            for keys, values, bias, outs in (
                (k_ref, v_ref, None, own),
                (ck_ref, cv_ref, bias_ref, cross),
            ):
                s = lax.dot_general(qm, keys[...], NT, preferred_element_type=jnp.float32)
                if bias is not None:
                    s = s + bias[...]
                top = jnp.max(s, axis=1, keepdims=True)
                e = jnp.exp(s - top)
                total = jnp.sum(e, axis=1, keepdims=True)
                out = jnp.dot(e.astype(jnp.bfloat16), values[...], preferred_element_type=jnp.float32)
                outs.append(out / total * mask)
                stats.append(top + jnp.log(total))
        o = own[0] + own[1]
        oy = cross[0] + cross[1]
        a_ref[where, :] = (o + gate * oy).astype(jnp.bfloat16)
        o_ref[where, :] = o.astype(jnp.bfloat16)
        oy_ref[where, :] = oy.astype(jnp.bfloat16)
        lane = lax.broadcasted_iota(jnp.int32, (step, PAIR), 1)
        tile = jnp.where(lane == 0, stats[0], jnp.where(lane == 1, stats[1], jnp.where(lane == 2, stats[2], stats[3])))
        stat_ref[0, :, where] = tile.T[:8, :]


def attend(query, key, value, ckey, cvalue, bias_row, gate_lanes):
    rows, keys, slots = query.shape[0], key.shape[0], ckey.shape[0]
    pairs = D // PAIR
    spec = lambda n: pl.BlockSpec((n, PAIR), lambda j: (0, j))
    return pl.pallas_call(
        attend_kernel,
        grid=(pairs,),
        in_specs=[
            spec(rows), spec(keys), spec(keys), spec(slots), spec(slots),
            pl.BlockSpec((1, slots), lambda j: (0, 0)), spec(1),
        ],
        out_specs=[spec(rows)] * 3 + [pl.BlockSpec((1, 8, rows), lambda j: (j, 0, 0))],
        out_shape=[jax.ShapeDtypeStruct((rows, D), jnp.bfloat16)] * 3
        + [jax.ShapeDtypeStruct((pairs, 8, rows), jnp.float32)],
        compiler_params=pltpu.CompilerParams(vmem_limit_bytes=48 * 2**20),
        cost_estimate=cost(16 * rows * (keys + slots) * D, 20e6, HEADS * rows * (keys + slots)),
    )(query, key, value, ckey, cvalue, bias_row, gate_lanes)


def back_part(k_tile, v_tile, bias, qm, grads, deltas, lses):
    masks = head_masks(jnp.bfloat16)
    dk = dv = add = None
    for h in range(2):
        st = dot(k_tile, qm[h], NT)
        if bias is not None:
            st = st + bias
        pt = jnp.exp(st - lses[h])
        dpt = dot(v_tile, grads[h], NT)
        dst = (pt * (dpt - deltas[h])).astype(jnp.bfloat16)
        terms = (
            dot(dst, qm[h]),
            dot(pt.astype(jnp.bfloat16), grads[h]),
            dot(dst, k_tile * masks[h], TN),
        )
        dk, dv, add = terms if h == 0 else (dk + terms[0], dv + terms[1], add + terms[2])
    return dk, dv, add


def head_sums(terms):
    t = terms.T
    return [
        jnp.sum(t[:HEAD_DIM], axis=0, keepdims=True),
        jnp.sum(t[HEAD_DIM:], axis=0, keepdims=True),
    ]


def split_heads(values):
    return [(values * m).astype(jnp.bfloat16) for m in head_masks(jnp.float32)]


def cross_back_kernel(q_ref, ck_ref, cv_ref, bias_ref, gate_ref, stat_ref, da_ref, oy_ref, dq_ref, dck_ref, dcv_ref, gsum_ref):
    qm = split_heads(q_ref[...].astype(jnp.float32) * HEAD_DIM**-0.5)
    da = da_ref[...].astype(jnp.float32)
    doy = (da * gate_ref[...]).astype(jnp.bfloat16).astype(jnp.float32)
    oy = oy_ref[...].astype(jnp.float32)
    gsum_ref[...] = jnp.sum(da * oy, axis=0, keepdims=True)
    stat = stat_ref[0]
    dk, dv, dq = back_part(
        ck_ref[...], cv_ref[...], bias_ref[...], qm, split_heads(doy), head_sums(doy * oy), [stat[1:2], stat[3:4]]
    )
    dck_ref[...] = dk.astype(dck_ref.dtype)
    dcv_ref[...] = dv.astype(dcv_ref.dtype)
    dq_ref[...] = (dq * HEAD_DIM**-0.5).astype(dq_ref.dtype)


def self_back_kernel(q_ref, k_ref, v_ref, stat_ref, da_ref, o_ref, dqc_ref, dq_ref, dk_ref, dv_ref):
    keys = k_ref.shape[0]
    step = min(keys, 256)
    qm = split_heads(q_ref[...].astype(jnp.float32) * HEAD_DIM**-0.5)
    da = da_ref[...].astype(jnp.float32)
    deltas = head_sums(da * o_ref[...].astype(jnp.float32))
    dam = split_heads(da)
    stat = stat_ref[0]
    dq = None
    for start in range(0, keys, step):
        where = pl.ds(start, step)
        dk, dv, add = back_part(k_ref[where, :], v_ref[where, :], None, qm, dam, deltas, [stat[0:1], stat[2:3]])
        dk_ref[where, :] = dk.astype(dk_ref.dtype)
        dv_ref[where, :] = dv.astype(dv_ref.dtype)
        dq = add if dq is None else dq + add
    dq = dq * HEAD_DIM**-0.5 + dqc_ref[...].astype(jnp.float32)
    dq_ref[...] = dq.astype(dq_ref.dtype)


def cross_back(query, ckey, cvalue, bias_col, gate_lanes, stats, grad_a, o_cross):
    rows, slots = query.shape[0], ckey.shape[0]
    pairs = D // PAIR
    spec = lambda n: pl.BlockSpec((n, PAIR), lambda j: (0, j))
    return pl.pallas_call(
        cross_back_kernel,
        grid=(pairs,),
        in_specs=[
            spec(rows), spec(slots), spec(slots),
            pl.BlockSpec((slots, 1), lambda j: (0, 0)), spec(1),
            pl.BlockSpec((1, 8, rows), lambda j: (j, 0, 0)),
            spec(rows), spec(rows),
        ],
        out_specs=[spec(rows), spec(slots), spec(slots), spec(1)],
        out_shape=[jax.ShapeDtypeStruct((n, D), jnp.bfloat16) for n in (rows, slots, slots)]
        + [jax.ShapeDtypeStruct((1, D), jnp.float32)],
        compiler_params=params(48),
        cost_estimate=cost(40 * rows * slots * D, 9e6, HEADS * rows * slots),
    )(query, ckey, cvalue, bias_col, gate_lanes, stats, grad_a, o_cross)


def self_back(query, key, value, stats, grad_a, o_self, dq_cross, first, count):
    rows, keys = query.shape[0], key.shape[0]
    spec = lambda n: pl.BlockSpec((n, PAIR), lambda j: (0, j + first))
    out = lambda n: pl.BlockSpec((n, PAIR), lambda j: (0, j))
    return pl.pallas_call(
        self_back_kernel,
        grid=(count,),
        in_specs=[
            spec(rows), spec(keys), spec(keys),
            pl.BlockSpec((1, 8, rows), lambda j: (j + first, 0, 0)),
            spec(rows), spec(rows), spec(rows),
        ],
        out_specs=[out(rows), out(keys), out(keys)],
        out_shape=[jax.ShapeDtypeStruct((n, count * PAIR), jnp.bfloat16) for n in (rows, keys, keys)],
        compiler_params=params(48),
        cost_estimate=cost(80 * rows * keys * count * PAIR, 1e6 * count, 2 * count * rows * keys),
    )(query, key, value, stats, grad_a, o_self, dq_cross)


NN = (((1,), (0,)), ((), ()))


def dot(a, b, dims=NN):
    return lax.dot_general(a, b, dims, preferred_element_type=jnp.float32)


def chunks(rows, step, body):
    def one(i, carry):
        body(pl.ds(pl.multiple_of(i * step, step), step))
        return carry

    lax.fori_loop(0, rows // step, one, 0)


def add_row(ref, index, terms):
    ref[index : index + 1, :] += jnp.sum(terms, axis=0, keepdims=True)


def partner(values):
    lane = lax.broadcasted_iota(jnp.int32, (values.shape[0], PAIR), 1)
    low = (lane & 31) < 16
    outs = []
    for start in range(0, values.shape[1], PAIR):
        tile = values[:, start : start + PAIR]
        outs.append(jnp.where(low, pltpu.roll(tile, PAIR - 16, 1), pltpu.roll(tile, 16, 1)))
    return jnp.concatenate(outs, axis=1)


def turn(values, cosine, sine):
    count = values.shape[1] // PAIR
    wide = lambda t: jnp.concatenate([t] * count, axis=1)
    return values * wide(cosine) + partner(values) * wide(sine)


def halves(values, which):
    mid = values.shape[1] // 2
    low, high = values[:, :mid], values[:, mid:]
    first = which == 0
    return jnp.where(first, low, high), jnp.where(first, high, low)


def small_spec(shape):
    return pl.BlockSpec(shape, lambda *_: (0,) * len(shape))


def params(mib=56):
    return pltpu.CompilerParams(vmem_limit_bytes=mib * 2**20)


def cost(flops, nbytes, trans=0):
    share = 0.05
    return pl.CostEstimate(
        flops=int(flops * share), bytes_accessed=int(nbytes * share), transcendentals=int(trans * share)
    )


def project_kernel(parts, own_rows, where_ref, tok_ref, gain_ref, mod_ref, cos_ref, sin_ref, own_ref, *refs):
    pieces = refs[:parts]
    hm_ref, full_ref, q_ref, k_ref, v_ref, qpre_ref, kpre_ref, pre_ref = refs[parts:]
    pid = pl.program_id(0)
    rows = tok_ref.shape[0]
    step = min(128, rows)
    tile = full_ref.shape[1]
    per = D // tile

    @pl.when(pid == 0)
    def hidden():
        def body(where):
            x = tok_ref[where, :].astype(jnp.float32)
            hid = x * rms_scale(x) * gain_ref[0:1]
            hm_ref[where, :] = (hid * (1.0 + mod_ref[1:2]) + mod_ref[0:1]).astype(jnp.bfloat16)

        chunks(rows, step, body)

    n = own_ref.shape[0]
    full_ref[pl.ds(pl.multiple_of(where_ref[0], n), n), :] = own_ref[...]
    for i, piece in enumerate(pieces):
        n = piece.shape[0]
        full_ref[pl.ds(pl.multiple_of(where_ref[i + 1], n), n), :] = piece[...]

    for j in range(2 * per):
        count = own_rows if j < per else rows

        @pl.when(pid == j)
        def pre(j=j, count=count):
            pre_ref[:count, (j % per) * tile : (j % per + 1) * tile] = dot(
                hm_ref[:count, :], full_ref[...]
            )

    @pl.when(pid >= 2 * per)
    def value():
        v_ref[...] = dot(hm_ref[...], full_ref[...]).astype(jnp.bfloat16)

    for last, count, out, keep, gain in (
        (per - 1, own_rows, q_ref, qpre_ref, 1),
        (2 * per - 1, rows, k_ref, kpre_ref, 2),
    ):

        @pl.when(pid == last)
        def finish(count=count, out=out, keep=keep, gain=gain):
            def body(where):
                p = pre_ref[where, :]
                n = p * rms_scale(p) * gain_ref[gain : gain + 1]
                out[where, :] = turn(n, cos_ref[where, :], sin_ref[where, :]).astype(jnp.bfloat16)
                keep[where, :] = p.astype(jnp.bfloat16)

            chunks(count, min(step, count), body)


def project(tokens_all, own_rows, gains, mods, cosine, sine, weight, tile=512):
    own, pieces, starts = weight
    rows = tokens_all.shape[0]
    n = 3 * D // tile
    vtile = 2 * D // tile
    outs = [
        ((rows, D), jnp.bfloat16, None),
        ((D, 3 * D), jnp.bfloat16, pl.BlockSpec((D, tile), lambda j, w: (0, j))),
        ((own_rows, D), jnp.bfloat16, None),
        ((rows, D), jnp.bfloat16, None),
        ((rows, D), jnp.bfloat16, pl.BlockSpec((rows, tile), lambda j, w: (0, jnp.maximum(j - vtile, 0)))),
        ((own_rows, D), jnp.bfloat16, None),
        ((rows, D), jnp.bfloat16, None),
    ]
    return pl.pallas_call(
        functools.partial(project_kernel, len(pieces), own_rows),
        grid_spec=pltpu.PrefetchScalarGridSpec(
            num_scalar_prefetch=1,
            grid=(n,),
            in_specs=[small_spec(a.shape) for a in (tokens_all, gains, mods, cosine, sine)]
            + [pl.BlockSpec((p.shape[0], tile), lambda j, w: (0, j)) for p in [own] + pieces],
            out_specs=[s if s is not None else small_spec(shape) for shape, _, s in outs],
            scratch_shapes=[pltpu.VMEM((rows, D), jnp.float32)],
        ),
        out_shape=[jax.ShapeDtypeStruct(shape, d) for shape, d, _ in outs],
        compiler_params=params(58),
        cost_estimate=cost(2 * D * D * (own_rows + 2 * rows), 60e6),
    )(jnp.stack(starts).astype(jnp.int32), tokens_all, gains, mods, cosine, sine, own, *pieces)


def output_kernel(which_ref, a_ref, w0_ref, w1_ref, x_ref, gain_ref, mod_ref, o_ref, mid_ref, hfm_ref):
    a0, a1 = halves(a_ref[...], which_ref[0])
    o = dot(a0, w0_ref[...]) + dot(a1, w1_ref[...])
    o_ref[...] = o.astype(jnp.bfloat16)
    on = o * rms_scale(o) * gain_ref[3:4]
    mid = x_ref[...].astype(jnp.float32) + jnp.tanh(mod_ref[2:3]) * on
    mid_ref[...] = mid
    hf = mid * rms_scale(mid) * gain_ref[4:5]
    hfm_ref[...] = (hf * (1.0 + mod_ref[4:5]) + mod_ref[3:4]).astype(jnp.bfloat16)


def output_step(which, combined, weight, tokens, gains, mods):
    rows = combined.shape[0]
    step = min(rows, 256)
    row_spec = pl.BlockSpec((step, D), lambda i, w: (i, 0))
    return pl.pallas_call(
        output_kernel,
        grid_spec=pltpu.PrefetchScalarGridSpec(
            num_scalar_prefetch=1,
            grid=(rows // step,),
            in_specs=[row_spec, small_spec(weight[0].shape), small_spec(weight[1].shape), row_spec]
            + [small_spec(gains.shape), small_spec(mods.shape)],
            out_specs=[row_spec] * 3,
        ),
        out_shape=[
            jax.ShapeDtypeStruct((rows, D), jnp.bfloat16),
            jax.ShapeDtypeStruct((rows, D), jnp.float32),
            jax.ShapeDtypeStruct((rows, D), jnp.bfloat16),
        ],
        compiler_params=params(),
        cost_estimate=cost(2 * rows * D * D, 15e6),
    )(which, combined, weight[0], weight[1], tokens, gains, mods)


def gate_up_kernel(which_ref, h_ref, g0_ref, g1_ref, u0_ref, u1_ref, ga_ref, up_ref, ff_ref, hs_ref):
    @pl.when(pl.program_id(0) == 0)
    def split():
        hs_ref[0], hs_ref[1] = halves(h_ref[...], which_ref[0])

    ga = dot(hs_ref[0], g0_ref[...]) + dot(hs_ref[1], g1_ref[...])
    up = dot(hs_ref[0], u0_ref[...]) + dot(hs_ref[1], u1_ref[...])
    ga_ref[...] = ga.astype(jnp.bfloat16)
    up_ref[...] = up.astype(jnp.bfloat16)
    ff_ref[...] = (ga / (1.0 + jnp.exp(-ga)) * up).astype(jnp.bfloat16)


def gate_up_step(which, hfm, weight, tile=512):
    rows = hfm.shape[0]
    n = FF // tile
    half = D // 2
    spec = lambda off: pl.BlockSpec((half, tile), lambda j, w: (0, j + off))
    out = pl.BlockSpec((rows, tile), lambda j, w: (0, j))
    return pl.pallas_call(
        gate_up_kernel,
        grid_spec=pltpu.PrefetchScalarGridSpec(
            num_scalar_prefetch=1,
            grid=(n,),
            in_specs=[small_spec(hfm.shape), spec(0), spec(0), spec(n), spec(n)],
            out_specs=[out] * 3,
            scratch_shapes=[pltpu.VMEM((2, rows, half), jnp.bfloat16)],
        ),
        out_shape=[jax.ShapeDtypeStruct((rows, FF), jnp.bfloat16)] * 3,
        compiler_params=params(),
        cost_estimate=cost(4 * rows * D * FF, 40e6, rows * FF),
    )(which, hfm, weight[0], weight[1], weight[0], weight[1])


def down_kernel(which_ref, ff_ref, w0_ref, w1_ref, mid_ref, cot_ref, gain_ref, mod_ref, out_ref, df_ref, sum_ref, f_ref, hs_ref):
    pid = pl.program_id(0)
    tile = w0_ref.shape[1]
    rows = ff_ref.shape[0]

    @pl.when(pid == 0)
    def split():
        hs_ref[0], hs_ref[1] = halves(ff_ref[...], which_ref[0])

    f_ref[pid] = dot(hs_ref[0], w0_ref[...]) + dot(hs_ref[1], w1_ref[...])

    @pl.when(pid == pl.num_programs(0) - 1)
    def finish():
        gate = jnp.tanh(mod_ref[5:6])
        sum_ref[...] = jnp.zeros_like(sum_ref)

        def body(where):
            f = jnp.concatenate([f_ref[j, where, :] for j in range(D // tile)], axis=1)
            rf = rms_scale(f)
            fn = f * rf * gain_ref[5:6]
            dy = cot_ref[where, :].astype(jnp.float32)
            out_ref[where, :] = (mid_ref[where, :] + gate * fn).astype(jnp.bfloat16)
            dfn = dy * gate
            add_row(sum_ref, 0, dy * fn)
            df, terms = norm_back(dfn, f, rf, gain_ref[5:6])
            add_row(sum_ref, 1, terms)
            df_ref[where, :] = df.astype(jnp.bfloat16)

        chunks(rows, min(64, rows), body)


def down_step(which, ffh, weight, middle, cotangent, gains, mods, tile=256):
    rows = ffh.shape[0]
    half = FF // 2
    spec = pl.BlockSpec((half, tile), lambda j, w: (0, j))
    full = small_spec((rows, D))
    return pl.pallas_call(
        down_kernel,
        grid_spec=pltpu.PrefetchScalarGridSpec(
            num_scalar_prefetch=1,
            grid=(D // tile,),
            in_specs=[small_spec(ffh.shape), spec, spec, full, full, small_spec(gains.shape), small_spec(mods.shape)],
            out_specs=[full, full, small_spec((8, D))],
            scratch_shapes=[
                pltpu.VMEM((D // tile, rows, tile), jnp.float32),
                pltpu.VMEM((2, rows, half), jnp.bfloat16),
            ],
        ),
        out_shape=[jax.ShapeDtypeStruct((rows, D), jnp.bfloat16)] * 2
        + [jax.ShapeDtypeStruct((8, D), jnp.float32)],
        compiler_params=params(),
        cost_estimate=cost(2 * rows * D * FF, 24e6),
    )(which, ffh, weight[0], weight[1], middle, cotangent, gains, mods)


def gate_up_back_kernel(which_ref, df_ref, ga_ref, up_ref, d0_ref, d1_ref, dgu_ref):
    pid = pl.program_id(0)
    n = pl.num_programs(0)

    def work(w_ref):
        dffh = dot(df_ref[...], w_ref[...], NT)
        ga = ga_ref[...].astype(jnp.float32)
        up = up_ref[...].astype(jnp.float32)
        s = 1.0 / (1.0 + jnp.exp(-ga))
        dgu_ref[0] = (dffh * up * (s * (1.0 + ga * (1.0 - s)))).astype(jnp.bfloat16)
        dgu_ref[1] = (dffh * (ga * s)).astype(jnp.bfloat16)

    @pl.when(pid < n // 2)
    def first():
        work(d0_ref)

    @pl.when(pid >= n // 2)
    def second():
        work(d1_ref)


def gate_up_back(which, df, ga, up, w_down, tile=512):
    rows = df.shape[0]
    n = FF // tile
    h = n // 2
    cols = pl.BlockSpec((rows, tile), lambda j, w: (0, (j + w[0] * h) % n))
    return pl.pallas_call(
        gate_up_back_kernel,
        grid_spec=pltpu.PrefetchScalarGridSpec(
            num_scalar_prefetch=1,
            grid=(n,),
            in_specs=[
                small_spec((rows, D)), cols, cols,
                pl.BlockSpec((tile, D), lambda j, w: (jnp.minimum(j, h - 1), 0)),
                pl.BlockSpec((tile, D), lambda j, w: (jnp.maximum(j - h, 0), 0)),
            ],
            out_specs=pl.BlockSpec((2, rows, tile), lambda j, w: (0, 0, (j + w[0] * h) % n)),
        ),
        out_shape=jax.ShapeDtypeStruct((2, rows, FF), jnp.bfloat16),
        compiler_params=params(),
        cost_estimate=cost(2 * rows * D * FF, 30e6, rows * FF),
    )(which, df, ga, up, w_down[0], w_down[1])


def ffn_back_kernel(
    which_ref, dgu_ref, g0_ref, g1_ref, u0_ref, u1_ref,
    mid_ref, cot_ref, o_ref, w0_ref, w1_ref, gain_ref, mod_ref,
    dmid_ref, do_ref, da_ref, sum_ref, acc_ref,
):
    pid = pl.program_id(0)
    n = pl.num_programs(0)
    rows = mid_ref.shape[0]
    which = which_ref[0]
    dga, dup = dgu_ref[0], dgu_ref[1]
    p0 = dot(dga, g0_ref[...], NT) + dot(dup, u0_ref[...], NT)
    p1 = dot(dga, g1_ref[...], NT) + dot(dup, u1_ref[...], NT)

    @pl.when(pid == 0)
    def clear():
        acc_ref[which] = p0
        acc_ref[1 - which] = p1

    @pl.when(pid > 0)
    def more():
        acc_ref[which] += p0
        acc_ref[1 - which] += p1

    @pl.when(pid == n - 1)
    def finish():
        sum_ref[...] = jnp.zeros_like(sum_ref)
        gate = jnp.tanh(mod_ref[2:3])

        def body(where):
            dhfm = jnp.concatenate([acc_ref[0, where, :], acc_ref[1, where, :]], axis=1)
            mid = mid_ref[where, :]
            r2 = rms_scale(mid)
            add_row(sum_ref, 0, dhfm)
            add_row(sum_ref, 1, dhfm * (mid * r2 * gain_ref[4:5]))
            dmid, terms = norm_back(dhfm * (1.0 + mod_ref[4:5]), mid, r2, gain_ref[4:5])
            add_row(sum_ref, 2, terms)
            dmid = cot_ref[where, :].astype(jnp.float32) + dmid
            dmid_ref[where, :] = dmid
            o = o_ref[where, :].astype(jnp.float32)
            ro = rms_scale(o)
            add_row(sum_ref, 3, dmid * (o * ro * gain_ref[3:4]))
            do, terms = norm_back(dmid * gate, o, ro, gain_ref[3:4])
            add_row(sum_ref, 4, terms)
            do_ref[where, :] = do.astype(jnp.bfloat16)

        chunks(rows, min(64, rows), body)
        do = do_ref[...]
        q0 = dot(do, w0_ref[...], NT).astype(jnp.bfloat16)
        q1 = dot(do, w1_ref[...], NT).astype(jnp.bfloat16)
        half = q0.shape[1]
        da_ref[:, :half] = jnp.where(which == 0, q0, q1)
        da_ref[:, half:] = jnp.where(which == 0, q1, q0)


def ffn_back(which, dgu, w_gate_up, w_out, middle, cotangent, o, gains, mods, tile=512):
    rows = middle.shape[0]
    n = FF // tile
    half = D // 2
    full = small_spec((rows, D))
    gspec = pl.BlockSpec((half, tile), lambda j, w: (0, j))
    uspec = pl.BlockSpec((half, tile), lambda j, w: (0, j + n))
    return pl.pallas_call(
        ffn_back_kernel,
        grid_spec=pltpu.PrefetchScalarGridSpec(
            num_scalar_prefetch=1,
            grid=(n,),
            in_specs=[
                pl.BlockSpec((2, rows, tile), lambda j, w: (0, 0, j)),
                gspec, gspec, uspec, uspec, full, full, full,
                small_spec(w_out[0].shape), small_spec(w_out[1].shape),
                small_spec(gains.shape), small_spec(mods.shape),
            ],
            out_specs=[full, full, full, small_spec((8, D))],
            scratch_shapes=[pltpu.VMEM((2, rows, half), jnp.float32)],
        ),
        out_shape=[jax.ShapeDtypeStruct((rows, D), jnp.float32)]
        + [jax.ShapeDtypeStruct((rows, D), jnp.bfloat16)] * 2
        + [jax.ShapeDtypeStruct((8, D), jnp.float32)],
        compiler_params=params(60),
        cost_estimate=cost(4 * rows * D * FF + 2 * rows * D * D, 55e6),
    )(
        which, dgu, w_gate_up[0], w_gate_up[1], w_gate_up[0], w_gate_up[1],
        middle, cotangent, o, w_out[0], w_out[1], gains, mods,
    )


def qk_back_kernel(own_blocks, parts, *refs):
    dq_refs, dk_refs, dv_refs = refs[:parts], refs[parts : 2 * parts], refs[2 * parts : 3 * parts]
    qpre_ref, kpre_ref, cos_ref, sin_ref, gain_ref, dqkv_ref, sum_ref = refs[3 * parts :]
    pid = pl.program_id(0)

    @pl.when(pid == 0)
    def clear():
        sum_ref[...] = jnp.zeros_like(sum_ref)

    def back(grad_refs, pre_ref, row):
        pre = pre_ref[...].astype(jnp.float32)
        grad = jnp.concatenate([g[...] for g in grad_refs], axis=1).astype(jnp.float32)
        grad = turn(grad, cos_ref[...], -sin_ref[...])
        d, terms = norm_back(grad, pre, rms_scale(pre), gain_ref[row : row + 1])
        add_row(sum_ref, row, terms)
        return d.astype(jnp.bfloat16)

    dqkv_ref[:, D : 2 * D] = back(dk_refs, kpre_ref, 2)
    width = D // parts
    for i, ref in enumerate(dv_refs):
        dqkv_ref[:, 2 * D + i * width : 2 * D + (i + 1) * width] = ref[...]

    @pl.when(pid < own_blocks)
    def with_query():
        dqkv_ref[:, :D] = back(dq_refs, qpre_ref, 1)

    @pl.when(pid >= own_blocks)
    def no_query():
        dqkv_ref[:, :D] = jnp.zeros((dqkv_ref.shape[0], D), jnp.bfloat16)


def qk_back(dq, dk, dv, qpre, kpre, cosine, sine, gains):
    own, rows = dq[0].shape[0], dk[0].shape[0]
    parts = len(dq)
    step = min(128, own)
    blocks = own // step
    row = lambda n: pl.BlockSpec((step, n), lambda i: (i, 0))
    own_row = lambda n: pl.BlockSpec((step, n), lambda i: (jnp.minimum(i, blocks - 1), 0))
    return pl.pallas_call(
        functools.partial(qk_back_kernel, blocks, parts),
        grid=(rows // step,),
        in_specs=[own_row(D // parts)] * parts + [row(D // parts)] * (2 * parts)
        + [own_row(D), row(D), row(PAIR), row(PAIR), small_spec(gains.shape)],
        out_specs=[row(3 * D), small_spec((8, D))],
        out_shape=[
            jax.ShapeDtypeStruct((rows, 3 * D), jnp.bfloat16),
            jax.ShapeDtypeStruct((8, D), jnp.float32),
        ],
        compiler_params=params(),
        cost_estimate=cost(60 * rows * D, 30e6),
    )(*dq, *dk, *dv, qpre, kpre, cosine, sine, gains)


def project_back_kernel(with_query, dqkv_ref, tok_ref, w_ref, gain_ref, mod_ref, dx_ref, sum_ref):
    @pl.when(pl.program_id(0) == 0)
    def clear():
        sum_ref[...] = jnp.zeros_like(sum_ref)

    first = 0 if with_query else D
    dhm = dot(dqkv_ref[:, first:], w_ref[:, first:], NT)
    x = tok_ref[...].astype(jnp.float32)
    r1 = rms_scale(x)
    add_row(sum_ref, 3, dhm)
    add_row(sum_ref, 4, dhm * (x * r1 * gain_ref[0:1]))
    dx, terms = norm_back(dhm * (1.0 + mod_ref[1:2]), x, r1, gain_ref[0:1])
    add_row(sum_ref, 0, terms)
    dx_ref[...] = dx.astype(jnp.bfloat16)


def project_back(dqkv, first, own, tokens_all, full_qkv, gains, mods):
    rows = dqkv.shape[0] - own if first else own
    step = min(256, own)
    skip = first // step
    row = pl.BlockSpec((step, D), lambda i: (i + skip, 0))
    return pl.pallas_call(
        functools.partial(project_back_kernel, first == 0),
        grid=(max(rows // step, 1),),
        in_specs=[pl.BlockSpec((step, 3 * D), lambda i: (i + skip, 0)), row]
        + [pl.BlockSpec(full_qkv.shape, lambda i: (0, 0), pipeline_mode=pl.Buffered(1))]
        + [small_spec(gains.shape), small_spec(mods.shape)],
        out_specs=[pl.BlockSpec((step, D), lambda i: (i, 0)), small_spec((8, D))],
        out_shape=[
            jax.ShapeDtypeStruct((rows, D), jnp.bfloat16),
            jax.ShapeDtypeStruct((8, D), jnp.float32),
        ],
        compiler_params=params(),
        cost_estimate=cost(6 * rows * D * D, 30e6),
    )(dqkv, tokens_all, full_qkv, gains, mods)


def product_kernel(where_ref, d_ref, a_ref, *refs):
    p = dot(d_ref[0], a_ref[...], TN)
    if len(refs) == 2:
        p = p + refs[0][0].astype(jnp.float32)
    refs[-1][0] = p.astype(jnp.bfloat16)


def product(dact, act, starts, lanes, received=None):
    parts, tokens, columns = dact.shape
    count = len(starts)
    width = lanes if lanes <= 512 else 512
    per = lanes // width
    tile = next(t for t in (2048, 1536, 1024, 512, 256, 128) if columns % t == 0)
    each = columns // tile
    out_spec = pl.BlockSpec((1, tile, width), lambda n, k, s: (k // per, n, k % per))
    return pl.pallas_call(
        product_kernel,
        grid_spec=pltpu.PrefetchScalarGridSpec(
            num_scalar_prefetch=1,
            grid=(parts * each, count * per),
            in_specs=[
                pl.BlockSpec((1, tokens, tile), lambda n, k, s: (n // each, 0, n % each)),
                pl.BlockSpec((tokens, width), lambda n, k, s: (0, s[k // per] * per + k % per)),
            ]
            + ([] if received is None else [out_spec]),
            out_specs=out_spec,
        ),
        out_shape=jax.ShapeDtypeStruct((count, parts * columns, lanes), jnp.bfloat16),
        compiler_params=params(),
        cost_estimate=cost(
            2 * tokens * parts * columns * lanes * count, 4 * parts * columns * lanes * count
        ),
    )(jnp.stack(starts).astype(jnp.int32), dact, act, *([] if received is None else [received]))


ORDERS = ["yxz", "xzy", "zyx"]


def bits_of(size):
    return size.bit_length() - 1


def swap(value, axis, mask, size):
    return lax.ppermute(value, axis, [(i, i ^ mask) for i in range(size)])


def after(value, *earlier):
    return lax.optimization_barrier((value,) + earlier)[0]


def special(env):
    return env[1] == 2 and bits_of(env[0]) >= 3


def gather_pieces(shard, routes, env):
    nd, nf, me, mine = env
    if not special(env):
        full = lax.all_gather(shard, "fsdp", axis=0, tiled=True)
        half = full.shape[0] // 2
        return (full[:half], [full[half:]], [jnp.int32(0), jnp.int32(half)]), shard
    rows = shard.shape[0]
    chunk = rows // len(routes)
    pieces, starts, firsts = [], [], []
    for r, route in enumerate(routes):
        piece_rows = chunk >> len(route)
        index = sum(((me >> b) & 1) << i for i, b in enumerate(route))
        base = r * chunk + (mine ^ 1) * rows
        part = lax.dynamic_slice_in_dim(shard, r * chunk + index * piece_rows, piece_rows, 0)
        held = [(0, swap(part, "fsdp", 1, nf))]
        firsts.append(held[0][1])
        for i, b in enumerate(route):
            held = held + [(rel | (1 << i), swap(p, "dp", 1 << b, nd)) for rel, p in held]
        for rel, p in held:
            pieces.append(p)
            starts.append(base + (index ^ rel) * piece_rows)
    return (shard, pieces, [mine * rows] + starts), firsts


def gather_half(shard, env, hold, late):
    nd, nf, me, mine = env
    if not special(env):
        full = lax.all_gather(shard, "fsdp", axis=0, tiled=True)
        half = full.shape[0] // 2
        return (full[:half], full[half:]), shard
    rows = shard.shape[0] // 8
    part = after(lax.dynamic_slice_in_dim(shard, (me & 7) * rows, rows, 0), *hold)
    got = swap(part, "fsdp", 1, nf)
    groups = [list(range(i, i + 8)) for i in range(0, nd, 8)]
    if late:
        got = after(got, *late)
    other = lax.all_gather(got, "dp", axis=0, tiled=True, axis_index_groups=groups)
    return (shard, other), got


def gather_relative(value, env):
    nf = env[1]
    blocks = [value]
    for b in range(bits_of(nf)):
        blocks = blocks + [swap(p, "fsdp", 1 << b, nf) for p in blocks]
    return jnp.concatenate(blocks, axis=0)


def reduce_relative(value, env):
    nf = env[1]
    total = None
    for b in reversed(range(bits_of(nf))):
        half = value.shape[0] // 2
        got = swap(value[half:], "fsdp", 1 << b, nf)
        total = value[:half].astype(jnp.float32) + got.astype(jnp.float32)
        value = total.astype(jnp.bfloat16)
    return value.astype(jnp.float32) if total is None else total


def sum_fsdp(value, env, anchor=None):
    nf = env[1]
    for b in range(bits_of(nf)):
        got = swap(value.astype(jnp.bfloat16), "fsdp", 1 << b, nf)
        if anchor is not None:
            got = after(got, anchor)
        value = value + got.astype(jnp.float32)
    return value


def gather_small(pack, env):
    nf, mine = env[1], env[3]
    if nf != 2:
        return lax.all_gather(pack, "fsdp", axis=1, tiled=True)
    got = swap(pack, "fsdp", 1, nf)
    return jnp.concatenate(
        [jnp.where(mine == 0, pack, got), jnp.where(mine == 0, got, pack)], axis=1
    )


def sum_wide(value, axes, env):
    for axis in axes:
        size = env[0] if axis == "dp" else env[1]
        for b in range(bits_of(size)):
            value = value + swap(value, axis, 1 << b, size)
    return value


def stages_of(order, env):
    kinds = {
        "y": [("f", b) for b in range(bits_of(env[1]))],
        "x": [("d", 1)],
        "z": [("d", 2)] if bits_of(env[0]) > 2 else [],
    }
    return [stage for letter in order for stage in kinds[letter]]


def ladder_step(cur, alive, stage, env, anchor):
    nd, nf, me, mine = env
    kind, b = stage
    if kind == "f":
        pairs = cur.reshape((cur.shape[0] // 2, 2) + cur.shape[1:])
        keep, got = pairs[:, 0], swap(pairs[:, 1], "fsdp", 1 << b, nf)
    else:
        axis = 1 + alive.index(b)
        bit = (me >> b) & 1
        keep = lax.dynamic_index_in_dim(cur, bit, axis, keepdims=False)
        got = swap(lax.dynamic_index_in_dim(cur, bit ^ 1, axis, keepdims=False), "dp", 1 << b, nd)
        alive = [d for d in alive if d != b]
    return keep, got, alive


def add_low(keep, got):
    return (keep.astype(jnp.float32) + got.astype(jnp.float32)).astype(jnp.bfloat16)


def finish_rows(done, env):
    nd, nf, me, mine = env
    core = me & 1
    sent = lax.dynamic_index_in_dim(done, core ^ 1, 0, keepdims=False)
    kept = lax.dynamic_index_in_dim(done, core, 0, keepdims=False)
    got = swap(sent, "dp", 1, nd)
    both = jnp.where(
        core == 0,
        jnp.concatenate([kept, got], axis=1),
        jnp.concatenate([got, kept], axis=1),
    )
    return both.T.astype(jnp.float32)


def core_product(dact, act, core, env, rows_only, received=None):
    nd, nf, me, mine = env
    count = 1 if rows_only else nf
    lanes = act.shape[1] // (2 * count)
    blocks = [core] if rows_only else [2 * (mine ^ r) + core for r in range(nf)]
    if lanes % 128 == 0:
        return product(dact, act, blocks, lanes, received)
    wide = jnp.concatenate(list(dact), axis=1)
    parts = [lax.dynamic_slice_in_dim(act, b * lanes, lanes, 1) for b in blocks]
    out = jnp.stack([dot(wide, p, TN) for p in parts])
    if received is not None:
        out = out + received.astype(jnp.float32)
    return out.astype(jnp.bfloat16)


class Reduction:
    def __init__(self, dact, act, portions, env, rows_only=False):
        self.env, self.dact, self.act = env, dact, act
        self.portions, self.rows_only = portions, rows_only
        nd, core = env[0], env[2] & 1
        self.partial = core_product(dact, act, core ^ 1, env, rows_only)
        self.sent = swap(self.partial, "dp", 1, nd)
        self.tie = [self.partial]
        self.flight = None
        self.done = False

    def launch(self):
        if not any(stages for _, _, stages in self.ladders):
            if len(self.ladders) > 1:
                alive = self.ladders[0][1]
                self.ladders = [
                    (jnp.concatenate([cur for cur, _, _ in self.ladders], axis=-1), alive, [])
                ]
            cur, alive, _ = self.ladders[0]
            if not alive:
                self.done = True
                return
            self.ladders = [(cur, alive, [("d", alive[-1])])]
        self.flight = [
            ladder_step(cur, alive, stages[0], self.env, None) + (stages[1:],)
            for cur, alive, stages in self.ladders
        ]

    def step(self, anchor):
        if self.done:
            return
        nd, bits = self.env[0], bits_of(self.env[0])
        if self.flight is None:
            core = self.env[2] & 1
            sent = after(self.sent, anchor)
            total = core_product(self.dact, self.act, core, self.env, self.rows_only, sent)
            total = total.reshape(
                (total.shape[0],) + (2,) * bits + (total.shape[1] // nd, total.shape[2])
            )
            alive = list(range(bits - 1, 0, -1))
            self.ladders, start = [], 0
            for width, order in self.portions:
                stages = stages_of(order, self.env)
                self.ladders.append((total[..., start : start + width], alive, stages))
                start += width
            self.tie = [total]
        else:
            self.ladders = []
            for keep, got, alive, stages in self.flight:
                self.ladders.append((add_low(keep, after(got, anchor)), alive, stages))
            self.tie = [cur for cur, _, _ in self.ladders]
        self.launch()

    def finish(self, anchor):
        while not self.done:
            self.step(anchor)
            anchor = self.tie[0]
        return finish_rows(self.ladders[0][0][0], self.env)


def then(value, anchor, *reductions):
    ties = [anchor]
    for r in reductions:
        if not r.done:
            r.step(anchor)
            ties += r.tie
    return after(value, *ties)


def portion_list(lanes, names):
    units = lanes // 128
    if lanes % 128 or units < len(names):
        return [(lanes, names[-1])]
    cuts = [units * i // len(names) * 128 for i in range(len(names) + 1)]
    return [(b - a, n) for a, b, n in zip(cuts, cuts[1:], names)]


def per_device(
    tokens,
    caption,
    modulation,
    caption_mask,
    positions,
    w_qkv,
    w_out,
    w_caption_kv,
    w_gate_up,
    w_down,
    norm_gains,
    caption_gain,
    cross_gate,
    cotangent,
):
    nd, nf = lax.axis_size("dp"), lax.axis_size("fsdp")
    me, mine = lax.axis_index("dp"), lax.axis_index("fsdp")
    env = (nd, nf, me, mine)
    own_rows = tokens.shape[1]
    heads = cross_gate.shape[0]
    which = (mine if special(env) else jnp.int32(0)).astype(jnp.int32)[None]
    pack = jnp.concatenate(
        [
            norm_gains,
            modulation[0],
            caption_gain[None],
            jnp.pad(cross_gate, (0, caption_gain.shape[0] - heads))[None],
        ]
    )
    pack = gather_small(pack, env)
    places = gather_relative(positions[0].T, env)
    gath_qkv, firsts = gather_pieces(w_qkv, [(1, 2, 0), (2, 1, 0)], env)
    tokens_all = gather_relative(after(tokens[0], *firsts), env)
    partial_kv = dot(caption[0], w_caption_kv)
    tokens_all = after(tokens_all, partial_kv)
    late = tuple(gath_qkv[1]) + (tokens_all, pack, places)
    full_gate_up, got = gather_half(w_gate_up, env, firsts, late)
    full_out, _ = gather_half(w_out, env, (got,), late)
    pack = pack.astype(jnp.float32)
    gains, mods, cap_gain = pack[:6], pack[6:12], pack[12]
    gate_heads = jnp.tanh(pack[13].reshape(nf, -1)[:, :heads].reshape(HEADS))
    gate_tanh = jnp.repeat(gate_heads, HEAD_DIM)[None]
    cosine, sine = rope_tables(places)
    hm, full_qkv, query_b, key_b, value_b, query_pre, key_pre = project(
        tokens_all, own_rows, gains, mods, cosine, sine, gath_qkv
    )
    cap_rows = sum_fsdp(after(partial_kv, tokens_all), env, hm)
    ckey_pre = cap_rows[:, :D]
    ckey_scale = rms_scale(ckey_pre)
    ckey_b = (ckey_pre * ckey_scale * cap_gain).astype(jnp.bfloat16)
    cvalue_b = cap_rows[:, D:].astype(jnp.bfloat16)
    bias = jnp.where(caption_mask[0] > 0, 0.0, -1e30).astype(jnp.float32)
    combined, self_out, cross_out, stats = attend(
        query_b, key_b, value_b, ckey_b, cvalue_b, bias[None], gate_tanh
    )
    full_down, _ = gather_half(w_down, env, (cvalue_b,), (stats,))
    projected, middle, ffn_in = output_step(which, combined, full_out, tokens[0], gains, mods)
    gate_part, up_part, ffn_inner = gate_up_step(which, ffn_in, full_gate_up)
    block_out, grad_down, down_sums = down_step(
        which, ffn_inner, full_down, middle, cotangent[0], gains, mods
    )
    lanes_d, lanes_f = D // (2 * nf), FF // (2 * nf)
    red_down = Reduction(grad_down[None], ffn_inner, portion_list(lanes_f, ORDERS), env)
    grad_down = after(grad_down, red_down.partial)
    grad_gate_up = gate_up_back(which, grad_down, gate_part, up_part, full_down)
    dgu = then(grad_gate_up, grad_gate_up, red_down)
    red_gate_up = Reduction(dgu, ffn_in, portion_list(lanes_d, ORDERS), env)
    dgu = after(dgu, red_gate_up.partial)
    grad_mid, grad_proj, grad_comb, ffn_sums = ffn_back(
        which, dgu, full_gate_up, full_out, middle, cotangent[0], projected, gains, mods
    )
    grad_comb = then(grad_comb, ffn_sums, red_down)
    dq_cross, grad_ckey, grad_cvalue, gate_sums = cross_back(
        query_b, ckey_b, cvalue_b, bias[:, None], gate_tanh, stats, grad_comb, cross_out
    )
    gate_terms = gate_sums[0].reshape(HEADS, HEAD_DIM).sum(axis=-1) * (1.0 - gate_heads**2)
    grad_ckey_pre, cap_gain_terms = norm_back(
        grad_ckey.astype(jnp.float32), ckey_pre, ckey_scale, cap_gain
    )
    grad_cap_kv = jnp.concatenate([grad_ckey_pre, grad_cvalue.astype(jnp.float32)], axis=-1)
    grad_cap_kv = grad_cap_kv.astype(jnp.bfloat16)
    tied = then(gate_sums, grad_cap_kv, red_down)
    grad_comb = then(grad_comb, tied, red_gate_up)
    red_out = Reduction(
        after(grad_proj, grad_comb)[None], combined, portion_list(lanes_d, ORDERS[2:]), env
    )
    grad_comb = then(grad_comb, red_out.partial, red_down)
    pairs = D // PAIR
    each = pairs // 4
    parts = []

    def attention_part(grads):
        parts.append(
            self_back(query_b, key_b, value_b, stats, grads, self_out, dq_cross, len(parts) * each, each)
        )
        return parts[-1][0]

    done = attention_part(grad_comb)
    grad_comb = then(grad_comb, done, red_down, red_out)
    done = attention_part(grad_comb)
    grad_cap_kv = sum_fsdp(grad_cap_kv.astype(jnp.float32), env, done).astype(jnp.bfloat16)
    red_caption = Reduction(
        grad_cap_kv[None], caption[0], portion_list(caption.shape[2] // 2, ["xz", "zx"]), env, True
    )
    grad_comb = after(grad_comb, red_caption.partial)
    done = attention_part(grad_comb)
    grad_comb = then(grad_comb, done, red_gate_up, red_out)
    done = then(grad_comb, done, red_caption)
    done = attention_part(done)
    grad_query, grad_key, grad_value = zip(*parts)
    grad_query = (then(grad_query[0], done, red_out),) + grad_query[1:]
    grad_mixed, qk_sums = qk_back(
        grad_query, grad_key, grad_value, query_pre, key_pre, cosine, sine, gains
    )
    grad_mixed = then(grad_mixed, qk_sums, red_gate_up)
    red_qkv = Reduction(grad_mixed[None], hm, portion_list(lanes_d, ORDERS), env)
    grad_mixed = then(grad_mixed, red_qkv.partial, red_gate_up, red_out)
    dx_other, other_sums = project_back(
        grad_mixed, own_rows, own_rows, tokens_all, full_qkv, gains, mods
    )
    grad_mixed = then(grad_mixed, other_sums, red_caption, red_qkv)
    dx_own, own_sums = project_back(grad_mixed, 0, own_rows, tokens_all, full_qkv, gains, mods)
    grad_cap_kv = then(grad_cap_kv, own_sums, red_caption, red_gate_up, red_out)
    grad_caption = dot(grad_cap_kv, w_caption_kv, NT).astype(jnp.bfloat16)
    anchor = grad_caption
    red_qkv.step(anchor)
    project_sums = own_sums + other_sums if nf > 1 else own_sums
    grad_inputs = jnp.concatenate([dx_own, dx_other]) if nf > 1 else dx_own
    grad_tokens = (grad_mid + reduce_relative(grad_inputs, env)).astype(jnp.bfloat16)
    small = jnp.concatenate(
        [
            project_sums[:1],
            qk_sums[1:3],
            jnp.stack(
                [
                    ffn_sums[4],
                    ffn_sums[2],
                    down_sums[1],
                    jnp.sum(cap_gain_terms, axis=0),
                    jnp.pad(gate_terms, (0, D - HEADS)),
                ]
            ),
        ]
    )
    small = sum_wide(small, ("fsdp", "dp"), env)
    mod_grads = jnp.stack(
        [
            project_sums[3],
            project_sums[4],
            ffn_sums[3] * (1.0 - jnp.tanh(mods[2]) ** 2),
            ffn_sums[0],
            ffn_sums[1],
            down_sums[0] * (1.0 - jnp.tanh(mods[5]) ** 2),
        ]
    )
    mod_grads = sum_wide(mod_grads, ("fsdp",), env)
    outs = []
    for r in (red_down, red_gate_up, red_out, red_caption, red_qkv):
        outs.append(r.finish(anchor))
    out_down, out_gate_up, out_out, out_caption, out_qkv = outs
    width = D // nf
    return (
        block_out[None],
        grad_tokens[None],
        grad_caption[None],
        lax.dynamic_slice_in_dim(mod_grads, mine * width, width, 1)[None],
        out_qkv,
        out_out,
        out_caption,
        out_gate_up,
        out_down,
        lax.dynamic_slice_in_dim(small[:6], mine * width, width, 1),
        lax.dynamic_slice_in_dim(small[6], mine * width, width, 0),
        lax.dynamic_slice_in_dim(small[7], mine * heads, heads, 0),
    )


def solution(mesh):
    placed = (
        P("dp", "fsdp", None),
        P("dp", None, "fsdp"),
        P("dp", None, "fsdp"),
        P("dp", None),
        P("dp", None, "fsdp"),
        P("fsdp", None),
        P("fsdp", None),
        P("fsdp", None),
        P("fsdp", None),
        P("fsdp", None),
        P(None, "fsdp"),
        P("fsdp"),
        P("fsdp"),
        P("dp", "fsdp", None),
    )
    return jax.shard_map(
        per_device,
        mesh=mesh,
        in_specs=placed,
        out_specs=(
            P("dp", "fsdp", None),
            P("dp", "fsdp", None),
            P("dp", None, "fsdp"),
            P("dp", None, "fsdp"),
            P("fsdp", "dp"),
            P("fsdp", "dp"),
            P("fsdp", "dp"),
            P("fsdp", "dp"),
            P("fsdp", "dp"),
            P(None, "fsdp"),
            P("fsdp"),
            P("fsdp"),
        ),
        check_vma=False,
    )
```

time: 2420 us -> 900 us (0.37)
  waiting for transfers between devices: 1650 us -> 247 us
  Pallas kernels: 0 us -> 395 us
  matrix products: 365 us -> 14.2 us
  other arithmetic: 160 us -> 71 us
  blocking collectives: 86.5 us -> 0 us
  starting transfers between devices: 0.86 us -> 70.9 us
  local copies, waits for them, and re-layouts: 137 us -> 80.2 us
    reduce_scatter x10 -> x0, waiting for transfers between devices: 866 us -> none  [the longest x1 271 us: per_device(): lax.psum_scatter(grad_w_gate_up.astype(jnp.bfloat16), 'fsdp', scatter_dim...]
    all_gather x7 -> x3, waiting for transfers between devices: 594 us -> 7.47 us  [gather_half(): lax.all_gather(got, 'dp', axis=0, tiled=True, axis_index_groups=groups)]
    pallas_call x0 -> x25, Pallas kernels: none -> 395 us  [the longest x10 114 us: product(): pl.pallas_call(product_kernel, grid_spec=pltpu.PrefetchScalarGridSpec(num...]
    dot_general x26 -> x2, matrix products: 356 us -> 14.2 us  [dot(): return lax.dot_general(a, b, dims, preferred_element_type=jnp.float32)]
    ppermute x0 -> x80, waiting for transfers between devices: none -> 239 us  [swap(): return lax.ppermute(value, axis, [(i, i ^ mask) for i in range(size)])]
    unnamed x25 -> x3, waiting for transfers between devices: 185 us -> 0.73 us
    ppermute x0 -> x80, starting transfers between devices: none -> 70.2 us  [swap(): return lax.ppermute(value, axis, [(i, i ^ mask) for i in range(size)])]
    psum x1 -> x0, blocking collectives: 61.7 us -> none  [per_device(): lax.psum((shard_grads[2], shard_grads[3], shard_grads[5]), 'dp')]
  transfers between devices with their start and end apart: 21 -> 83, of which waited for: 15 -> 35; matrix products, arithmetic and copies ran while one was open for 22% -> 16% of each run, Pallas kernels for 0% -> 33%
where the time goes in v1:
time: 900 us; the launch traced here: 894 us
  Pallas kernels  395 us (44%)
  waiting for transfers between devices  247 us (27%)
  local copies, waits for them, and re-layouts  80.2 us (9%)
  other arithmetic  71 us (8%)
  starting transfers between devices  70.9 us (8%)
  between operations  15.6 us (2%)
  matrix products  14.2 us (2%)
    ppermute x80, waiting for transfers between devices, swap(): return lax.ppermute(value, axis, [(i, i ^ mask) for i in range(size)])  239 us
    pallas_call x10, Pallas kernels, product(): pl.pallas_call(product_kernel, grid_spec=pltpu.PrefetchScalarGridSpec(num...  114 us
    ppermute x80, starting transfers between devices, swap(): return lax.ppermute(value, axis, [(i, i ^ mask) for i in range(size)])  70.2 us
    pallas_call x4, Pallas kernels, self_back(): pl.pallas_call(self_back_kernel, grid=(count,), in_specs=[spec(rows), spe...  45.1 us
    pallas_call x1, Pallas kernels, attend(): pl.pallas_call(attend_kernel, grid=(pairs,), in_specs=[spec(rows), spec(k...  42.1 us
    pallas_call x1, Pallas kernels, ffn_back(): pl.pallas_call(ffn_back_kernel, grid_spec=pltpu.PrefetchScalarGridSpec(nu...  35.2 us
    convert_element_type x37, other arithmetic, add_low(): (keep.astype(jnp.float32) + got.astype(jnp.float32)).astype(jnp.bfloat16)  35.2 us
    pallas_call x1, Pallas kernels, project(): pl.pallas_call(functools.partial(project_kernel, len(pieces), own_rows),...  35 us
  transfers between devices with their start and end apart: 83, of which 35 were waited for; matrix products, arithmetic and copies ran while one was open for 16% of the time, Pallas kernels for 33%

profile of v1, /device:TPU:0, one launch (start us, length us, event | category | flops | bytes accessed | tf_op | source)
XLA Modules:
  0.0 893.5 jit_solution(5887301590355768327)
XLA Ops:
  79.0 27.0 %collective-permute-done.20 = bf16[96,8192]{1,0:T(8,128)(2,1)} collective-permute-done((bf16[96,8192]{1,0:T(8,128)(2,1)}, bf16[96,8192]{1,0:T(8,128)(2,1)}, u32[]{:S(2)}, u32[]{:S(2)}) %collective-permute-start.20) | collective-permute-done | bytes 1572896 | tf_op jit(solution)/shard_map/ppermute | solution.py:731
  124.7 35.0 %shard_map.229 = (bf16[1024,1536]{1,0:T(8,128)(2,1)}, bf16[1536,4608]{1,0:T(8,128)(2,1)}, bf16[512,1536]{1,0:T(8,128)(2,1)}, bf16[1024,1536]{1,0:T(8,128)(2,1)},...) custom-call(s32[17]{0:T(128)} %stack.125.where_ref, ...), custom_call_target="tpu_custom_call" | custom-call | flops 603979776 | bytes 3000000 | tf_op jit(solution)/shard_map/pallas_call | solution.py:330
  164.2 42.1 %shard_map.230 = (bf16[512,1536]{1,0:T(8,128)(2,1)S(1)}, bf16[512,1536]{1,0:T(8,128)(2,1)S(1)}, bf16[512,1536]{1,0:T(8,128)(2,1)}, f32[12,8,512]{2,1,0:T(8,128)S(1)}) custom-call(bf16[512,1536]{1,0:T(8,128)(2,1)} %get-tuple-element.132.q_ref, bf16[1024,1536]{1,0:T(8,128)(2,1)} %get-tuple-element.133.k_ref, bf16[1024,1536]{1,0:T(8,128)(2,1)} %get-tuple-element.134.v_ref, ...), custom_call_target="tpu_custom_call" | custom-call | flops 805306368 | bytes 1000000 | tf_op jit(solution)/shard_map/pallas_call | solution.py:86
  219.0 20.7 %shard_map.232 = (bf16[512,4096]{1,0:T(8,128)(2,1)}, bf16[512,4096]{1,0:T(8,128)(2,1)}, bf16[512,4096]{1,0:T(8,128)(2,1)}) custom-call(s32[1]{0:T(128)} %bitcast.which_ref, bf16[512,1536]{1,0:T(8,128)(2,1)} %get-tuple-element.143.h_ref.a_ref, bf16[768,8192]{1,0:T(8,128)(2,1)} %u0_ref.3, bf16[768,8192]{1,0:T(8,128)(2,1)} %all-gather.6.cloned.1.call-done.g1_ref.u1_ref, ...), custom_call_target="tpu_custom_call" | custom-call | flops 644245120 | bytes 2000000 | tf_op jit(solution)/shard_map/pallas_call | solution.py:398
  247.1 18.2 %shard_map.233 = (bf16[512,1536]{1,0:T(8,128)(2,1)}, bf16[512,1536]{1,0:T(8,128)(2,1)}, f32[8,1536]{1,0:T(8,128)}) custom-call(s32[1]{0:T(128)} %bitcast.which_ref, bf16[512,4096]{1,0:T(8,128)(2,1)} %get-tuple-element.144.ff_ref.a_ref, bf16[2048,1536]{1,0:T(8,128)(2,1)} %d0_ref.1, bf16[2048,1536]{1,0:T(8,128)(2,1)} %all-gather.8.cloned.1.call-done.w1_ref.d1_ref, ...), custom_call_target="tpu_custom_call" | custom-call | flops 322122560 | bytes 1200000 | tf_op jit(solution)/shard_map/pallas_call | solution.py:449
  274.4 17.4 %shard_map.235.d_ref.dgu_ref = bf16[2,512,4096]{2,1,0:T(8,128)(2,1)} custom-call(s32[1]{0:T(128)} %bitcast.which_ref, bf16[512,1536]{1,0:T(8,128)(2,1)} %get-tuple-element.151.df_ref, bf16[512,4096]{1,0:T(8,128)(2,1)} %get-tuple-element.152.ga_ref, bf16[512,4096]{1,0:T(8,128)(2,1)} %get-tuple-element.153.up_ref, bf16[2048,1536]{1,0:T(8,128)(2,1)} %d0_ref.1, ...), custom_call_target="tpu_custom_call" | custom-call | flops 322122560 | bytes 1500000 | tf_op jit(solution)/shard_map/pallas_call | solution.py:494
  291.8 9.6 %shard_map.236 = bf16[2,1536,1024]{2,1,0:T(8,128)(2,1)} custom-call(s32[2]{0:T(128)} %pad_add_fusion.2.where_ref, bf16[1,512,1536]{2,1,0:T(8,128)(2,1)} %bitcast.340, bf16[512,4096]{1,0:T(8,128)(2,1)} %get-tuple-element.144.ff_ref.a_ref, bf16[2,1536,1024]{2,1,0:T(8,128)(2,1)} %collective-permute-done.23.refs_0_), custom_call_target="tpu_custom_call" | custom-call | flops 161061280 | bytes 629145 | tf_op jit(solution)/shard_map/pallas_call | solution.py:703
  301.4 16.7 %shard_map.237 = bf16[2,8192,384]{2,1,0:T(8,128)(2,1)} custom-call(s32[2]{0:T(128)} %pad_add_fusion.1.where_ref, bf16[2,512,4096]{2,1,0:T(8,128)(2,1)} %shard_map.235.d_ref.dgu_ref, bf16[512,1536]{1,0:T(8,128)(2,1)} %get-tuple-element.143.h_ref.a_ref), custom_call_target="tpu_custom_call" | custom-call | flops 322122560 | bytes 1258291 | tf_op jit(solution)/shard_map/pallas_call | solution.py:703
  331.2 35.2 %shard_map.238 = (f32[512,1536]{1,0:T(8,128)}, bf16[512,1536]{1,0:T(8,128)(2,1)}, bf16[512,1536]{1,0:T(8,128)(2,1)}, f32[8,1536]{1,0:T(8,128)}) custom-call(s32[1]{0:T(128)} %bitcast.which_ref, bf16[2,512,4096]{2,1,0:T(8,128)(2,1)} %shard_map.235.d_ref.dgu_ref, bf16[768,8192]{1,0:T(8,128)(2,1)} %u0_ref.3, ...), custom_call_target="tpu_custom_call" | custom-call | flops 765041024 | bytes 2750000 | tf_op jit(solution)/shard_map/pallas_call | solution.py:573
  374.2 13.7 %shard_map.239 = (bf16[512,1536]{1,0:T(8,128)(2,1)S(1)}, bf16[256,1536]{1,0:T(8,128)(2,1)S(1)}, bf16[256,1536]{1,0:T(8,128)(2,1)S(1)}, f32[1,1536]{1,0:T(1,128)S(1)}) custom-call(bf16[512,1536]{1,0:T(8,128)(2,1)} %get-tuple-element.132.q_ref, bf16[256,1536]{1,0:T(8,128)(2,1)S(1)} %multiply_convert_fusion.ck_ref, bf16[256,1536]{1,0:T(8,128)(2,1)S(1)} %slice.335.cv_ref, ...), custom_call_target="tpu_custom_call" | custom-call | flops 402653184 | bytes 450000 | tf_op jit(solution)/shard_map/pallas_call | solution.py:170
  391.1 20.5 %shard_map.240 = bf16[2,8192,384]{2,1,0:T(8,128)(2,1)} custom-call(s32[2]{0:T(128)} %pad_add_fusion.2.where_ref, bf16[2,512,4096]{2,1,0:T(8,128)(2,1)} %shard_map.235.d_ref.dgu_ref, bf16[512,1536]{1,0:T(8,128)(2,1)} %get-tuple-element.143.h_ref.a_ref, bf16[2,8192,384]{2,1,0:T(8,128)(2,1)} %collective-permute-done.30.refs_0_), custom_call_target="tpu_custom_call" | custom-call | flops 322122560 | bytes 1258291 | tf_op jit(solution)/shard_map/pallas_call | solution.py:703
  435.3 11.5 %shard_map.242 = (bf16[512,384]{1,0:T(8,128)(2,1)S(1)}, bf16[1024,384]{1,0:T(8,128)(2,1)S(1)}, bf16[1024,384]{1,0:T(8,128)(2,1)S(1)}) custom-call(bf16[512,1536]{1,0:T(8,128)(2,1)S(1)} %copy-done, bf16[1024,1536]{1,0:T(8,128)(2,1)} %get-tuple-element.133.k_ref, bf16[1024,1536]{1,0:T(8,128)(2,1)} %get-tuple-element.134.v_ref, ...), custom_call_target="tpu_custom_call" | custom-call | flops 805306368 | bytes 150000 | tf_op jit(solution)/shard_map/pallas_call | solution.py:191
  459.2 11.2 %shard_map.244 = (bf16[512,384]{1,0:T(8,128)(2,1)S(1)}, bf16[1024,384]{1,0:T(8,128)(2,1)S(1)}, bf16[1024,384]{1,0:T(8,128)(2,1)S(1)}) custom-call(bf16[512,1536]{1,0:T(8,128)(2,1)S(1)} %copy-done, bf16[1024,1536]{1,0:T(8,128)(2,1)} %get-tuple-element.133.k_ref, bf16[1024,1536]{1,0:T(8,128)(2,1)} %get-tuple-element.134.v_ref, ...), custom_call_target="tpu_custom_call" | custom-call | flops 805306368 | bytes 150000 | tf_op jit(solution)/shard_map/pallas_call | solution.py:191
  498.6 11.3 %shard_map.246 = (bf16[512,384]{1,0:T(8,128)(2,1)S(1)}, bf16[1024,384]{1,0:T(8,128)(2,1)S(1)}, bf16[1024,384]{1,0:T(8,128)(2,1)S(1)}) custom-call(bf16[512,1536]{1,0:T(8,128)(2,1)S(1)} %copy-done, bf16[1024,1536]{1,0:T(8,128)(2,1)} %get-tuple-element.133.k_ref, bf16[1024,1536]{1,0:T(8,128)(2,1)} %get-tuple-element.134.v_ref, ...), custom_call_target="tpu_custom_call" | custom-call | flops 805306368 | bytes 150000 | tf_op jit(solution)/shard_map/pallas_call | solution.py:191
  509.9 26.4 %collective-permute-done.39 = bf16[2,2,2,2,512,128]{5,4,3,2,1,0:T(8,128)(2,1)} collective-permute-done((bf16[2,2,2,2,512,128]{5,4,3,2,1,0:T(8,128)(2,1)}, bf16[2,2,2,2,512,128]{5,4,3,2,1,0:T(8,128)(2,1)}, u32[]{:S(2)}, u32[]{:S(2)}) %collective-permute-start.39) | collective-permute-done | bytes 2097184 | tf_op jit(solution)/shard_map/ppermute | solution.py:731
  577.5 11.1 %shard_map.248 = (bf16[512,384]{1,0:T(8,128)(2,1)S(1)}, bf16[1024,384]{1,0:T(8,128)(2,1)S(1)}, bf16[1024,384]{1,0:T(8,128)(2,1)S(1)}) custom-call(bf16[512,1536]{1,0:T(8,128)(2,1)S(1)} %copy-done, bf16[1024,1536]{1,0:T(8,128)(2,1)} %get-tuple-element.133.k_ref, bf16[1024,1536]{1,0:T(8,128)(2,1)} %get-tuple-element.134.v_ref, ...), custom_call_target="tpu_custom_call" | custom-call | flops 805306368 | bytes 150000 | tf_op jit(solution)/shard_map/pallas_call | solution.py:191
  592.1 14.1 %shard_map.249 = (bf16[1024,4608]{1,0:T(8,128)(2,1)}, f32[8,1536]{1,0:T(8,128)}) custom-call(bf16[512,384]{1,0:T(8,128)(2,1)} %copy-done.15, bf16[512,384]{1,0:T(8,128)(2,1)} %copy-done.16, bf16[512,384]{1,0:T(8,128)(2,1)} %copy-done.17, bf16[512,384]{1,0:T(8,128)(2,1)} %copy-done.18, bf16[1024,384]{1,0:T(8,128)(2,1)} %copy-done.7, ...), custom_call_target="tpu_custom_call" | custom-call | flops 4718592 | bytes 1500000 | tf_op jit(solution)/shard_map/pallas_call | solution.py:636
  611.2 16.4 %shard_map.250 = bf16[2,4608,384]{2,1,0:T(8,128)(2,1)} custom-call(s32[2]{0:T(128)} %pad_add_fusion.1.where_ref, bf16[1,1024,4608]{2,1,0:T(8,128)(2,1)} %bitcast.330, bf16[1024,1536]{1,0:T(8,128)(2,1)} %get-tuple-element.136.a_ref), custom_call_target="tpu_custom_call" | custom-call | flops 362387872 | bytes 707788 | tf_op jit(solution)/shard_map/pallas_call | solution.py:703
  666.2 14.1 %shard_map.251 = (bf16[512,1536]{1,0:T(8,128)(2,1)}, f32[8,1536]{1,0:T(8,128)}) custom-call(bf16[1024,4608]{1,0:T(8,128)(2,1)} %get-tuple-element.227.dqkv_ref, bf16[1024,1536]{1,0:T(8,128)(2,1)} %pad_maximum_fusion.tok_ref, bf16[1536,4608]{1,0:T(8,128)(2,1)} %get-tuple-element.222.w_ref, f32[6,1536]{1,0:T(8,128)} %get-tuple-element.285.gain_ref.refs_16_, ...), custom_call_target="tpu_custom_call" | custom-call | flops 362387872 | bytes 1500000 | tf_op jit(solution)/shard_map/pallas_call | solution.py:672
  680.3 34.0 %collective-permute-done.51 = bf16[1,2,2,2,192,512]{5,4,3,2,1,0:T(8,128)(2,1)} collective-permute-done((bf16[1,2,2,2,192,512]{5,4,3,2,1,0:T(8,128)(2,1)}, bf16[1,2,2,2,192,512]{5,4,3,2,1,0:T(8,128)(2,1)}, u32[]{:S(2)}, u32[]{:S(2)}) %collective-permute-start.51) | collective-permute-done | bytes 1572896 | tf_op jit(solution)/shard_map/ppermute | solution.py:731
  723.4 17.9 %shard_map.252 = bf16[2,4608,384]{2,1,0:T(8,128)(2,1)} custom-call(s32[2]{0:T(128)} %pad_add_fusion.2.where_ref, bf16[1,1024,4608]{2,1,0:T(8,128)(2,1)} %bitcast.331, bf16[1024,1536]{1,0:T(8,128)(2,1)} %get-tuple-element.136.a_ref, bf16[2,4608,384]{2,1,0:T(8,128)(2,1)} %collective-permute-done.52.refs_0_), custom_call_target="tpu_custom_call" | custom-call | flops 362387872 | bytes 707788 | tf_op jit(solution)/shard_map/pallas_call | solution.py:703
  741.3 16.3 %shard_map.253 = (bf16[512,1536]{1,0:T(8,128)(2,1)}, f32[8,1536]{1,0:T(8,128)}) custom-call(bf16[1024,4608]{1,0:T(8,128)(2,1)} %get-tuple-element.227.dqkv_ref, bf16[1024,1536]{1,0:T(8,128)(2,1)} %pad_maximum_fusion.tok_ref, bf16[1536,4608]{1,0:T(8,128)(2,1)} %get-tuple-element.222.w_ref, f32[6,1536]{1,0:T(8,128)} %get-tuple-element.285.gain_ref.refs_16_, ...), custom_call_target="tpu_custom_call" | custom-call | flops 362387872 | bytes 1500000 | tf_op jit(solution)/shard_map/pallas_call | solution.py:672
  820.9 18.1 %collective-permute-done.62 = bf16[2,2,2,2,288,128]{5,4,3,1,0,2:T(8,128)(2,1)S(1)} collective-permute-done((bf16[2,2,2,2,288,128]{5,4,3,1,0,2:T(8,128)(2,1)S(1)}, bf16[2,2,2,2,288,128]{5,4,3,1,0,2:T(8,128)(2,1)S(1)}, u32[]{:S(2)}, u32[]{:S(2)}) %collective-permute-start.62) | collective-permute-done | bytes 1179680 | tf_op jit(solution)/shard_map/ppermute | solution.py:731
  871.1 12.9 %collective-permute-done.68 = bf16[1,2,288,384]{3,2,1,0:T(8,128)(2,1)S(1)} collective-permute-done((bf16[1,2,288,384]{3,2,1,0:T(8,128)(2,1)S(1)}, bf16[1,2,288,384]{3,2,1,0:T(8,128)(2,1)S(1)}, u32[]{:S(2)}, u32[]{:S(2)}) %collective-permute-start.68) | collective-permute-done | bytes 442400 | tf_op jit(solution)/shard_map/ppermute | solution.py:731
  (482 shorter events, 406.7 us)
Async XLA Ops:
  7.2 203.0 %all-gather.4.cloned.1.call-start = ((), (), s32[]{:S(2)}) async-start(), calls=%async_computation | async-start | bytes 2654208 | tf_op jit(solution)/shard_map/all_gather | solution.py:778
  39.1 66.9 %collective-permute-start.20 = (bf16[96,8192]{1,0:T(8,128)(2,1)}, bf16[96,8192]{1,0:T(8,128)(2,1)}, u32[]{:S(2)}, u32[]{:S(2)}) collective-permute-start(bf16[96,8192]{1,0:T(8,128)(2,1)} %constant_dynamic-slice_fusion.14), channel_id=1, source_target_pairs={{0,1},{1,0},{2,3},{3,2},{4,5},{5,4},{6,7},{7,6},{8,9},{9,8},{10,11... | collective-permute-start | bytes 4718600 | tf_op jit(solution)/shard_map/ppermute | solution.py:731
  113.0 106.0 %all-gather.6.cloned.1.call-start = ((), (), s32[]{:S(2)}) async-start(), calls=%async_computation.1 | async-start | bytes 14155776 | tf_op jit(solution)/shard_map/all_gather | solution.py:778
  113.8 133.3 %all-gather.8.cloned.1.call-start = ((), (), s32[]{:S(2)}) async-start(), calls=%async_computation.2 | async-start | bytes 7077888 | tf_op jit(solution)/shard_map/all_gather | solution.py:778
  163.4 45.3 %collective-permute-start.22 = (bf16[256,1536]{1,0:T(8,128)(2,1)S(1)}, bf16[256,1536]{1,0:T(8,128)(2,1)S(1)}, u32[]{:S(2)}, u32[]{:S(2)}) collective-permute-start(bf16[256,1536]{1,0:T(8,128)(2,1)S(1)} %copy-done.49), channel_id=1, source_target_pairs={{0,1},{1,0},{2,3},{3,2},{4,5},{5,4},{6,7},{7,6},{8,9},{9,8},{10,11... | collective-permute-start | bytes 2359304 | tf_op jit(solution)/shard_map/ppermute | solution.py:731
  318.1 73.0 %collective-permute-start.30 = (bf16[2,8192,384]{2,1,0:T(8,128)(2,1)}, bf16[2,8192,384]{2,1,0:T(8,128)(2,1)}, u32[]{:S(2)}, u32[]{:S(2)}) collective-permute-start(bf16[2,8192,384]{2,1,0:T(8,128)(2,1)} %shard_map.237), channel_id=1, source_target_pairs={{0,2},{2,0},{4,6},{6,4},{8,10},{10,8},{12,14},{14,12},{16,18},{18,... | collective-permute-start | bytes 37748744 | tf_op jit(solution)/shard_map/ppermute | solution.py:731
  322.7 46.6 %collective-permute-start.26 = (bf16[2,2,2,2,96,384]{5,4,3,2,1,0:T(8,128)(2,1)}, bf16[2,2,2,2,96,384]{5,4,3,2,1,0:T(8,128)(2,1)}, u32[]{:S(2)}, u32[]{:S(2)}) collective-permute-start(bf16[2,2,2,2,96,384]{5,4,3,2,1,0:T(8,128)(2,1)} %dynamic-slice_bitcast_fusion.4), channel_id=1, source_target_pairs={{0,8},{2,10},{4,12},{6,14},{8,0},{10,2},{12,4},{14,6},{16,24},{18,... | collective-permute-start | bytes 3538952 | tf_op jit(solution)/shard_map/ppermute | solution.py:731
  420.7 49.8 %collective-permute-start.36 = (bf16[256,3072]{1,0:T(8,128)(2,1)}, bf16[256,3072]{1,0:T(8,128)(2,1)}, u32[]{:S(2)}, u32[]{:S(2)}) collective-permute-start(bf16[256,3072]{1,0:T(8,128)(2,1)} %pad_maximum_fusion.1), channel_id=1, source_target_pairs={{0,1},{1,0},{2,3},{3,2},{4,5},{5,4},{6,7},{7,6},{8,9},{9,8},{10,11... | collective-permute-start | bytes 4718600 | tf_op jit(solution)/shard_map/ppermute | solution.py:731
  480.6 89.2 %collective-permute-start.41 = (bf16[1,3072,1024]{2,1,0:T(8,128)(2,1)}, bf16[1,3072,1024]{2,1,0:T(8,128)(2,1)}, u32[]{:S(2)}, u32[]{:S(2)}) collective-permute-start(bf16[1,3072,1024]{2,1,0:T(8,128)(2,1)} %shard_map.245), channel_id=1, source_target_pairs={{0,2},{2,0},{4,6},{6,4},{8,10},{10,8},{12,14},{14,12},{16,18},{18,... | collective-permute-start | bytes 18874376 | tf_op jit(solution)/shard_map/ppermute | solution.py:731
  487.5 48.7 %collective-permute-start.39 = (bf16[2,2,2,2,512,128]{5,4,3,2,1,0:T(8,128)(2,1)}, bf16[2,2,2,2,512,128]{5,4,3,2,1,0:T(8,128)(2,1)}, u32[]{:S(2)}, u32[]{:S(2)}) collective-permute-start(bf16[2,2,2,2,512,128]{5,4,3,2,1,0:T(8,128)(2,1)} %dynamic-slice_bitcast_fusion), channel_id=1, source_target_pairs={{0,8},{2,10},{4,12},{6,14},{8,0},{10,2},{12,4},{14,6},{16,24},{18,... | collective-permute-start | bytes 6291464 | tf_op jit(solution)/shard_map/ppermute | solution.py:731
  491.4 48.1 %collective-permute-start.38 = (bf16[2,2,2,2,512,128]{5,4,3,1,0,2:T(8,128)(2,1)}, bf16[2,2,2,2,512,128]{5,4,3,1,0,2:T(8,128)(2,1)}, u32[]{:S(2)}, u32[]{:S(2)}) collective-permute-start(bf16[2,2,2,2,512,128]{5,4,3,1,0,2:T(8,128)(2,1)} %bitcast.325), channel_id=1, source_target_pairs={{0,4},{2,6},{4,0},{6,2},{8,12},{10,14},{12,8},{14,10},{16,20},{18,... | collective-permute-start | bytes 6291464 | tf_op jit(solution)/shard_map/ppermute | solution.py:731
  494.0 48.1 %collective-permute-start.37 = (bf16[1,2,2,2,2,512,128]{6,5,4,1,2,3,0:T(8,128)(2,1)}, bf16[1,2,2,2,2,512,128]{6,5,4,1,2,3,0:T(8,128)(2,1)}, u32[]{:S(2)}, u32[]{:S(2)}) collective-permute-start(bf16[1,2,2,2,2,512,128]{6,5,4,1,2,3,0:T(8,128)(2,1)} %slice_bitcast_fusion), channel_id=1, source_target_pairs={{0,1},{1,0},{2,3},{3,2},{4,5},{5,4},{6,7},{7,6},{8,9},{9,8},{10,11... | collective-permute-start | bytes 6291464 | tf_op jit(solution)/shard_map/ppermute | solution.py:731
  496.6 65.0 %collective-permute-start.40 = (bf16[2,2,2,2,96,384]{5,4,3,2,1,0:T(8,128)(2,1)}, bf16[2,2,2,2,96,384]{5,4,3,2,1,0:T(8,128)(2,1)}, u32[]{:S(2)}, u32[]{:S(2)}) collective-permute-start(bf16[2,2,2,2,96,384]{5,4,3,2,1,0:T(8,128)(2,1)} %dynamic-slice_bitcast_fusion.3), channel_id=1, source_target_pairs={{0,8},{2,10},{4,12},{6,14},{8,0},{10,2},{12,4},{14,6},{16,24},{18,... | collective-permute-start | bytes 3538952 | tf_op jit(solution)/shard_map/ppermute | solution.py:731
  545.3 60.9 %collective-permute-start.45 = (bf16[1,2,2,2,512,128]{5,4,3,2,1,0:T(8,128)(2,1)}, bf16[1,2,2,2,512,128]{5,4,3,2,1,0:T(8,128)(2,1)}, u32[]{:S(2)}, u32[]{:S(2)}) collective-permute-start(bf16[1,2,2,2,512,128]{5,4,3,2,1,0:T(8,128)(2,1)} %slice_bitcast_fusion.4), channel_id=1, source_target_pairs={{0,1},{1,0},{2,3},{3,2},{4,5},{5,4},{6,7},{7,6},{8,9},{9,8},{10,11... | collective-permute-start | bytes 3145736 | tf_op jit(solution)/shard_map/ppermute | solution.py:731
  550.3 56.0 %collective-permute-start.44 = (bf16[2,2,2,512,128]{4,3,2,1,0:T(8,128)(2,1)}, bf16[2,2,2,512,128]{4,3,2,1,0:T(8,128)(2,1)}, u32[]{:S(2)}, u32[]{:S(2)}) collective-permute-start(bf16[2,2,2,512,128]{4,3,2,1,0:T(8,128)(2,1)} %dynamic-slice_bitcast_fusion.5), channel_id=1, source_target_pairs={{0,8},{2,10},{4,12},{6,14},{8,0},{10,2},{12,4},{14,6},{16,24},{18,... | collective-permute-start | bytes 3145736 | tf_op jit(solution)/shard_map/ppermute | solution.py:731
  627.6 95.8 %collective-permute-start.52 = (bf16[2,4608,384]{2,1,0:T(8,128)(2,1)}, bf16[2,4608,384]{2,1,0:T(8,128)(2,1)}, u32[]{:S(2)}, u32[]{:S(2)}) collective-permute-start(bf16[2,4608,384]{2,1,0:T(8,128)(2,1)} %shard_map.250), channel_id=1, source_target_pairs={{0,2},{2,0},{4,6},{6,4},{8,10},{10,8},{12,14},{14,12},{16,18},{18,... | collective-permute-start | bytes 21233672 | tf_op jit(solution)/shard_map/ppermute | solution.py:731
  650.1 64.2 %collective-permute-start.51 = (bf16[1,2,2,2,192,512]{5,4,3,2,1,0:T(8,128)(2,1)}, bf16[1,2,2,2,192,512]{5,4,3,2,1,0:T(8,128)(2,1)}, u32[]{:S(2)}, u32[]{:S(2)}) collective-permute-start(bf16[1,2,2,2,192,512]{5,4,3,2,1,0:T(8,128)(2,1)} %dynamic-slice_bitcast_fusion.1), channel_id=1, source_target_pairs={{0,8},{2,10},{4,12},{6,14},{8,0},{10,2},{12,4},{14,6},{16,24},{18,... | collective-permute-start | bytes 4718600 | tf_op jit(solution)/shard_map/ppermute | solution.py:731
  660.5 57.1 %collective-permute-start.50 = (bf16[1,2,2,2,192,512]{5,4,3,1,2,0:T(8,128)(2,1)}, bf16[1,2,2,2,192,512]{5,4,3,1,2,0:T(8,128)(2,1)}, u32[]{:S(2)}, u32[]{:S(2)}) collective-permute-start(bf16[1,2,2,2,192,512]{5,4,3,1,2,0:T(8,128)(2,1)} %bitcast.326), channel_id=1, source_target_pairs={{0,4},{2,6},{4,0},{6,2},{8,12},{10,14},{12,8},{14,10},{16,20},{18,... | collective-permute-start | bytes 4718600 | tf_op jit(solution)/shard_map/ppermute | solution.py:731
  661.5 112.2 %collective-permute-start.57 = (bf16[1,2,96,384]{3,2,1,0:T(8,128)(2,1)S(1)}, bf16[1,2,96,384]{3,2,1,0:T(8,128)(2,1)}, u32[]{:S(2)}, u32[]{:S(2)}) collective-permute-start(bf16[1,2,96,384]{3,2,1,0:T(8,128)(2,1)S(1)} %dynamic-slice_bitcast_fusion.29), channel_id=1, source_target_pairs={{0,16},{2,18},{4,20},{6,22},{8,24},{10,26},{12,28},{14,30},{16,0},... | collective-permute-start | bytes 442376 | tf_op jit(solution)/shard_map/ppermute | solution.py:731
  665.2 93.3 %collective-permute-start.56 = (bf16[1,2,512,384]{3,2,1,0:T(8,128)(2,1)}, bf16[1,2,512,384]{3,2,1,0:T(8,128)(2,1)}, u32[]{:S(2)}, u32[]{:S(2)}) collective-permute-start(bf16[1,2,512,384]{3,2,1,0:T(8,128)(2,1)} %dynamic-slice_bitcast_fusion.7), channel_id=1, source_target_pairs={{0,16},{2,18},{4,20},{6,22},{8,24},{10,26},{12,28},{14,30},{16,0},... | collective-permute-start | bytes 2359304 | tf_op jit(solution)/shard_map/ppermute | solution.py:731
  714.3 71.7 %collective-permute-start.53 = (bf16[512,1536]{1,0:T(8,128)(2,1)}, bf16[512,1536]{1,0:T(8,128)(2,1)}, u32[]{:S(2)}, u32[]{:S(2)}) collective-permute-start(bf16[512,1536]{1,0:T(8,128)(2,1)} %get-tuple-element.229), channel_id=1, source_target_pairs={{0,1},{1,0},{2,3},{3,2},{4,5},{5,4},{6,7},{7,6},{8,9},{9,8},{10,11... | collective-permute-start | bytes 4718600 | tf_op jit(solution)/shard_map/ppermute | solution.py:731
  723.4 44.1 %collective-permute-start.54 = (bf16[1,2,2,192,512]{4,3,2,1,0:T(8,128)(2,1)}, bf16[1,2,2,192,512]{4,3,2,1,0:T(8,128)(2,1)}, u32[]{:S(2)}, u32[]{:S(2)}) collective-permute-start(bf16[1,2,2,192,512]{4,3,2,1,0:T(8,128)(2,1)} %dynamic-slice_bitcast_fusion.9), channel_id=1, source_target_pairs={{0,8},{2,10},{4,12},{6,14},{8,0},{10,2},{12,4},{14,6},{16,24},{18,... | collective-permute-start | bytes 2359304 | tf_op jit(solution)/shard_map/ppermute | solution.py:731
  762.3 106.3 %collective-permute-start.73 = (bf16[512,384]{0,1:T(8,128)(2,1)}, bf16[512,384]{0,1:T(8,128)(2,1)}, u32[]{:S(2)}, u32[]{:S(2)}) collective-permute-start(bf16[512,384]{0,1:T(8,128)(2,1)} %bitcast.144), channel_id=1, source_target_pairs={{0,2},{2,0},{4,6},{6,4},{8,10},{10,8},{12,14},{14,12},{16,18},{18,... | collective-permute-start | bytes 1179656 | tf_op jit(solution)/shard_map/ppermute | solution.py:731
  769.9 47.6 %collective-permute-start.71 = (bf16[1,2,192,1024]{3,2,1,0:T(8,128)(2,1)}, bf16[1,2,192,1024]{3,2,1,0:T(8,128)(2,1)}, u32[]{:S(2)}, u32[]{:S(2)}) collective-permute-start(bf16[1,2,192,1024]{3,2,1,0:T(8,128)(2,1)} %fusion.39), channel_id=1, source_target_pairs={{0,16},{2,18},{4,20},{6,22},{8,24},{10,26},{12,28},{14,30},{16,0},... | collective-permute-start | bytes 2359304 | tf_op jit(solution)/shard_map/ppermute | solution.py:731
  (129 other events, 1677.4 us)
Sparse Core Ops, SparseCore 0:
  113.2 21.6 all-gather.3
  136.4 64.7 all-gather.5
  209.7 37.3 all-gather.7

commit v2 on v1

--- a/solution.py
+++ b/solution.py
@@ -685,39 +685,118 @@
     )(dqkv, tokens_all, full_qkv, gains, mods)
 
 
-def product_kernel(where_ref, d_ref, a_ref, *refs):
+def product_kernel(widths, has_received, where_ref, d_ref, a_ref, *refs):
     p = dot(d_ref[0], a_ref[...], TN)
-    if len(refs) == 2:
+    outs = refs[1:] if has_received else refs
+    if has_received:
         p = p + refs[0][0].astype(jnp.float32)
-    refs[-1][0] = p.astype(jnp.bfloat16)
-
-
-def product(dact, act, starts, lanes, received=None):
+    p = p.astype(jnp.bfloat16)
+    start = 0
+    for out, width in zip(outs, widths):
+        out[0] = p[:, start : start + width]
+        start += width
+
+
+def product(dact, act, starts, lanes, received=None, widths=None):
     parts, tokens, columns = dact.shape
     count = len(starts)
-    width = lanes if lanes <= 512 else 512
-    per = lanes // width
-    tile = next(t for t in (2048, 1536, 1024, 512, 256, 128) if columns % t == 0)
+    widths = list(widths or [lanes])
+    tile = next(
+        t for t in (2048, 1536, 1024, 512, 256, 128) if columns % t == 0 and t * lanes <= 2048 * 512
+    )
     each = columns // tile
-    out_spec = pl.BlockSpec((1, tile, width), lambda n, k, s: (k // per, n, k % per))
+    spec = lambda w: pl.BlockSpec((1, tile, w), lambda n, k, s: (k, n, 0))
     return pl.pallas_call(
-        product_kernel,
+        functools.partial(product_kernel, widths, received is not None),
         grid_spec=pltpu.PrefetchScalarGridSpec(
             num_scalar_prefetch=1,
-            grid=(parts * each, count * per),
+            grid=(parts * each, count),
             in_specs=[
                 pl.BlockSpec((1, tokens, tile), lambda n, k, s: (n // each, 0, n % each)),
-                pl.BlockSpec((tokens, width), lambda n, k, s: (0, s[k // per] * per + k % per)),
+                pl.BlockSpec((tokens, lanes), lambda n, k, s: (0, s[k])),
             ]
-            + ([] if received is None else [out_spec]),
-            out_specs=out_spec,
+            + ([] if received is None else [spec(lanes)]),
+            out_specs=[spec(w) for w in widths],
         ),
-        out_shape=jax.ShapeDtypeStruct((count, parts * columns, lanes), jnp.bfloat16),
+        out_shape=[
+            jax.ShapeDtypeStruct((count, parts * columns, w), jnp.bfloat16) for w in widths
+        ],
         compiler_params=params(),
         cost_estimate=cost(
             2 * tokens * parts * columns * lanes * count, 4 * parts * columns * lanes * count
         ),
     )(jnp.stack(starts).astype(jnp.int32), dact, act, *([] if received is None else [received]))
+
+
+def split_product_kernel(portions, count, where_ref, d_ref, *refs):
+    acts, received, outs = refs[:count], refs[count], refs[count + 1 :]
+    prods = [
+        (dot(d_ref[0], acts[f][...], TN) + received[f].astype(jnp.float32)).astype(jnp.bfloat16)
+        for f in range(count)
+    ]
+    half = prods[0].shape[0] // 2
+    start = 0
+    for i, (width, letter) in enumerate(portions):
+        keep, send = outs[2 * i], outs[2 * i + 1]
+        lanes = slice(start, start + width)
+        start += width
+        if letter == "y":
+            keep[...] = prods[0][:, lanes]
+            send[...] = prods[1][:, lanes]
+        elif letter == "x":
+            low = where_ref[count] == 0
+            for f in range(count):
+                a, b = prods[f][:half, lanes], prods[f][half:, lanes]
+                keep[f] = jnp.where(low, a, b)
+                send[f] = jnp.where(low, b, a)
+        else:
+            mine = pl.program_id(0) % 2 == where_ref[count + 1]
+
+            @pl.when(mine)
+            def to_keep(keep=keep, lanes=lanes):
+                for f in range(count):
+                    keep[f] = prods[f][:, lanes]
+
+            @pl.when(jnp.logical_not(mine))
+            def to_send(send=send, lanes=lanes):
+                for f in range(count):
+                    send[f] = prods[f][:, lanes]
+
+
+def split_product(dact, act, starts, lanes, received, portions, bits, nd):
+    parts, tokens, columns = dact.shape
+    count = len(starts)
+    total = parts * columns
+    tile = 4 * (total // nd)
+    each = columns // tile
+    specs, shapes = [], []
+    for width, letter in portions:
+        if letter == "y":
+            spec, shape = pl.BlockSpec((tile, width), lambda n, s: (n, 0)), (total, width)
+        elif letter == "x":
+            spec = pl.BlockSpec((count, tile // 2, width), lambda n, s: (0, n, 0))
+            shape = (count, total // 2, width)
+        else:
+            spec = pl.BlockSpec((count, tile, width), lambda n, s: (0, n // 2, 0))
+            shape = (count, total // 2, width)
+        specs += [spec] * 2
+        shapes += [jax.ShapeDtypeStruct(shape, jnp.bfloat16)] * 2
+    act_spec = lambda f: pl.BlockSpec((tokens, lanes), lambda n, s: (0, s[f]))
+    outs = pl.pallas_call(
+        functools.partial(split_product_kernel, portions, count),
+        grid_spec=pltpu.PrefetchScalarGridSpec(
+            num_scalar_prefetch=1,
+            grid=(total // tile,),
+            in_specs=[pl.BlockSpec((1, tokens, tile), lambda n, s: (n // each, 0, n % each))]
+            + [act_spec(f) for f in range(count)]
+            + [pl.BlockSpec((count, tile, lanes), lambda n, s: (0, n, 0))],
+            out_specs=specs,
+        ),
+        out_shape=shapes,
+        compiler_params=params(),
+        cost_estimate=cost(2 * tokens * total * lanes * count, 4 * total * lanes * count),
+    )(jnp.stack(list(starts) + list(bits)).astype(jnp.int32), dact, *([act] * count), received)
+    return list(zip(outs[::2], outs[1::2]))
 
 
 ORDERS = ["yxz", "xzy", "zyx"]
@@ -818,48 +897,95 @@
     )
 
 
-def sum_wide(value, axes, env):
-    for axis in axes:
-        size = env[0] if axis == "dp" else env[1]
-        for b in range(bits_of(size)):
-            value = value + swap(value, axis, 1 << b, size)
-    return value
-
-
 def stages_of(order, env):
     kinds = {
-        "y": [("f", b) for b in range(bits_of(env[1]))],
-        "x": [("d", 1)],
-        "z": [("d", 2)] if bits_of(env[0]) > 2 else [],
+        "y": [("fsdp", b) for b in range(bits_of(env[1]))],
+        "x": [("dp", 1)],
+        "z": [("dp", 2)] if bits_of(env[0]) > 2 else [],
     }
     return [stage for letter in order for stage in kinds[letter]]
 
 
-def ladder_step(cur, alive, stage, env, anchor):
-    nd, nf, me, mine = env
-    kind, b = stage
-    if kind == "f":
-        pairs = cur.reshape((cur.shape[0] // 2, 2) + cur.shape[1:])
-        keep, got = pairs[:, 0], swap(pairs[:, 1], "fsdp", 1 << b, nf)
-    else:
-        axis = 1 + alive.index(b)
-        bit = (me >> b) & 1
-        keep = lax.dynamic_index_in_dim(cur, bit, axis, keepdims=False)
-        got = swap(lax.dynamic_index_in_dim(cur, bit ^ 1, axis, keepdims=False), "dp", 1 << b, nd)
-        alive = [d for d in alive if d != b]
-    return keep, got, alive
-
-
-def add_low(keep, got):
-    return (keep.astype(jnp.float32) + got.astype(jnp.float32)).astype(jnp.bfloat16)
-
-
-def finish_rows(done, env):
-    nd, nf, me, mine = env
-    core = me & 1
-    sent = lax.dynamic_index_in_dim(done, core ^ 1, 0, keepdims=False)
-    kept = lax.dynamic_index_in_dim(done, core, 0, keepdims=False)
-    got = swap(sent, "dp", 1, nd)
+def add_low(terms):
+    total = terms[0].astype(jnp.float32)
+    for term in terms[1:]:
+        total = total + term.astype(jnp.float32)
+    return total.astype(jnp.bfloat16)
+
+
+class Flow:
+    most = 5
+
+    def __init__(self, env):
+        self.env, self.pending, self.flying = env, [], []
+
+    def send(self, operand, axis, mask, land, rank):
+        self.pending.append((operand, axis, mask, land, rank))
+
+    def turn(self, outs, ins):
+        nd, nf = self.env[:2]
+        flying, self.flying = self.flying, []
+        if flying:
+            tied = lax.optimization_barrier(tuple(got for got, _ in flying) + tuple(outs))
+            for got, (_, land) in zip(tied, flying):
+                land(got)
+        pending = sorted(self.pending, key=lambda p: p[4])
+        pending, self.pending = pending[: self.most], pending[self.most :]
+        sends = tuple(p[0] for p in pending)
+        tied = lax.optimization_barrier(sends + tuple(ins) + tuple(outs))
+        for operand, (_, axis, mask, land, _) in zip(tied, pending):
+            size = nd if axis == "dp" else nf
+            self.flying.append((swap(operand, axis, mask, size), land))
+        return tied[len(sends) : len(sends) + len(ins)]
+
+    def drain(self, outs):
+        while self.flying or self.pending:
+            self.turn(outs, ())
+            outs = ()
+
+
+class Ladder:
+    def __init__(self, current, alive, stages, env):
+        self.current, self.alive, self.stages, self.env = current, alive, stages, env
+        self.sent = None
+
+    def split(self, axis, b):
+        t = self.current
+        if axis == "fsdp":
+            pairs = t.reshape((t.shape[0] // 2, 2) + t.shape[1:])
+            return pairs[:, 0], pairs[:, 1]
+        place = 1 + self.alive.index(b)
+        bit = (self.env[2] >> b) & 1
+        self.alive = [d for d in self.alive if d != b]
+        before, after_dims = t.shape[:place], t.shape[place + 1 :]
+        rows = 1
+        for n in after_dims[:-1]:
+            rows *= n
+        count = 1
+        for n in before:
+            count *= n
+        flat = t.reshape(count, 2, rows, t.shape[-1])
+        pick = lambda i: lax.dynamic_index_in_dim(flat, i, 1, keepdims=False).reshape(
+            before + after_dims
+        )
+        return pick(bit), pick(bit ^ 1)
+
+    def launch(self, flow, landed, rank):
+        axis, b = self.stages.pop(0)
+        if self.sent is None:
+            kept, send = self.split(axis, b)
+        else:
+            kept, send, self.sent = self.current, self.sent, None
+
+        def land(got):
+            self.current = add_low([kept, got.reshape(kept.shape)])
+            landed()
+
+        flow.send(send, axis, 1 << b, land, rank)
+
+
+def join_rows(kept, got, env):
+    core = env[2] & 1
     both = jnp.where(
         core == 0,
         jnp.concatenate([kept, got], axis=1),
@@ -868,88 +994,123 @@
     return both.T.astype(jnp.float32)
 
 
-def core_product(dact, act, core, env, rows_only, received=None):
+def core_product(dact, act, core, env, rows_only, received=None, widths=None):
     nd, nf, me, mine = env
     count = 1 if rows_only else nf
     lanes = act.shape[1] // (2 * count)
     blocks = [core] if rows_only else [2 * (mine ^ r) + core for r in range(nf)]
     if lanes % 128 == 0:
-        return product(dact, act, blocks, lanes, received)
+        outs = product(dact, act, blocks, lanes, received, widths)
+        return outs if widths else outs[0]
     wide = jnp.concatenate(list(dact), axis=1)
     parts = [lax.dynamic_slice_in_dim(act, b * lanes, lanes, 1) for b in blocks]
     out = jnp.stack([dot(wide, p, TN) for p in parts])
     if received is not None:
         out = out + received.astype(jnp.float32)
-    return out.astype(jnp.bfloat16)
+    out = out.astype(jnp.bfloat16)
+    if widths is None:
+        return out
+    cuts = [sum(widths[:i]) for i in range(len(widths))]
+    return [out[:, :, a : a + w] for a, w in zip(cuts, widths)]
 
 
 class Reduction:
-    def __init__(self, dact, act, portions, env, rows_only=False):
-        self.env, self.dact, self.act = env, dact, act
+    def __init__(self, dact, act, portions, flow, rank, rows_only=False):
+        self.flow, self.env, self.act, self.rank = flow, flow.env, act, rank
         self.portions, self.rows_only = portions, rows_only
-        nd, core = env[0], env[2] & 1
-        self.partial = core_product(dact, act, core ^ 1, env, rows_only)
-        self.sent = swap(self.partial, "dp", 1, nd)
-        self.tie = [self.partial]
-        self.flight = None
-        self.done = False
+        core = self.env[2] & 1
+        self.partial = core_product(dact, act, core ^ 1, self.env, rows_only)
+        flow.send(self.partial, "dp", 1, self.receive, 0)
+
+    def receive(self, got):
+        self.sent = got
+
+    def keep(self, dact):
+        nd, nf, me, mine = self.env
+        core, bits = me & 1, bits_of(nd)
+        alive = list(range(bits - 1, 0, -1))
+        tail = (2, self.sent.shape[1] // nd)
+        self.ladders = []
+        if special(self.env):
+            count = 1 if self.rows_only else nf
+            blocks = [core] if self.rows_only else [2 * (mine ^ r) + core for r in range(nf)]
+            pairs = split_product(
+                dact, self.act, blocks, self.act.shape[1] // (2 * count), self.sent,
+                [(w, order[0]) for w, order in self.portions], [(me >> 1) & 1, (me >> 2) & 1], nd,
+            )
+            for (kept, sent), (_, order) in zip(pairs, self.portions):
+                stages = stages_of(order, self.env)
+                axis, b = stages[0]
+                left = [d for d in alive if axis != "dp" or d != b]
+                lead = 1 if axis == "fsdp" else count
+                shape = (lead,) + (2,) * len(left) + tail + (kept.shape[-1],)
+                ladder = Ladder(kept.reshape(shape), left, stages, self.env)
+                ladder.sent = sent
+                self.ladders.append(ladder)
+            first = pairs[0][0]
+        else:
+            widths = [w for w, _ in self.portions]
+            totals = core_product(dact, self.act, core, self.env, self.rows_only, self.sent, widths)
+            for total, (_, order) in zip(totals, self.portions):
+                shape = (total.shape[0],) + (2,) * (bits - 1) + tail + (total.shape[2],)
+                stages = stages_of(order, self.env)
+                self.ladders.append(Ladder(total.reshape(shape), alive, stages, self.env))
+            first = totals[0]
+        self.launch()
+        return first
 
     def launch(self):
-        if not any(stages for _, _, stages in self.ladders):
-            if len(self.ladders) > 1:
-                alive = self.ladders[0][1]
-                self.ladders = [
-                    (jnp.concatenate([cur for cur, _, _ in self.ladders], axis=-1), alive, [])
-                ]
-            cur, alive, _ = self.ladders[0]
-            if not alive:
-                self.done = True
-                return
-            self.ladders = [(cur, alive, [("d", alive[-1])])]
-        self.flight = [
-            ladder_step(cur, alive, stages[0], self.env, None) + (stages[1:],)
-            for cur, alive, stages in self.ladders
+        ladders = self.ladders
+        if ladders[0].stages:
+            self.waiting = len(ladders)
+            for ladder in ladders:
+                ladder.launch(self.flow, self.landed, self.rank)
+            return
+        if len(ladders) > 1:
+            joined = jnp.concatenate([r.current for r in ladders], axis=-1)
+            self.ladders = ladders = [Ladder(joined, ladders[0].alive, [], self.env)]
+        if ladders[0].alive:
+            ladders[0].stages = [("dp", ladders[0].alive[-1])]
+            self.launch()
+            return
+        core = self.env[2] & 1
+        rows = ladders[0].current[0]
+        kept = lax.dynamic_index_in_dim(rows, core, 0, keepdims=False)
+
+        def land(got):
+            self.result = join_rows(kept, got, self.env)
+
+        sent = lax.dynamic_index_in_dim(rows, core ^ 1, 0, keepdims=False)
+        self.flow.send(sent, "dp", 1, land, 3)
+
+    def landed(self):
+        self.waiting -= 1
+        if not self.waiting:
+            self.launch()
+
+
+class WideSum:
+    def __init__(self, value, axes, flow, rank):
+        env = flow.env
+        self.rank = rank
+        self.value, self.flow = value, flow
+        self.hops = [
+            (axis, 1 << b)
+            for axis in axes
+            for b in range(bits_of(env[0] if axis == "dp" else env[1]))
         ]
-
-    def step(self, anchor):
-        if self.done:
-            return
-        nd, bits = self.env[0], bits_of(self.env[0])
-        if self.flight is None:
-            core = self.env[2] & 1
-            sent = after(self.sent, anchor)
-            total = core_product(self.dact, self.act, core, self.env, self.rows_only, sent)
-            total = total.reshape(
-                (total.shape[0],) + (2,) * bits + (total.shape[1] // nd, total.shape[2])
-            )
-            alive = list(range(bits - 1, 0, -1))
-            self.ladders, start = [], 0
-            for width, order in self.portions:
-                stages = stages_of(order, self.env)
-                self.ladders.append((total[..., start : start + width], alive, stages))
-                start += width
-            self.tie = [total]
-        else:
-            self.ladders = []
-            for keep, got, alive, stages in self.flight:
-                self.ladders.append((add_low(keep, after(got, anchor)), alive, stages))
-            self.tie = [cur for cur, _, _ in self.ladders]
         self.launch()
 
-    def finish(self, anchor):
-        while not self.done:
-            self.step(anchor)
-            anchor = self.tie[0]
-        return finish_rows(self.ladders[0][0][0], self.env)
-
-
-def then(value, anchor, *reductions):
-    ties = [anchor]
-    for r in reductions:
-        if not r.done:
-            r.step(anchor)
-            ties += r.tie
-    return after(value, *ties)
+    def launch(self):
+        if self.hops:
+            axis, mask = self.hops.pop(0)
+            self.flow.send(self.value, axis, mask, self.land, self.rank)
+
+    def land(self, got):
+        self.value = self.value.astype(jnp.float32) + got.astype(jnp.float32)
+        if got.dtype == jnp.bfloat16:
+            self.value = self.value.astype(jnp.bfloat16)
+        self.launch()
 
 
 def portion_list(lanes, names):
@@ -1023,16 +1184,19 @@
         which, ffn_inner, full_down, middle, cotangent[0], gains, mods
     )
     lanes_d, lanes_f = D // (2 * nf), FF // (2 * nf)
-    red_down = Reduction(grad_down[None], ffn_inner, portion_list(lanes_f, ORDERS), env)
-    grad_down = after(grad_down, red_down.partial)
-    grad_gate_up = gate_up_back(which, grad_down, gate_part, up_part, full_down)
-    dgu = then(grad_gate_up, grad_gate_up, red_down)
-    red_gate_up = Reduction(dgu, ffn_in, portion_list(lanes_d, ORDERS), env)
-    dgu = after(dgu, red_gate_up.partial)
+    flow = Flow(env)
+    red_down = Reduction(grad_down[None], ffn_inner, portion_list(lanes_f, ORDERS), flow, 1)
+    (grad_down_b,) = flow.turn((red_down.partial,), (grad_down,))
+    dgu = gate_up_back(which, grad_down_b, gate_part, up_part, full_down)
+    (grad_down_b,) = flow.turn((dgu,), (grad_down_b,))
+    done = red_down.keep(grad_down_b[None])
+    (dgu,) = flow.turn((done,), (dgu,))
+    red_gate_up = Reduction(dgu, ffn_in, portion_list(lanes_d, ORDERS), flow, 1)
+    (dgu_b,) = flow.turn((red_gate_up.partial,), (dgu,))
     grad_mid, grad_proj, grad_comb, ffn_sums = ffn_back(
-        which, dgu, full_gate_up, full_out, middle, cotangent[0], projected, gains, mods
-    )
-    grad_comb = then(grad_comb, ffn_sums, red_down)
+        which, dgu_b, full_gate_up, full_out, middle, cotangent[0], projected, gains, mods
+    )
+    grad_comb, grad_proj = flow.turn((ffn_sums,), (grad_comb, grad_proj))
     dq_cross, grad_ckey, grad_cvalue, gate_sums = cross_back(
         query_b, ckey_b, cvalue_b, bias[:, None], gate_tanh, stats, grad_comb, cross_out
     )
@@ -1041,13 +1205,10 @@
         grad_ckey.astype(jnp.float32), ckey_pre, ckey_scale, cap_gain
     )
     grad_cap_kv = jnp.concatenate([grad_ckey_pre, grad_cvalue.astype(jnp.float32)], axis=-1)
-    grad_cap_kv = grad_cap_kv.astype(jnp.bfloat16)
-    tied = then(gate_sums, grad_cap_kv, red_down)
-    grad_comb = then(grad_comb, tied, red_gate_up)
-    red_out = Reduction(
-        after(grad_proj, grad_comb)[None], combined, portion_list(lanes_d, ORDERS[2:]), env
-    )
-    grad_comb = then(grad_comb, red_out.partial, red_down)
+    cap_sum = WideSum(grad_cap_kv.astype(jnp.bfloat16), ("fsdp",), flow, 0)
+    red_out = Reduction(grad_proj[None], combined, portion_list(lanes_d, ORDERS[2:]), flow, 1.5)
+    dgu_b, grad_comb = flow.turn((gate_sums, red_out.partial), (dgu_b, grad_comb))
+    done = red_gate_up.keep(dgu_b)
     pairs = D // PAIR
     each = pairs // 4
     parts = []
@@ -1058,38 +1219,35 @@
         )
         return parts[-1][0]
 
-    done = attention_part(grad_comb)
-    grad_comb = then(grad_comb, done, red_down, red_out)
-    done = attention_part(grad_comb)
-    grad_cap_kv = sum_fsdp(grad_cap_kv.astype(jnp.float32), env, done).astype(jnp.bfloat16)
+    first = attention_part(grad_comb)
+    while nf > 2 and cap_sum.hops:
+        flow.turn((done,), ())
+    grad_comb, grad_proj = flow.turn((done, first), (grad_comb, grad_proj))
+    grad_cap_kv = cap_sum.value
     red_caption = Reduction(
-        grad_cap_kv[None], caption[0], portion_list(caption.shape[2] // 2, ["xz", "zx"]), env, True
-    )
-    grad_comb = after(grad_comb, red_caption.partial)
-    done = attention_part(grad_comb)
-    grad_comb = then(grad_comb, done, red_gate_up, red_out)
-    done = then(grad_comb, done, red_caption)
-    done = attention_part(done)
+        grad_cap_kv[None], caption[0], portion_list(caption.shape[2] // 2, ["xz", "zx"]), flow, 1.2, True
+    )
+    out_done = red_out.keep(grad_proj[None])
+    dones = [attention_part(grad_comb) for _ in range(3)]
     grad_query, grad_key, grad_value = zip(*parts)
-    grad_query = (then(grad_query[0], done, red_out),) + grad_query[1:]
+    (dq0,) = flow.turn([red_caption.partial, out_done] + dones, (grad_query[0],))
+    grad_query = (dq0,) + grad_query[1:]
     grad_mixed, qk_sums = qk_back(
         grad_query, grad_key, grad_value, query_pre, key_pre, cosine, sine, gains
     )
-    grad_mixed = then(grad_mixed, qk_sums, red_gate_up)
-    red_qkv = Reduction(grad_mixed[None], hm, portion_list(lanes_d, ORDERS), env)
-    grad_mixed = then(grad_mixed, red_qkv.partial, red_gate_up, red_out)
+    red_qkv = Reduction(grad_mixed[None], hm, portion_list(lanes_d, ORDERS), flow, 0.5)
+    grad_mixed, grad_cap_kv = flow.turn((red_qkv.partial,), (grad_mixed, grad_cap_kv))
+    done = red_caption.keep(grad_cap_kv[None])
     dx_other, other_sums = project_back(
         grad_mixed, own_rows, own_rows, tokens_all, full_qkv, gains, mods
     )
-    grad_mixed = then(grad_mixed, other_sums, red_caption, red_qkv)
+    dx_got = []
+    if nf == 2:
+        flow.send(dx_other, "fsdp", 1, dx_got.append, 0)
+    (grad_mixed,) = flow.turn((done, other_sums), (grad_mixed,))
+    done = red_qkv.keep(grad_mixed[None])
     dx_own, own_sums = project_back(grad_mixed, 0, own_rows, tokens_all, full_qkv, gains, mods)
-    grad_cap_kv = then(grad_cap_kv, own_sums, red_caption, red_gate_up, red_out)
-    grad_caption = dot(grad_cap_kv, w_caption_kv, NT).astype(jnp.bfloat16)
-    anchor = grad_caption
-    red_qkv.step(anchor)
     project_sums = own_sums + other_sums if nf > 1 else own_sums
-    grad_inputs = jnp.concatenate([dx_own, dx_other]) if nf > 1 else dx_own
-    grad_tokens = (grad_mid + reduce_relative(grad_inputs, env)).astype(jnp.bfloat16)
     small = jnp.concatenate(
         [
             project_sums[:1],
@@ -1105,7 +1263,7 @@
             ),
         ]
     )
-    small = sum_wide(small, ("fsdp", "dp"), env)
+    small_sum = WideSum(small, ("fsdp", "dp"), flow, 2)
     mod_grads = jnp.stack(
         [
             project_sums[3],
@@ -1116,11 +1274,19 @@
             down_sums[0] * (1.0 - jnp.tanh(mods[5]) ** 2),
         ]
     )
-    mod_grads = sum_wide(mod_grads, ("fsdp",), env)
-    outs = []
-    for r in (red_down, red_gate_up, red_out, red_caption, red_qkv):
-        outs.append(r.finish(anchor))
-    out_down, out_gate_up, out_out, out_caption, out_qkv = outs
+    mod_sum = WideSum(mod_grads, ("fsdp",), flow, 4)
+    (grad_cap_kv,) = flow.turn((done, own_sums), (grad_cap_kv,))
+    if nf == 2:
+        dx = dx_own.astype(jnp.float32) + dx_got[0].astype(jnp.float32)
+    else:
+        dx = reduce_relative(jnp.concatenate([dx_own, dx_other]) if nf > 1 else dx_own, env)
+    grad_tokens = (grad_mid + dx).astype(jnp.bfloat16)
+    grad_caption = dot(grad_cap_kv, w_caption_kv, NT).astype(jnp.bfloat16)
+    flow.drain((grad_caption, grad_tokens))
+    small, mod_grads = small_sum.value, mod_sum.value
+    out_down, out_gate_up, out_out, out_caption, out_qkv = (
+        r.result for r in (red_down, red_gate_up, red_out, red_caption, red_qkv)
+    )
     width = D // nf
     return (
         block_out[None],

time: 900 us -> 827 us (0.919)
  waiting for transfers between devices: 247 us -> 205 us
  local copies, waits for them, and re-layouts: 80.2 us -> 51.9 us
    ppermute x80, waiting for transfers between devices: 239 us -> 196 us  [swap(): return lax.ppermute(value, axis, [(i, i ^ mask) for i in range(size)])]
    slice x4 -> x0, local copies, waits for them, and re-layouts: 15.7 us -> none  [step(): self.ladders.append((total[..., start:start + width], alive, stages))]
    squeeze x38 -> x12, local copies, waits for them, and re-layouts: 20.2 us -> 5.43 us  [the longest x7 3 us: split(): return (pairs[:, 0], pairs[:, 1])]
    unnamed x146 -> x131, local copies, waits for them, and re-layouts: 21.4 us -> 17.9 us
  transfers between devices with their start and end apart: 83 -> 83, of which waited for: 35 -> 27; matrix products, arithmetic and copies ran while one was open for 16% -> 8% of each run, Pallas kernels for 33% -> 41%
where the time goes in v2:
time: 827 us; the launch traced here: 821 us
  Pallas kernels  393 us (48%)
  waiting for transfers between devices  205 us (25%)
  starting transfers between devices  77.3 us (9%)
  other arithmetic  63.6 us (8%)
  local copies, waits for them, and re-layouts  51.9 us (6%)
  between operations  15.4 us (2%)
  matrix products  14.1 us (2%)
    ppermute x80, waiting for transfers between devices, swap(): return lax.ppermute(value, axis, [(i, i ^ mask) for i in range(size)])  196 us
    ppermute x80, starting transfers between devices, swap(): return lax.ppermute(value, axis, [(i, i ^ mask) for i in range(size)])  76.7 us
    pallas_call x5, Pallas kernels, split_product(): pl.pallas_call(functools.partial(split_product_kernel, portions, count),...  59 us
    pallas_call x5, Pallas kernels, product(): pl.pallas_call(functools.partial(product_kernel, widths, received is not...  54.4 us
    pallas_call x4, Pallas kernels, self_back(): pl.pallas_call(self_back_kernel, grid=(count,), in_specs=[spec(rows), spe...  45.4 us
    pallas_call x1, Pallas kernels, attend(): pl.pallas_call(attend_kernel, grid=(pairs,), in_specs=[spec(rows), spec(k...  42.1 us
    pallas_call x1, Pallas kernels, ffn_back(): pl.pallas_call(ffn_back_kernel, grid_spec=pltpu.PrefetchScalarGridSpec(nu...  35.3 us
    pallas_call x1, Pallas kernels, project(): pl.pallas_call(functools.partial(project_kernel, len(pieces), own_rows),...  35 us
  transfers between devices with their start and end apart: 83, of which 27 were waited for; matrix products, arithmetic and copies ran while one was open for 8% of the time, Pallas kernels for 41%

profile of v2, /device:TPU:0, one launch (start us, length us, event | category | flops | bytes accessed | tf_op | source)
XLA Modules:
  0.0 821.0 jit_solution(9430522200640901433)
XLA Ops:
  77.5 29.1 %collective-permute-done.20 = bf16[96,8192]{1,0:T(8,128)(2,1)} collective-permute-done((bf16[96,8192]{1,0:T(8,128)(2,1)}, bf16[96,8192]{1,0:T(8,128)(2,1)}, u32[]{:S(2)}, u32[]{:S(2)}) %collective-permute-start.20) | collective-permute-done | bytes 1572896 | tf_op jit(solution)/shard_map/ppermute | solution.py:810
  126.3 35.0 %shard_map.229 = (bf16[1024,1536]{1,0:T(8,128)(2,1)}, bf16[1536,4608]{1,0:T(8,128)(2,1)}, bf16[512,1536]{1,0:T(8,128)(2,1)}, bf16[1024,1536]{1,0:T(8,128)(2,1)},...) custom-call(s32[17]{0:T(128)} %stack.142.where_ref, ...), custom_call_target="tpu_custom_call" | custom-call | flops 603979776 | bytes 3000000 | tf_op jit(solution)/shard_map/pallas_call | solution.py:330
  166.0 42.1 %shard_map.230 = (bf16[512,1536]{1,0:T(8,128)(2,1)S(1)}, bf16[512,1536]{1,0:T(8,128)(2,1)S(1)}, bf16[512,1536]{1,0:T(8,128)(2,1)}, f32[12,8,512]{2,1,0:T(8,128)S(1)}) custom-call(bf16[512,1536]{1,0:T(8,128)(2,1)} %get-tuple-element.219.q_ref, bf16[1024,1536]{1,0:T(8,128)(2,1)} %get-tuple-element.220.k_ref, bf16[1024,1536]{1,0:T(8,128)(2,1)} %get-tuple-element.221.v_ref, ...), custom_call_target="tpu_custom_call" | custom-call | flops 805306368 | bytes 1000000 | tf_op jit(solution)/shard_map/pallas_call | solution.py:86
  220.7 20.5 %shard_map.232 = (bf16[512,4096]{1,0:T(8,128)(2,1)}, bf16[512,4096]{1,0:T(8,128)(2,1)}, bf16[512,4096]{1,0:T(8,128)(2,1)}) custom-call(s32[1]{0:T(128)} %bitcast.which_ref, bf16[512,1536]{1,0:T(8,128)(2,1)} %get-tuple-element.230.h_ref.a_ref.refs_0_.refs_1_, bf16[768,8192]{1,0:T(8,128)(2,1)} %u0_ref.3, ...), custom_call_target="tpu_custom_call" | custom-call | flops 644245120 | bytes 2000000 | tf_op jit(solution)/shard_map/pallas_call | solution.py:398
  249.7 18.2 %shard_map.233 = (bf16[512,1536]{1,0:T(8,128)(2,1)}, bf16[512,1536]{1,0:T(8,128)(2,1)}, f32[8,1536]{1,0:T(8,128)}) custom-call(s32[1]{0:T(128)} %bitcast.which_ref, bf16[512,4096]{1,0:T(8,128)(2,1)} %get-tuple-element.231.ff_ref.a_ref.refs_0_.refs_1_, bf16[2048,1536]{1,0:T(8,128)(2,1)} %d0_ref.1, ...), custom_call_target="tpu_custom_call" | custom-call | flops 322122560 | bytes 1200000 | tf_op jit(solution)/shard_map/pallas_call | solution.py:449
  278.8 17.4 %shard_map.235.d_ref.dgu_ref = bf16[2,512,4096]{2,1,0:T(8,128)(2,1)} custom-call(s32[1]{0:T(128)} %bitcast.which_ref, bf16[512,1536]{1,0:T(8,128)(2,1)} %get-tuple-element.241.df_ref, bf16[512,4096]{1,0:T(8,128)(2,1)} %get-tuple-element.239.ga_ref, bf16[512,4096]{1,0:T(8,128)(2,1)} %get-tuple-element.240.up_ref, bf16[2048,1536]{1,0:T(8,128)(2,1)} %d0_ref.1, ...), custom_call_target="tpu_custom_call" | custom-call | flops 322122560 | bytes 1500000 | tf_op jit(solution)/shard_map/pallas_call | solution.py:494
  296.2 10.0 %shard_map.236 = (bf16[1536,256]{1,0:T(8,128)(2,1)}, bf16[1536,256]{1,0:T(8,128)(2,1)}, bf16[2,768,384]{2,1,0:T(8,128)(2,1)}, bf16[2,768,384]{2,1,0:T(8,128)(2,1...) custom-call(s32[4]{0:T(128)} %pad_add_fusion.2.where_ref, bf16[1,512,1536]{2,1,0:T(8,128)(2,1)} %bitcast.240, ...), custom_call_target="tpu_custom_call" | custom-call | flops 161061280 | bytes 629145 | tf_op jit(solution)/shard_map/pallas_call | solution.py:785
  309.7 16.7 %shard_map.237 = bf16[2,8192,384]{2,1,0:T(8,128)(2,1)} custom-call(s32[2]{0:T(128)} %pad_add_fusion.1.where_ref, bf16[2,512,4096]{2,1,0:T(8,128)(2,1)} %shard_map.235.d_ref.dgu_ref, bf16[512,1536]{1,0:T(8,128)(2,1)} %get-tuple-element.230.h_ref.a_ref.refs_0_.refs_1_), custom_call_target="tpu_custom_call" | custom-call | flops 322122560 | bytes 1258291 | tf_op jit(solution)/shard_map/pallas_call | solution.py:709
  344.5 35.3 %shard_map.238 = (f32[512,1536]{1,0:T(8,128)}, bf16[512,1536]{1,0:T(8,128)(2,1)}, bf16[512,1536]{1,0:T(8,128)(2,1)}, f32[8,1536]{1,0:T(8,128)}) custom-call(s32[1]{0:T(128)} %bitcast.which_ref, bf16[2,512,4096]{2,1,0:T(8,128)(2,1)} %shard_map.235.d_ref.dgu_ref, bf16[768,8192]{1,0:T(8,128)(2,1)} %u0_ref.3, ...), custom_call_target="tpu_custom_call" | custom-call | flops 765041024 | bytes 2750000 | tf_op jit(solution)/shard_map/pallas_call | solution.py:573
  384.3 13.7 %shard_map.239 = (bf16[512,1536]{1,0:T(8,128)(2,1)S(1)}, bf16[256,1536]{1,0:T(8,128)(2,1)S(1)}, bf16[256,1536]{1,0:T(8,128)(2,1)S(1)}, f32[1,1536]{1,0:T(1,128)S(1)}) custom-call(bf16[512,1536]{1,0:T(8,128)(2,1)} %get-tuple-element.219.q_ref, bf16[256,1536]{1,0:T(8,128)(2,1)S(1)} %multiply_convert_fusion.ck_ref, bf16[256,1536]{1,0:T(8,128)(2,1)S(1)} %slice.238.cv_ref, ...), custom_call_target="tpu_custom_call" | custom-call | flops 402653184 | bytes 450000 | tf_op jit(solution)/shard_map/pallas_call | solution.py:170
  419.4 17.3 %shard_map.241 = (bf16[8192,128]{1,0:T(8,128)(2,1)}, bf16[8192,128]{1,0:T(8,128)(2,1)}, bf16[2,4096,128]{2,1,0:T(8,128)(2,1)}, bf16[2,4096,128]{2,1,0:T(8,128)(2...) custom-call(s32[4]{0:T(128)} %pad_add_fusion.2.where_ref, ...), custom_call_target="tpu_custom_call" | custom-call | flops 322122560 | bytes 1258291 | tf_op jit(solution)/shard_map/pallas_call | solution.py:785
  436.7 11.5 %shard_map.242 = (bf16[512,384]{1,0:T(8,128)(2,1)S(1)}, bf16[1024,384]{1,0:T(8,128)(2,1)S(1)}, bf16[1024,384]{1,0:T(8,128)(2,1)S(1)}) custom-call(bf16[512,1536]{1,0:T(8,128)(2,1)S(1)} %copy-done, bf16[1024,1536]{1,0:T(8,128)(2,1)} %get-tuple-element.220.k_ref, bf16[1024,1536]{1,0:T(8,128)(2,1)} %get-tuple-element.221.v_ref, ...), custom_call_target="tpu_custom_call" | custom-call | flops 805306368 | bytes 150000 | tf_op jit(solution)/shard_map/pallas_call | solution.py:191
  473.4 11.1 %shard_map.245 = (bf16[512,384]{1,0:T(8,128)(2,1)S(1)}, bf16[1024,384]{1,0:T(8,128)(2,1)S(1)}, bf16[1024,384]{1,0:T(8,128)(2,1)S(1)}) custom-call(bf16[512,1536]{1,0:T(8,128)(2,1)S(1)} %copy-done, bf16[1024,1536]{1,0:T(8,128)(2,1)} %get-tuple-element.220.k_ref, bf16[1024,1536]{1,0:T(8,128)(2,1)} %get-tuple-element.221.v_ref, ...), custom_call_target="tpu_custom_call" | custom-call | flops 805306368 | bytes 150000 | tf_op jit(solution)/shard_map/pallas_call | solution.py:191
  486.2 11.4 %shard_map.246 = (bf16[512,384]{1,0:T(8,128)(2,1)S(1)}, bf16[1024,384]{1,0:T(8,128)(2,1)S(1)}, bf16[1024,384]{1,0:T(8,128)(2,1)S(1)}) custom-call(bf16[512,1536]{1,0:T(8,128)(2,1)S(1)} %copy-done, bf16[1024,1536]{1,0:T(8,128)(2,1)} %get-tuple-element.220.k_ref, bf16[1024,1536]{1,0:T(8,128)(2,1)} %get-tuple-element.221.v_ref, ...), custom_call_target="tpu_custom_call" | custom-call | flops 805306368 | bytes 150000 | tf_op jit(solution)/shard_map/pallas_call | solution.py:191
  499.2 11.4 %shard_map.247 = (bf16[512,384]{1,0:T(8,128)(2,1)S(1)}, bf16[1024,384]{1,0:T(8,128)(2,1)S(1)}, bf16[1024,384]{1,0:T(8,128)(2,1)S(1)}) custom-call(bf16[512,1536]{1,0:T(8,128)(2,1)S(1)} %copy-done, bf16[1024,1536]{1,0:T(8,128)(2,1)} %get-tuple-element.220.k_ref, bf16[1024,1536]{1,0:T(8,128)(2,1)} %get-tuple-element.221.v_ref, ...), custom_call_target="tpu_custom_call" | custom-call | flops 805306368 | bytes 150000 | tf_op jit(solution)/shard_map/pallas_call | solution.py:191
  526.7 13.7 %shard_map.248 = (bf16[1024,4608]{1,0:T(8,128)(2,1)}, f32[8,1536]{1,0:T(8,128)}) custom-call(bf16[512,384]{1,0:T(8,128)(2,1)} %copy-done.13, bf16[512,384]{1,0:T(8,128)(2,1)} %copy-done.14, bf16[512,384]{1,0:T(8,128)(2,1)} %copy-done.15, bf16[512,384]{1,0:T(8,128)(2,1)} %copy-done.16, bf16[1024,384]{1,0:T(8,128)(2,1)} %copy-done.5, ...), custom_call_target="tpu_custom_call" | custom-call | flops 4718592 | bytes 1500000 | tf_op jit(solution)/shard_map/pallas_call | solution.py:636
  540.4 16.7 %shard_map.249 = bf16[2,4608,384]{2,1,0:T(8,128)(2,1)} custom-call(s32[2]{0:T(128)} %pad_add_fusion.1.where_ref, bf16[1,1024,4608]{2,1,0:T(8,128)(2,1)} %bitcast.237, bf16[1024,1536]{1,0:T(8,128)(2,1)} %get-tuple-element.223.a_ref.refs_0_.refs_1_), custom_call_target="tpu_custom_call" | custom-call | flops 362387872 | bytes 707788 | tf_op jit(solution)/shard_map/pallas_call | solution.py:709
  557.1 16.4 %collective-permute-done.43 = bf16[2,2,2,512,128]{4,3,2,1,0:T(8,128)(2,1)S(1)} collective-permute-done((bf16[2,2,2,512,128]{4,3,2,1,0:T(8,128)(2,1)}, bf16[2,2,2,512,128]{4,3,2,1,0:T(8,128)(2,1)S(1)}, u32[]{:S(2)}, u32[]{:S(2)}) %collective-permute-start.43) | collective-permute-done | bytes 1048608 | tf_op jit(solution)/shard_map/ppermute | solution.py:810
  592.7 13.9 %shard_map.250 = (bf16[512,1536]{1,0:T(8,128)(2,1)}, f32[8,1536]{1,0:T(8,128)}) custom-call(bf16[1024,4608]{1,0:T(8,128)(2,1)} %get-tuple-element.353.dqkv_ref, bf16[1024,1536]{1,0:T(8,128)(2,1)} %pad_maximum_fusion.tok_ref, bf16[1536,4608]{1,0:T(8,128)(2,1)} %get-tuple-element.336.w_ref, f32[6,1536]{1,0:T(8,128)} %get-tuple-element.493.gain_ref.refs_16_, ...), custom_call_target="tpu_custom_call" | custom-call | flops 362387872 | bytes 1500000 | tf_op jit(solution)/shard_map/pallas_call | solution.py:672
  618.7 16.0 %shard_map.252 = (bf16[512,1536]{1,0:T(8,128)(2,1)}, f32[8,1536]{1,0:T(8,128)}) custom-call(bf16[1024,4608]{1,0:T(8,128)(2,1)} %get-tuple-element.353.dqkv_ref, bf16[1024,1536]{1,0:T(8,128)(2,1)} %pad_maximum_fusion.tok_ref, bf16[1536,4608]{1,0:T(8,128)(2,1)} %get-tuple-element.336.w_ref, f32[6,1536]{1,0:T(8,128)} %get-tuple-element.493.gain_ref.refs_16_, ...), custom_call_target="tpu_custom_call" | custom-call | flops 362387872 | bytes 1500000 | tf_op jit(solution)/shard_map/pallas_call | solution.py:672
  634.7 16.2 %shard_map.253 = (bf16[4608,128]{1,0:T(8,128)(2,1)}, bf16[4608,128]{1,0:T(8,128)(2,1)}, bf16[2,2304,128]{2,1,0:T(8,128)(2,1)}, bf16[2,2304,128]{2,1,0:T(8,128)(2...) custom-call(s32[4]{0:T(128)} %pad_add_fusion.2.where_ref, bf16[1,1024,4608]{2,1,0:T(8,128)(2,1)} %bitcast.238, ...), custom_call_target="tpu_custom_call" | custom-call | flops 362387872 | bytes 707788 | tf_op jit(solution)/shard_map/pallas_call | solution.py:785
  687.5 26.6 %collective-permute-done.59 = bf16[1,2,2,192,512]{4,3,2,1,0:T(8,128)(2,1)S(1)} collective-permute-done((bf16[1,2,2,192,512]{4,3,2,1,0:T(8,128)(2,1)}, bf16[1,2,2,192,512]{4,3,2,1,0:T(8,128)(2,1)S(1)}, u32[]{:S(2)}, u32[]{:S(2)}) %collective-permute-start.59) | collective-permute-done | bytes 786464 | tf_op jit(solution)/shard_map/ppermute | solution.py:810
  736.4 27.0 %collective-permute-done.65 = bf16[1,2,96,384]{3,2,1,0:T(8,128)(2,1)S(1)} collective-permute-done((bf16[1,2,96,384]{3,2,1,0:T(8,128)(2,1)}, bf16[1,2,96,384]{3,2,1,0:T(8,128)(2,1)S(1)}, u32[]{:S(2)}, u32[]{:S(2)}) %collective-permute-start.65) | collective-permute-done | bytes 147488 | tf_op jit(solution)/shard_map/ppermute | solution.py:810
  783.8 13.0 %collective-permute-done.71 = bf16[1,2,288,384]{3,2,1,0:T(8,128)(2,1)} collective-permute-done((bf16[1,2,288,384]{3,2,1,0:T(8,128)(2,1)S(1)}, bf16[1,2,288,384]{3,2,1,0:T(8,128)(2,1)}, u32[]{:S(2)}, u32[]{:S(2)}) %collective-permute-start.71) | collective-permute-done | bytes 442400 | tf_op jit(solution)/shard_map/ppermute | solution.py:810
  (450 shorter events, 345.3 us)
Async XLA Ops:
  7.2 204.8 %all-gather.4.cloned.1.call-start = ((), (), s32[]{:S(2)}) async-start(), calls=%async_computation | async-start | bytes 2654208 | tf_op jit(solution)/shard_map/all_gather | solution.py:857
  37.6 69.0 %collective-permute-start.20 = (bf16[96,8192]{1,0:T(8,128)(2,1)}, bf16[96,8192]{1,0:T(8,128)(2,1)}, u32[]{:S(2)}, u32[]{:S(2)}) collective-permute-start(bf16[96,8192]{1,0:T(8,128)(2,1)} %constant_dynamic-slice_fusion.44), channel_id=1, source_target_pairs={{0,1},{1,0},{2,3},{3,2},{4,5},{5,4},{6,7},{7,6},{8,9},{9,8},{10,11... | collective-permute-start | bytes 4718600 | tf_op jit(solution)/shard_map/ppermute | solution.py:810
  115.3 105.4 %all-gather.6.cloned.1.call-start = ((), (), s32[]{:S(2)}) async-start(), calls=%async_computation.1 | async-start | bytes 14155776 | tf_op jit(solution)/shard_map/all_gather | solution.py:857
  116.0 133.7 %all-gather.8.cloned.1.call-start = ((), (), s32[]{:S(2)}) async-start(), calls=%async_computation.2 | async-start | bytes 7077888 | tf_op jit(solution)/shard_map/all_gather | solution.py:857
  118.7 42.7 %collective-permute-start.19 = (bf16[256,3072]{1,0:T(8,128)(2,1)}, bf16[256,3072]{1,0:T(8,128)(2,1)}, u32[]{:S(2)}, u32[]{:S(2)}) collective-permute-start(bf16[256,3072]{1,0:T(8,128)(2,1)} %convert_element_type.908), channel_id=1, source_target_pairs={{0,1},{1,0},{2,3},{3,2},{4,5},{5,4},{6,7},{7,6},{8,9},{9,8},{10,11... | collective-permute-start | bytes 4718600 | tf_op jit(solution)/shard_map/ppermute | solution.py:810
  165.0 45.4 %collective-permute-start.22 = (bf16[256,1536]{1,0:T(8,128)(2,1)S(1)}, bf16[256,1536]{1,0:T(8,128)(2,1)S(1)}, u32[]{:S(2)}, u32[]{:S(2)}) collective-permute-start(bf16[256,1536]{1,0:T(8,128)(2,1)S(1)} %copy-done.42), channel_id=1, source_target_pairs={{0,1},{1,0},{2,3},{3,2},{4,5},{5,4},{6,7},{7,6},{8,9},{9,8},{10,11... | collective-permute-start | bytes 2359304 | tf_op jit(solution)/shard_map/ppermute | solution.py:810
  341.2 38.6 %collective-permute-start.27 = (bf16[2,8192,384]{2,1,0:T(8,128)(2,1)}, bf16[2,8192,384]{2,1,0:T(8,128)(2,1)}, u32[]{:S(2)}, u32[]{:S(2)}) collective-permute-start(bf16[2,8192,384]{2,1,0:T(8,128)(2,1)} %shard_map.237), channel_id=1, source_target_pairs={{0,2},{2,0},{4,6},{6,4},{8,10},{10,8},{12,14},{14,12},{16,18},{18,... | collective-permute-start | bytes 37748744 | tf_op jit(solution)/shard_map/ppermute | solution.py:810
  341.2 38.6 %collective-permute-start.29 = (bf16[2,2,2,96,384]{4,3,2,1,0:T(8,128)(2,1)}, bf16[2,2,2,96,384]{4,3,2,1,0:T(8,128)(2,1)}, u32[]{:S(2)}, u32[]{:S(2)}) collective-permute-start(bf16[2,2,2,96,384]{4,3,2,1,0:T(8,128)(2,1)} %bitcast.39), channel_id=1, source_target_pairs={{0,8},{2,10},{4,12},{6,14},{8,0},{10,2},{12,4},{14,6},{16,24},{18,... | collective-permute-start | bytes 1769480 | tf_op jit(solution)/shard_map/ppermute | solution.py:810
  454.5 56.2 %collective-permute-start.37 = (bf16[8192,128]{1,0:T(8,128)(2,1)}, bf16[8192,128]{1,0:T(8,128)(2,1)}, u32[]{:S(2)}, u32[]{:S(2)}) collective-permute-start(bf16[8192,128]{1,0:T(8,128)(2,1)} %get-tuple-element.297), channel_id=1, source_target_pairs={{0,1},{1,0},{2,3},{3,2},{4,5},{5,4},{6,7},{7,6},{8,9},{9,8},{10,11... | collective-permute-start | bytes 6291464 | tf_op jit(solution)/shard_map/ppermute | solution.py:810
  455.9 54.8 %collective-permute-start.38 = (bf16[2,4096,128]{2,1,0:T(8,128)(2,1)}, bf16[2,4096,128]{2,1,0:T(8,128)(2,1)}, u32[]{:S(2)}, u32[]{:S(2)}) collective-permute-start(bf16[2,4096,128]{2,1,0:T(8,128)(2,1)} %get-tuple-element.298), channel_id=1, source_target_pairs={{0,4},{2,6},{4,0},{6,2},{8,12},{10,14},{12,8},{14,10},{16,20},{18,... | collective-permute-start | bytes 6291464 | tf_op jit(solution)/shard_map/ppermute | solution.py:810
  457.4 53.3 %collective-permute-start.39 = (bf16[2,4096,128]{2,1,0:T(8,128)(2,1)}, bf16[2,4096,128]{2,1,0:T(8,128)(2,1)}, u32[]{:S(2)}, u32[]{:S(2)}) collective-permute-start(bf16[2,4096,128]{2,1,0:T(8,128)(2,1)} %get-tuple-element.299), channel_id=1, source_target_pairs={{0,8},{2,10},{4,12},{6,14},{8,0},{10,2},{12,4},{14,6},{16,24},{18,... | collective-permute-start | bytes 6291464 | tf_op jit(solution)/shard_map/ppermute | solution.py:810
  457.9 52.7 %collective-permute-start.40 = (bf16[96,1024]{1,0:T(8,128)(2,1)S(1)}, bf16[96,1024]{1,0:T(8,128)(2,1)S(1)}, u32[]{:S(2)}, u32[]{:S(2)}) collective-permute-start(bf16[96,1024]{1,0:T(8,128)(2,1)S(1)} %get-tuple-element.300), channel_id=1, source_target_pairs={{0,2},{2,0},{4,6},{6,4},{8,10},{10,8},{12,14},{14,12},{16,18},{18,... | collective-permute-start | bytes 589832 | tf_op jit(solution)/shard_map/ppermute | solution.py:810
  522.5 51.1 %collective-permute-start.41 = (bf16[1,3072,1024]{2,1,0:T(8,128)(2,1)}, bf16[1,3072,1024]{2,1,0:T(8,128)(2,1)}, u32[]{:S(2)}, u32[]{:S(2)}) collective-permute-start(bf16[1,3072,1024]{2,1,0:T(8,128)(2,1)} %shard_map.243), channel_id=1, source_target_pairs={{0,2},{2,0},{4,6},{6,4},{8,10},{10,8},{12,14},{14,12},{16,18},{18,... | collective-permute-start | bytes 18874376 | tf_op jit(solution)/shard_map/ppermute | solution.py:810
  523.0 50.6 %collective-permute-start.45 = (bf16[2,768,384]{2,1,0:T(8,128)(2,1)}, bf16[2,768,384]{2,1,0:T(8,128)(2,1)S(1)}, u32[]{:S(2)}, u32[]{:S(2)}) collective-permute-start(bf16[2,768,384]{2,1,0:T(8,128)(2,1)} %get-tuple-element.330), channel_id=1, source_target_pairs={{0,8},{2,10},{4,12},{6,14},{8,0},{10,2},{12,4},{14,6},{16,24},{18,... | collective-permute-start | bytes 3538952 | tf_op jit(solution)/shard_map/ppermute | solution.py:810
  525.0 48.6 %collective-permute-start.43 = (bf16[2,2,2,512,128]{4,3,2,1,0:T(8,128)(2,1)}, bf16[2,2,2,512,128]{4,3,2,1,0:T(8,128)(2,1)S(1)}, u32[]{:S(2)}, u32[]{:S(2)}) collective-permute-start(bf16[2,2,2,512,128]{4,3,2,1,0:T(8,128)(2,1)} %bitcast.66), channel_id=1, source_target_pairs={{0,8},{2,10},{4,12},{6,14},{8,0},{10,2},{12,4},{14,6},{16,24},{18,... | collective-permute-start | bytes 3145736 | tf_op jit(solution)/shard_map/ppermute | solution.py:810
  526.1 47.4 %collective-permute-start.44 = (bf16[1,2,2,2,512,128]{5,4,3,2,1,0:T(8,128)(2,1)}, bf16[1,2,2,2,512,128]{5,4,3,2,1,0:T(8,128)(2,1)}, u32[]{:S(2)}, u32[]{:S(2)}) collective-permute-start(bf16[1,2,2,2,512,128]{5,4,3,2,1,0:T(8,128)(2,1)} %slice_bitcast_fusion.1), channel_id=1, source_target_pairs={{0,1},{1,0},{2,3},{3,2},{4,5},{5,4},{6,7},{7,6},{8,9},{9,8},{10,11... | collective-permute-start | bytes 3145736 | tf_op jit(solution)/shard_map/ppermute | solution.py:810
  609.4 52.5 %collective-permute-start.51 = (bf16[512,1536]{1,0:T(8,128)(2,1)}, bf16[512,1536]{1,0:T(8,128)(2,1)}, u32[]{:S(2)}, u32[]{:S(2)}) collective-permute-start(bf16[512,1536]{1,0:T(8,128)(2,1)} %get-tuple-element.355), channel_id=1, source_target_pairs={{0,1},{1,0},{2,3},{3,2},{4,5},{5,4},{6,7},{7,6},{8,9},{9,8},{10,11... | collective-permute-start | bytes 4718600 | tf_op jit(solution)/shard_map/ppermute | solution.py:810
  610.0 51.9 %collective-permute-start.53 = (bf16[1,1536,512]{2,1,0:T(8,128)(2,1)}, bf16[1,1536,512]{2,1,0:T(8,128)(2,1)}, u32[]{:S(2)}, u32[]{:S(2)}) collective-permute-start(bf16[1,1536,512]{2,1,0:T(8,128)(2,1)} %get-tuple-element.357), channel_id=1, source_target_pairs={{0,4},{2,6},{4,0},{6,2},{8,12},{10,14},{12,8},{14,10},{16,20},{18,... | collective-permute-start | bytes 4718600 | tf_op jit(solution)/shard_map/ppermute | solution.py:810
  611.5 52.1 %collective-permute-start.54 = (bf16[1,1536,512]{2,1,0:T(8,128)(2,1)}, bf16[1,1536,512]{2,1,0:T(8,128)(2,1)S(1)}, u32[]{:S(2)}, u32[]{:S(2)}) collective-permute-start(bf16[1,1536,512]{2,1,0:T(8,128)(2,1)} %get-tuple-element.358), channel_id=1, source_target_pairs={{0,8},{2,10},{4,12},{6,14},{8,0},{10,2},{12,4},{14,6},{16,24},{18,... | collective-permute-start | bytes 4718600 | tf_op jit(solution)/shard_map/ppermute | solution.py:810
  612.1 49.9 %collective-permute-start.52 = (bf16[1,2,512,384]{3,2,1,0:T(8,128)(2,1)}, bf16[1,2,512,384]{3,2,1,0:T(8,128)(2,1)S(1)}, u32[]{:S(2)}, u32[]{:S(2)}) collective-permute-start(bf16[1,2,512,384]{3,2,1,0:T(8,128)(2,1)} %bitcast.87), channel_id=1, source_target_pairs={{0,16},{2,18},{4,20},{6,22},{8,24},{10,26},{12,28},{14,30},{16,0},... | collective-permute-start | bytes 2359304 | tf_op jit(solution)/shard_map/ppermute | solution.py:810
  668.6 45.5 %collective-permute-start.56 = (bf16[4608,128]{1,0:T(8,128)(2,1)}, bf16[4608,128]{1,0:T(8,128)(2,1)}, u32[]{:S(2)}, u32[]{:S(2)}) collective-permute-start(bf16[4608,128]{1,0:T(8,128)(2,1)} %get-tuple-element.372), channel_id=1, source_target_pairs={{0,1},{1,0},{2,3},{3,2},{4,5},{5,4},{6,7},{7,6},{8,9},{9,8},{10,11... | collective-permute-start | bytes 3538952 | tf_op jit(solution)/shard_map/ppermute | solution.py:810
  670.0 44.1 %collective-permute-start.57 = (bf16[2,2304,128]{2,1,0:T(8,128)(2,1)}, bf16[2,2304,128]{2,1,0:T(8,128)(2,1)S(1)}, u32[]{:S(2)}, u32[]{:S(2)}) collective-permute-start(bf16[2,2304,128]{2,1,0:T(8,128)(2,1)} %get-tuple-element.373), channel_id=1, source_target_pairs={{0,4},{2,6},{4,0},{6,2},{8,12},{10,14},{12,8},{14,10},{16,20},{18,... | collective-permute-start | bytes 3538952 | tf_op jit(solution)/shard_map/ppermute | solution.py:810
  670.7 43.4 %collective-permute-start.58 = (bf16[2,2304,128]{2,1,0:T(8,128)(2,1)}, bf16[2,2304,128]{2,1,0:T(8,128)(2,1)S(1)}, u32[]{:S(2)}, u32[]{:S(2)}) collective-permute-start(bf16[2,2304,128]{2,1,0:T(8,128)(2,1)} %get-tuple-element.374), channel_id=1, source_target_pairs={{0,8},{2,10},{4,12},{6,14},{8,0},{10,2},{12,4},{14,6},{16,24},{18,... | collective-permute-start | bytes 3538952 | tf_op jit(solution)/shard_map/ppermute | solution.py:810
  722.9 40.6 %collective-permute-start.64 = (bf16[1,2,192,1024]{3,2,1,0:T(8,128)(2,1)}, bf16[1,2,192,1024]{3,2,1,0:T(8,128)(2,1)}, u32[]{:S(2)}, u32[]{:S(2)}) collective-permute-start(bf16[1,2,192,1024]{3,2,1,0:T(8,128)(2,1)} %bitcast.108), channel_id=1, source_target_pairs={{0,16},{2,18},{4,20},{6,22},{8,24},{10,26},{12,28},{14,30},{16,0},... | collective-permute-start | bytes 2359304 | tf_op jit(solution)/shard_map/ppermute | solution.py:810
  (124 other events, 1668.9 us)
Sparse Core Ops, SparseCore 0:
  115.4 22.5 all-gather.3
  139.6 64.7 all-gather.5
  211.5 38.2 all-gather.7

commit v3 on v2

--- a/solution.py
+++ b/solution.py
@@ -260,29 +260,36 @@
     )
 
 
-def project_kernel(parts, own_rows, where_ref, tok_ref, gain_ref, mod_ref, cos_ref, sin_ref, own_ref, *refs):
+def project_kernel(parts, own_rows, where_ref, tok_ref, other_ref, gain_ref, mod_ref, cos_ref, sin_ref, own_ref, *refs):
     pieces = refs[:parts]
     hm_ref, full_ref, q_ref, k_ref, v_ref, qpre_ref, kpre_ref, pre_ref = refs[parts:]
     pid = pl.program_id(0)
-    rows = tok_ref.shape[0]
-    step = min(128, rows)
+    rows = own_rows + other_ref.shape[0]
+    step = min(128, own_rows)
     tile = full_ref.shape[1]
     per = D // tile
 
     @pl.when(pid == 0)
     def hidden():
-        def body(where):
-            x = tok_ref[where, :].astype(jnp.float32)
-            hid = x * rms_scale(x) * gain_ref[0:1]
-            hm_ref[where, :] = (hid * (1.0 + mod_ref[1:2]) + mod_ref[0:1]).astype(jnp.bfloat16)
-
-        chunks(rows, step, body)
+        for source, first in ((tok_ref, 0), (other_ref, own_rows)):
+
+            def body(i, carry, source=source, first=first):
+                x = source[pl.ds(pl.multiple_of(i * step, step), step), :].astype(jnp.float32)
+                hid = x * rms_scale(x) * gain_ref[0:1]
+                hid = (hid * (1.0 + mod_ref[1:2]) + mod_ref[0:1]).astype(jnp.bfloat16)
+                hm_ref[pl.ds(pl.multiple_of(first + i * step, step), step), :] = hid
+                return carry
+
+            lax.fori_loop(0, source.shape[0] // step, body, 0)
 
     n = own_ref.shape[0]
     full_ref[pl.ds(pl.multiple_of(where_ref[0], n), n), :] = own_ref[...]
-    for i, piece in enumerate(pieces):
-        n = piece.shape[0]
-        full_ref[pl.ds(pl.multiple_of(where_ref[i + 1], n), n), :] = piece[...]
+    i = 1
+    for piece in pieces:
+        n = piece.shape[1]
+        for k in range(piece.shape[0]):
+            full_ref[pl.ds(pl.multiple_of(where_ref[i], n), n), :] = piece[k]
+            i += 1
 
     for j in range(2 * per):
         count = own_rows if j < per else rows
@@ -313,9 +320,10 @@
             chunks(count, min(step, count), body)
 
 
-def project(tokens_all, own_rows, gains, mods, cosine, sine, weight, tile=512):
+def project(tokens, others, gains, mods, cosine, sine, weight, tile=512):
     own, pieces, starts = weight
-    rows = tokens_all.shape[0]
+    own_rows = tokens.shape[0]
+    rows = own_rows + others.shape[0]
     n = 3 * D // tile
     vtile = 2 * D // tile
     outs = [
@@ -332,15 +340,16 @@
         grid_spec=pltpu.PrefetchScalarGridSpec(
             num_scalar_prefetch=1,
             grid=(n,),
-            in_specs=[small_spec(a.shape) for a in (tokens_all, gains, mods, cosine, sine)]
-            + [pl.BlockSpec((p.shape[0], tile), lambda j, w: (0, j)) for p in [own] + pieces],
+            in_specs=[small_spec(a.shape) for a in (tokens, others, gains, mods, cosine, sine)]
+            + [pl.BlockSpec((own.shape[0], tile), lambda j, w: (0, j))]
+            + [pl.BlockSpec(p.shape[:2] + (tile,), lambda j, w: (0, 0, j)) for p in pieces],
             out_specs=[s if s is not None else small_spec(shape) for shape, _, s in outs],
             scratch_shapes=[pltpu.VMEM((rows, D), jnp.float32)],
         ),
         out_shape=[jax.ShapeDtypeStruct(shape, d) for shape, d, _ in outs],
         compiler_params=params(58),
         cost_estimate=cost(2 * D * D * (own_rows + 2 * rows), 60e6),
-    )(jnp.stack(starts).astype(jnp.int32), tokens_all, gains, mods, cosine, sine, own, *pieces)
+    )(jnp.stack(starts).astype(jnp.int32), tokens, others, gains, mods, cosine, sine, own, *pieces)
 
 
 def output_kernel(which_ref, a_ref, w0_ref, w1_ref, x_ref, gain_ref, mod_ref, o_ref, mid_ref, hfm_ref):
@@ -664,11 +673,11 @@
     dx_ref[...] = dx.astype(jnp.bfloat16)
 
 
-def project_back(dqkv, first, own, tokens_all, full_qkv, gains, mods):
+def project_back(dqkv, first, own, tokens, full_qkv, gains, mods):
     rows = dqkv.shape[0] - own if first else own
     step = min(256, own)
     skip = first // step
-    row = pl.BlockSpec((step, D), lambda i: (i + skip, 0))
+    row = pl.BlockSpec((step, D), lambda i: (i, 0))
     return pl.pallas_call(
         functools.partial(project_back_kernel, first == 0),
         grid=(max(rows // step, 1),),
@@ -682,7 +691,7 @@
         ],
         compiler_params=params(),
         cost_estimate=cost(6 * rows * D * D, 30e6),
-    )(dqkv, tokens_all, full_qkv, gains, mods)
+    )(dqkv, tokens, full_qkv, gains, mods)
 
 
 def product_kernel(widths, has_received, where_ref, d_ref, a_ref, *refs):
@@ -818,44 +827,41 @@
     return env[1] == 2 and bits_of(env[0]) >= 3
 
 
-def gather_pieces(shard, routes, env):
-    nd, nf, me, mine = env
+class Pieces:
+    def __init__(self, shard, first, chunk, route, flow):
+        nd, nf, me, mine = flow.env
+        self.flow, self.route, self.stack = flow, list(enumerate(route)), None
+        rows = chunk >> len(route)
+        index = sum(((me >> b) & 1) << i for i, b in enumerate(route))
+        base = first + (mine ^ 1) * shard.shape[0]
+        self.starts = [base + (index ^ rel) * rows for rel in range(1 << len(route))]
+        part = lax.dynamic_slice_in_dim(shard, first + index * rows, rows, 0)
+        flow.send(part[None], "fsdp", 1, self.land, 0)
+
+    def land(self, got):
+        held = [] if self.stack is None else [self.stack]
+        if not self.route:
+            self.pieces = held + [got]
+            return
+        self.stack = jnp.concatenate(held + [got]) if held else got
+        if self.route:
+            _, b = self.route.pop(0)
+            self.flow.send(self.stack, "dp", 1 << b, self.land, 0)
+
+
+def slice_for(shard, env):
+    rows = shard.shape[0] // 8
+    return lax.dynamic_slice_in_dim(shard, (env[2] & 7) * rows, rows, 0)
+
+
+def gather_half(shard, got, env):
+    nd = env[0]
     if not special(env):
         full = lax.all_gather(shard, "fsdp", axis=0, tiled=True)
         half = full.shape[0] // 2
-        return (full[:half], [full[half:]], [jnp.int32(0), jnp.int32(half)]), shard
-    rows = shard.shape[0]
-    chunk = rows // len(routes)
-    pieces, starts, firsts = [], [], []
-    for r, route in enumerate(routes):
-        piece_rows = chunk >> len(route)
-        index = sum(((me >> b) & 1) << i for i, b in enumerate(route))
-        base = r * chunk + (mine ^ 1) * rows
-        part = lax.dynamic_slice_in_dim(shard, r * chunk + index * piece_rows, piece_rows, 0)
-        held = [(0, swap(part, "fsdp", 1, nf))]
-        firsts.append(held[0][1])
-        for i, b in enumerate(route):
-            held = held + [(rel | (1 << i), swap(p, "dp", 1 << b, nd)) for rel, p in held]
-        for rel, p in held:
-            pieces.append(p)
-            starts.append(base + (index ^ rel) * piece_rows)
-    return (shard, pieces, [mine * rows] + starts), firsts
-
-
-def gather_half(shard, env, hold, late):
-    nd, nf, me, mine = env
-    if not special(env):
-        full = lax.all_gather(shard, "fsdp", axis=0, tiled=True)
-        half = full.shape[0] // 2
-        return (full[:half], full[half:]), shard
-    rows = shard.shape[0] // 8
-    part = after(lax.dynamic_slice_in_dim(shard, (me & 7) * rows, rows, 0), *hold)
-    got = swap(part, "fsdp", 1, nf)
+        return (full[:half], full[half:])
     groups = [list(range(i, i + 8)) for i in range(0, nd, 8)]
-    if late:
-        got = after(got, *late)
-    other = lax.all_gather(got, "dp", axis=0, tiled=True, axis_index_groups=groups)
-    return (shard, other), got
+    return (shard, lax.all_gather(got, "dp", axis=0, tiled=True, axis_index_groups=groups))
 
 
 def gather_relative(value, env):
@@ -887,14 +893,9 @@
     return value
 
 
-def gather_small(pack, env):
-    nf, mine = env[1], env[3]
-    if nf != 2:
-        return lax.all_gather(pack, "fsdp", axis=1, tiled=True)
-    got = swap(pack, "fsdp", 1, nf)
-    return jnp.concatenate(
-        [jnp.where(mine == 0, pack, got), jnp.where(mine == 0, got, pack)], axis=1
-    )
+def side_by_side(own, got, mine):
+    first = mine == 0
+    return jnp.concatenate([jnp.where(first, own, got), jnp.where(first, got, own)], axis=1)
 
 
 def stages_of(order, env):
@@ -918,24 +919,29 @@
 
     def __init__(self, env):
         self.env, self.pending, self.flying = env, [], []
-
-    def send(self, operand, axis, mask, land, rank):
-        self.pending.append((operand, axis, mask, land, rank))
+        self.mark = jnp.zeros((8, 128), jnp.float32)
+
+    def send(self, operand, axis, mask, land, rank, windows=1):
+        self.pending.append((operand, axis, mask, land, rank, windows))
 
     def turn(self, outs, ins):
         nd, nf = self.env[:2]
-        flying, self.flying = self.flying, []
-        if flying:
-            tied = lax.optimization_barrier(tuple(got for got, _ in flying) + tuple(outs))
-            for got, (_, land) in zip(tied, flying):
+        landing = [(got, land) for got, land, left in self.flying if left == 1]
+        self.flying = [(got, land, left - 1) for got, land, left in self.flying if left > 1]
+        if landing:
+            gots = tuple(got for got, _ in landing)
+            tied = lax.optimization_barrier(gots + tuple(outs) + (self.mark,))
+            self.mark = tied[-1]
+            for got, (_, land) in zip(tied, landing):
                 land(got)
         pending = sorted(self.pending, key=lambda p: p[4])
-        pending, self.pending = pending[: self.most], pending[self.most :]
+        pending, self.pending = pending[: self.most - len(self.flying)], pending[self.most - len(self.flying) :]
         sends = tuple(p[0] for p in pending)
-        tied = lax.optimization_barrier(sends + tuple(ins) + tuple(outs))
-        for operand, (_, axis, mask, land, _) in zip(tied, pending):
+        tied = lax.optimization_barrier(sends + tuple(ins) + tuple(outs) + (self.mark,))
+        self.mark = tied[-1]
+        for operand, (_, axis, mask, land, _, windows) in zip(tied, pending):
             size = nd if axis == "dp" else nf
-            self.flying.append((swap(operand, axis, mask, size), land))
+            self.flying.append((swap(operand, axis, mask, size), land, windows))
         return tied[len(sends) : len(sends) + len(ins)]
 
     def drain(self, outs):
@@ -970,7 +976,7 @@
         )
         return pick(bit), pick(bit ^ 1)
 
-    def launch(self, flow, landed, rank):
+    def launch(self, flow, landed, rank, windows=1):
         axis, b = self.stages.pop(0)
         if self.sent is None:
             kept, send = self.split(axis, b)
@@ -981,7 +987,7 @@
             self.current = add_low([kept, got.reshape(kept.shape)])
             landed()
 
-        flow.send(send, axis, 1 << b, land, rank)
+        flow.send(send, axis, 1 << b, land, rank, windows)
 
 
 def join_rows(kept, got, env):
@@ -1015,7 +1021,8 @@
 
 
 class Reduction:
-    def __init__(self, dact, act, portions, flow, rank, rows_only=False):
+    def __init__(self, dact, act, portions, flow, rank, rows_only=False, last_windows=1):
+        self.windows, self.last_windows = 1, last_windows
         self.flow, self.env, self.act, self.rank = flow, flow.env, act, rank
         self.portions, self.rows_only = portions, rows_only
         core = self.env[2] & 1
@@ -1064,13 +1071,14 @@
         if ladders[0].stages:
             self.waiting = len(ladders)
             for ladder in ladders:
-                ladder.launch(self.flow, self.landed, self.rank)
+                ladder.launch(self.flow, self.landed, self.rank, self.windows)
             return
         if len(ladders) > 1:
             joined = jnp.concatenate([r.current for r in ladders], axis=-1)
             self.ladders = ladders = [Ladder(joined, ladders[0].alive, [], self.env)]
         if ladders[0].alive:
             ladders[0].stages = [("dp", ladders[0].alive[-1])]
+            self.windows = self.last_windows
             self.launch()
             return
         core = self.env[2] & 1
@@ -1090,27 +1098,29 @@
 
 
 class WideSum:
-    def __init__(self, value, axes, flow, rank):
-        env = flow.env
-        self.rank = rank
-        self.value, self.flow = value, flow
-        self.hops = [
-            (axis, 1 << b)
-            for axis in axes
-            for b in range(bits_of(env[0] if axis == "dp" else env[1]))
-        ]
+    def __init__(self, value, groups, flow, rank):
+        self.value, self.flow, self.rank, self.groups = value, flow, rank, list(groups)
+        self.passed = []
         self.launch()
 
     def launch(self):
-        if self.hops:
-            axis, mask = self.hops.pop(0)
-            self.flow.send(self.value, axis, mask, self.land, self.rank)
+        self.passed.append(self.value)
+        if self.groups:
+            axis, masks = self.groups.pop(0)
+            self.waiting, self.total = len(masks), self.value.astype(jnp.float32)
+            for mask in masks:
+                self.flow.send(self.value, axis, mask, self.land, self.rank)
 
     def land(self, got):
-        self.value = self.value.astype(jnp.float32) + got.astype(jnp.float32)
-        if got.dtype == jnp.bfloat16:
-            self.value = self.value.astype(jnp.bfloat16)
-        self.launch()
+        self.total = self.total + got.astype(jnp.float32)
+        self.waiting -= 1
+        if not self.waiting:
+            self.value = self.total.astype(got.dtype)
+            self.launch()
+
+
+def hops(axis, size):
+    return [(axis, [1 << b]) for b in range(bits_of(size))]
 
 
 def portion_list(lanes, names):
@@ -1151,40 +1161,77 @@
             jnp.pad(cross_gate, (0, caption_gain.shape[0] - heads))[None],
         ]
     )
-    pack = gather_small(pack, env)
-    places = gather_relative(positions[0].T, env)
-    gath_qkv, firsts = gather_pieces(w_qkv, [(1, 2, 0), (2, 1, 0)], env)
-    tokens_all = gather_relative(after(tokens[0], *firsts), env)
-    partial_kv = dot(caption[0], w_caption_kv)
-    tokens_all = after(tokens_all, partial_kv)
-    late = tuple(gath_qkv[1]) + (tokens_all, pack, places)
-    full_gate_up, got = gather_half(w_gate_up, env, firsts, late)
-    full_out, _ = gather_half(w_out, env, (got,), late)
+    flow = Flow(env)
+    if special(env):
+        landed = {}
+        keep_as = lambda name: functools.partial(landed.__setitem__, name)
+        half = w_qkv.shape[0] // 2
+        gathers = [Pieces(w_qkv, 0, half, (1, 2, 0), flow), Pieces(w_qkv, half, half, (2, 1, 0), flow)]
+        flow.send(pack, "fsdp", 1, keep_as("pack"), 0)
+        flow.send(positions[0].T, "fsdp", 1, keep_as("places"), 0)
+        flow.turn((), ())
+        flow.send(slice_for(w_gate_up, env), "fsdp", 1, keep_as("gate_up"), 0)
+        (caption_in,) = flow.turn((), (caption[0],))
+        pack = side_by_side(pack, landed["pack"], mine)
+        places = jnp.concatenate([positions[0].T, landed["places"]])
+        partial_kv = dot(caption_in, w_caption_kv)
+        flow.send(tokens[0], "fsdp", 1, keep_as("tokens"), 0)
+        (places,) = flow.turn((partial_kv,), (places,))
+        full_gate_up = gather_half(w_gate_up, landed["gate_up"], env)
+        cosine, sine = rope_tables(places)
+        flow.turn((cosine, sine), ())
+        flow.turn((), ())
+        tokens_other = landed["tokens"]
+        flow.send(partial_kv.astype(jnp.bfloat16), "fsdp", 1, keep_as("caption"), 0)
+        flow.send(slice_for(w_out, env), "fsdp", 1, keep_as("out"), 0)
+        pieces = [p for g in gathers for p in g.pieces]
+        starts = [mine * w_qkv.shape[0]] + [s for g in gathers for s in g.starts]
+        gath_qkv = (w_qkv, pieces, starts)
+        (tokens_other,) = flow.turn((), (tokens_other,))
+    else:
+        pack = lax.all_gather(pack, "fsdp", axis=1, tiled=True)
+        cosine, sine = rope_tables(gather_relative(positions[0].T, env))
+        full = lax.all_gather(w_qkv, "fsdp", axis=0, tiled=True)
+        half = full.shape[0] // 2
+        gath_qkv = (full[:half], [full[half:][None]], [jnp.int32(0), jnp.int32(half)])
+        tokens_other = gather_relative(tokens[0], env)[own_rows:]
+        partial_kv = dot(caption[0], w_caption_kv)
+        full_gate_up = gather_half(w_gate_up, None, env)
     pack = pack.astype(jnp.float32)
     gains, mods, cap_gain = pack[:6], pack[6:12], pack[12]
     gate_heads = jnp.tanh(pack[13].reshape(nf, -1)[:, :heads].reshape(HEADS))
     gate_tanh = jnp.repeat(gate_heads, HEAD_DIM)[None]
-    cosine, sine = rope_tables(places)
+    bias = jnp.where(caption_mask[0] > 0, 0.0, -1e30).astype(jnp.float32)
     hm, full_qkv, query_b, key_b, value_b, query_pre, key_pre = project(
-        tokens_all, own_rows, gains, mods, cosine, sine, gath_qkv
-    )
-    cap_rows = sum_fsdp(after(partial_kv, tokens_all), env, hm)
+        tokens[0], tokens_other, gains, mods, cosine, sine, gath_qkv
+    )
+    if special(env):
+        (query_b,) = flow.turn((hm,), (query_b,))
+        cap_rows = partial_kv + landed["caption"].astype(jnp.float32)
+        full_out = gather_half(w_out, after(landed["out"], full_gate_up[1]), env)
+        flow.send(slice_for(w_down, env), "fsdp", 1, keep_as("down"), 0)
+        (query_b,) = flow.turn((), (query_b,))
+    else:
+        cap_rows = sum_fsdp(partial_kv, env)
+        full_out = gather_half(w_out, None, env)
     ckey_pre = cap_rows[:, :D]
     ckey_scale = rms_scale(ckey_pre)
     ckey_b = (ckey_pre * ckey_scale * cap_gain).astype(jnp.bfloat16)
     cvalue_b = cap_rows[:, D:].astype(jnp.bfloat16)
-    bias = jnp.where(caption_mask[0] > 0, 0.0, -1e30).astype(jnp.float32)
     combined, self_out, cross_out, stats = attend(
         query_b, key_b, value_b, ckey_b, cvalue_b, bias[None], gate_tanh
     )
-    full_down, _ = gather_half(w_down, env, (cvalue_b,), (stats,))
+    if special(env):
+        (combined,) = flow.turn((stats,), (combined,))
+        full_down = gather_half(w_down, landed["down"], env)
+    else:
+        full_down = gather_half(w_down, None, env)
     projected, middle, ffn_in = output_step(which, combined, full_out, tokens[0], gains, mods)
     gate_part, up_part, ffn_inner = gate_up_step(which, ffn_in, full_gate_up)
     block_out, grad_down, down_sums = down_step(
         which, ffn_inner, full_down, middle, cotangent[0], gains, mods
     )
     lanes_d, lanes_f = D // (2 * nf), FF // (2 * nf)
-    flow = Flow(env)
     red_down = Reduction(grad_down[None], ffn_inner, portion_list(lanes_f, ORDERS), flow, 1)
     (grad_down_b,) = flow.turn((red_down.partial,), (grad_down,))
     dgu = gate_up_back(which, grad_down_b, gate_part, up_part, full_down)
@@ -1205,7 +1252,7 @@
         grad_ckey.astype(jnp.float32), ckey_pre, ckey_scale, cap_gain
     )
     grad_cap_kv = jnp.concatenate([grad_ckey_pre, grad_cvalue.astype(jnp.float32)], axis=-1)
-    cap_sum = WideSum(grad_cap_kv.astype(jnp.bfloat16), ("fsdp",), flow, 0)
+    cap_sum = WideSum(grad_cap_kv.astype(jnp.bfloat16), hops("fsdp", nf), flow, 0)
     red_out = Reduction(grad_proj[None], combined, portion_list(lanes_d, ORDERS[2:]), flow, 1.5)
     dgu_b, grad_comb = flow.turn((gate_sums, red_out.partial), (dgu_b, grad_comb))
     done = red_gate_up.keep(dgu_b)
@@ -1220,12 +1267,12 @@
         return parts[-1][0]
 
     first = attention_part(grad_comb)
-    while nf > 2 and cap_sum.hops:
+    while nf > 2 and cap_sum.groups:
         flow.turn((done,), ())
     grad_comb, grad_proj = flow.turn((done, first), (grad_comb, grad_proj))
     grad_cap_kv = cap_sum.value
     red_caption = Reduction(
-        grad_cap_kv[None], caption[0], portion_list(caption.shape[2] // 2, ["xz", "zx"]), flow, 1.2, True
+        grad_cap_kv[None], caption[0], portion_list(caption.shape[2] // 2, ["xz", "zx"]), flow, 1.2, True, 1
     )
     out_done = red_out.keep(grad_proj[None])
     dones = [attention_part(grad_comb) for _ in range(3)]
@@ -1239,14 +1286,14 @@
     grad_mixed, grad_cap_kv = flow.turn((red_qkv.partial,), (grad_mixed, grad_cap_kv))
     done = red_caption.keep(grad_cap_kv[None])
     dx_other, other_sums = project_back(
-        grad_mixed, own_rows, own_rows, tokens_all, full_qkv, gains, mods
+        grad_mixed, own_rows, own_rows, tokens_other, full_qkv, gains, mods
     )
     dx_got = []
     if nf == 2:
         flow.send(dx_other, "fsdp", 1, dx_got.append, 0)
     (grad_mixed,) = flow.turn((done, other_sums), (grad_mixed,))
     done = red_qkv.keep(grad_mixed[None])
-    dx_own, own_sums = project_back(grad_mixed, 0, own_rows, tokens_all, full_qkv, gains, mods)
+    dx_own, own_sums = project_back(grad_mixed, 0, own_rows, tokens[0], full_qkv, gains, mods)
     project_sums = own_sums + other_sums if nf > 1 else own_sums
     small = jnp.concatenate(
         [
@@ -1263,7 +1310,6 @@
             ),
         ]
     )
-    small_sum = WideSum(small, ("fsdp", "dp"), flow, 2)
     mod_grads = jnp.stack(
         [
             project_sums[3],
@@ -1274,7 +1320,11 @@
             down_sums[0] * (1.0 - jnp.tanh(mods[5]) ** 2),
         ]
     )
-    mod_sum = WideSum(mod_grads, ("fsdp",), flow, 4)
+    along = hops("dp", nd)
+    if special(env):
+        along = along[2:] + [("dp", [1, 2, 3])]
+    small = jnp.concatenate([small, mod_grads, jnp.zeros((2, D), jnp.float32)])
+    small_sum = WideSum(small, hops("fsdp", nf) + along, flow, 1.3)
     (grad_cap_kv,) = flow.turn((done, own_sums), (grad_cap_kv,))
     if nf == 2:
         dx = dx_own.astype(jnp.float32) + dx_got[0].astype(jnp.float32)
@@ -1283,7 +1333,7 @@
     grad_tokens = (grad_mid + dx).astype(jnp.bfloat16)
     grad_caption = dot(grad_cap_kv, w_caption_kv, NT).astype(jnp.bfloat16)
     flow.drain((grad_caption, grad_tokens))
-    small, mod_grads = small_sum.value, mod_sum.value
+    small, mod_grads = small_sum.value, small_sum.passed[bits_of(nf)][8:14]
     out_down, out_gate_up, out_out, out_caption, out_qkv = (
         r.result for r in (red_down, red_gate_up, red_out, red_caption, red_qkv)
     )

time: 827 us -> 827 us (level)
  other arithmetic: 63.6 us -> 53.1 us
  waiting for transfers between devices: 205 us -> 214 us
    ppermute x80 -> x72, waiting for transfers between devices: 196 us -> 204 us  [swap(): return lax.ppermute(value, axis, [(i, i ^ mask) for i in range(size)])]
    ppermute x80 -> x72, starting transfers between devices: 76.7 us -> 71.2 us  [swap(): return lax.ppermute(value, axis, [(i, i ^ mask) for i in range(size)])]
    unnamed x131 -> x122, local copies, waits for them, and re-layouts: 17.9 us -> 21.5 us
  transfers between devices with their start and end apart: 83 -> 75, of which waited for: 27 -> 28; matrix products, arithmetic and copies ran while one was open for 8% -> 7% of each run, Pallas kernels for 41% -> 41%
where the time goes in v3:
time: 827 us; the launch traced here: 816 us
  Pallas kernels  394 us (48%)
  waiting for transfers between devices  214 us (26%)
  starting transfers between devices  71.3 us (9%)
  other arithmetic  53.1 us (6%)
  local copies, waits for them, and re-layouts  50.9 us (6%)
  matrix products  17.5 us (2%)
  between operations  15.3 us (2%)
    ppermute x72, waiting for transfers between devices, swap(): return lax.ppermute(value, axis, [(i, i ^ mask) for i in range(size)])  204 us
    ppermute x72, starting transfers between devices, swap(): return lax.ppermute(value, axis, [(i, i ^ mask) for i in range(size)])  71.2 us
    pallas_call x5, Pallas kernels, split_product(): pl.pallas_call(functools.partial(split_product_kernel, portions, count),...  59.5 us
    pallas_call x5, Pallas kernels, product(): pl.pallas_call(functools.partial(product_kernel, widths, received is not...  54.6 us
    pallas_call x4, Pallas kernels, self_back(): pl.pallas_call(self_back_kernel, grid=(count,), in_specs=[spec(rows), spe...  45 us
    pallas_call x1, Pallas kernels, attend(): pl.pallas_call(attend_kernel, grid=(pairs,), in_specs=[spec(rows), spec(k...  42.4 us
    pallas_call x1, Pallas kernels, project(): pl.pallas_call(functools.partial(project_kernel, len(pieces), own_rows),...  35.3 us
    pallas_call x1, Pallas kernels, ffn_back(): pl.pallas_call(ffn_back_kernel, grid_spec=pltpu.PrefetchScalarGridSpec(nu...  34.9 us
  transfers between devices with their start and end apart: 75, of which 28 were waited for; matrix products, arithmetic and copies ran while one was open for 7% of the time, Pallas kernels for 41%

profile of v3, /device:TPU:0, one launch (start us, length us, event | category | flops | bytes accessed | tf_op | source)
XLA Modules:
  0.0 815.7 jit_solution(10190742543439372522)
XLA Ops:
  16.6 16.6 %collective-permute-done.3 = s32[512,2]{0,1:T(2,128)S(1)} collective-permute-done((s32[512,2]{0,1:T(2,128)S(1)}, s32[512,2]{0,1:T(2,128)S(1)}, u32[]{:S(2)}, u32[]{:S(2)}) %collective-permute-start.3) | collective-permute-done | bytes 4128 | tf_op jit(solution)/shard_map/ppermute | solution.py:819
  47.7 21.3 %collective-permute-done.4 = bf16[96,8192]{1,0:T(8,128)(2,1)} collective-permute-done((bf16[96,8192]{1,0:T(8,128)(2,1)S(1)}, bf16[96,8192]{1,0:T(8,128)(2,1)}, u32[]{:S(2)}, u32[]{:S(2)}) %collective-permute-start.4) | collective-permute-done | bytes 1572896 | tf_op jit(solution)/shard_map/ppermute | solution.py:819
  78.2 25.6 %collective-permute-done.8 = bf16[2,48,4608]{2,1,0:T(8,128)(2,1)S(1)} collective-permute-done((bf16[2,48,4608]{2,1,0:T(8,128)(2,1)S(1)}, bf16[2,48,4608]{2,1,0:T(8,128)(2,1)S(1)}, u32[]{:S(2)}, u32[]{:S(2)}) %collective-permute-start.8) | collective-permute-done | bytes 884768 | tf_op jit(solution)/shard_map/ppermute | solution.py:819
  119.5 35.3 %shard_map.229 = (bf16[1024,1536]{1,0:T(8,128)(2,1)}, bf16[1536,4608]{1,0:T(8,128)(2,1)}, bf16[512,1536]{1,0:T(8,128)(2,1)}, bf16[1024,1536]{1,0:T(8,128)(2,1)},...) custom-call(s32[17]{0:T(128)} %stack.138.where_ref, ...), custom_call_target="tpu_custom_call" | custom-call | flops 603979776 | bytes 3000000 | tf_op jit(solution)/shard_map/pallas_call | solution.py:338
  165.6 42.4 %shard_map.230 = (bf16[512,1536]{1,0:T(8,128)(2,1)S(1)}, bf16[512,1536]{1,0:T(8,128)(2,1)S(1)}, bf16[512,1536]{1,0:T(8,128)(2,1)}, f32[12,8,512]{2,1,0:T(8,128)S(1)}) custom-call(bf16[512,1536]{1,0:T(8,128)(2,1)} %get-tuple-element.318.q_ref, bf16[1024,1536]{1,0:T(8,128)(2,1)} %get-tuple-element.319.k_ref, bf16[1024,1536]{1,0:T(8,128)(2,1)} %get-tuple-element.320.v_ref, ...), custom_call_target="tpu_custom_call" | custom-call | flops 805306368 | bytes 1000000 | tf_op jit(solution)/shard_map/pallas_call | solution.py:86
  219.6 21.2 %shard_map.232 = (bf16[512,4096]{1,0:T(8,128)(2,1)}, bf16[512,4096]{1,0:T(8,128)(2,1)}, bf16[512,4096]{1,0:T(8,128)(2,1)}) custom-call(s32[1]{0:T(128)} %bitcast.which_ref, bf16[512,1536]{1,0:T(8,128)(2,1)} %get-tuple-element.331.h_ref.a_ref.refs_0_.refs_1_, bf16[768,8192]{1,0:T(8,128)(2,1)} %u0_ref.3, ...), custom_call_target="tpu_custom_call" | custom-call | flops 644245120 | bytes 2000000 | tf_op jit(solution)/shard_map/pallas_call | solution.py:407
  250.2 18.2 %shard_map.233 = (bf16[512,1536]{1,0:T(8,128)(2,1)}, bf16[512,1536]{1,0:T(8,128)(2,1)}, f32[8,1536]{1,0:T(8,128)}) custom-call(s32[1]{0:T(128)} %bitcast.which_ref, bf16[512,4096]{1,0:T(8,128)(2,1)} %get-tuple-element.332.ff_ref.a_ref.refs_0_.refs_1_, bf16[2048,1536]{1,0:T(8,128)(2,1)} %d0_ref.1, ...), custom_call_target="tpu_custom_call" | custom-call | flops 322122560 | bytes 1200000 | tf_op jit(solution)/shard_map/pallas_call | solution.py:458
  279.3 17.4 %shard_map.235.d_ref.dgu_ref = bf16[2,512,4096]{2,1,0:T(8,128)(2,1)} custom-call(s32[1]{0:T(128)} %bitcast.which_ref, bf16[512,1536]{1,0:T(8,128)(2,1)} %get-tuple-element.344.df_ref, bf16[512,4096]{1,0:T(8,128)(2,1)} %get-tuple-element.339.ga_ref, bf16[512,4096]{1,0:T(8,128)(2,1)} %get-tuple-element.340.up_ref, bf16[2048,1536]{1,0:T(8,128)(2,1)} %d0_ref.1, ...), custom_call_target="tpu_custom_call" | custom-call | flops 322122560 | bytes 1500000 | tf_op jit(solution)/shard_map/pallas_call | solution.py:503
  310.7 16.8 %shard_map.237 = bf16[2,8192,384]{2,1,0:T(8,128)(2,1)} custom-call(s32[2]{0:T(128)} %pad_add_fusion.1.where_ref, bf16[2,512,4096]{2,1,0:T(8,128)(2,1)} %shard_map.235.d_ref.dgu_ref, bf16[512,1536]{1,0:T(8,128)(2,1)} %get-tuple-element.331.h_ref.a_ref.refs_0_.refs_1_), custom_call_target="tpu_custom_call" | custom-call | flops 322122560 | bytes 1258291 | tf_op jit(solution)/shard_map/pallas_call | solution.py:718
  346.2 34.9 %shard_map.238 = (f32[512,1536]{1,0:T(8,128)}, bf16[512,1536]{1,0:T(8,128)(2,1)}, bf16[512,1536]{1,0:T(8,128)(2,1)}, f32[8,1536]{1,0:T(8,128)}) custom-call(s32[1]{0:T(128)} %bitcast.which_ref, bf16[2,512,4096]{2,1,0:T(8,128)(2,1)} %shard_map.235.d_ref.dgu_ref, bf16[768,8192]{1,0:T(8,128)(2,1)} %u0_ref.3, ...), custom_call_target="tpu_custom_call" | custom-call | flops 765041024 | bytes 2750000 | tf_op jit(solution)/shard_map/pallas_call | solution.py:582
  386.9 13.7 %shard_map.239 = (bf16[512,1536]{1,0:T(8,128)(2,1)S(1)}, bf16[256,1536]{1,0:T(8,128)(2,1)S(1)}, bf16[256,1536]{1,0:T(8,128)(2,1)S(1)}, f32[1,1536]{1,0:T(1,128)S(1)}) custom-call(bf16[512,1536]{1,0:T(8,128)(2,1)} %get-tuple-element.318.q_ref, bf16[256,1536]{1,0:T(8,128)(2,1)S(1)} %multiply_convert_fusion.ck_ref, bf16[256,1536]{1,0:T(8,128)(2,1)S(1)} %slice.223.cv_ref, ...), custom_call_target="tpu_custom_call" | custom-call | flops 402653184 | bytes 450000 | tf_op jit(solution)/shard_map/pallas_call | solution.py:170
  422.1 17.4 %shard_map.241 = (bf16[8192,128]{1,0:T(8,128)(2,1)}, bf16[8192,128]{1,0:T(8,128)(2,1)}, bf16[2,4096,128]{2,1,0:T(8,128)(2,1)}, bf16[2,4096,128]{2,1,0:T(8,128)(2...) custom-call(s32[4]{0:T(128)} %pad_add_fusion.2.where_ref, ...), custom_call_target="tpu_custom_call" | custom-call | flops 322122560 | bytes 1258291 | tf_op jit(solution)/shard_map/pallas_call | solution.py:794
  439.5 11.1 %shard_map.242 = (bf16[512,384]{1,0:T(8,128)(2,1)S(1)}, bf16[1024,384]{1,0:T(8,128)(2,1)S(1)}, bf16[1024,384]{1,0:T(8,128)(2,1)S(1)}) custom-call(bf16[512,1536]{1,0:T(8,128)(2,1)S(1)} %copy-done, bf16[1024,1536]{1,0:T(8,128)(2,1)} %get-tuple-element.319.k_ref, bf16[1024,1536]{1,0:T(8,128)(2,1)} %get-tuple-element.320.v_ref, ...), custom_call_target="tpu_custom_call" | custom-call | flops 805306368 | bytes 150000 | tf_op jit(solution)/shard_map/pallas_call | solution.py:191
  476.2 11.1 %shard_map.245 = (bf16[512,384]{1,0:T(8,128)(2,1)S(1)}, bf16[1024,384]{1,0:T(8,128)(2,1)S(1)}, bf16[1024,384]{1,0:T(8,128)(2,1)S(1)}) custom-call(bf16[512,1536]{1,0:T(8,128)(2,1)S(1)} %copy-done, bf16[1024,1536]{1,0:T(8,128)(2,1)} %get-tuple-element.319.k_ref, bf16[1024,1536]{1,0:T(8,128)(2,1)} %get-tuple-element.320.v_ref, ...), custom_call_target="tpu_custom_call" | custom-call | flops 805306368 | bytes 150000 | tf_op jit(solution)/shard_map/pallas_call | solution.py:191
  488.9 11.4 %shard_map.246 = (bf16[512,384]{1,0:T(8,128)(2,1)S(1)}, bf16[1024,384]{1,0:T(8,128)(2,1)S(1)}, bf16[1024,384]{1,0:T(8,128)(2,1)S(1)}) custom-call(bf16[512,1536]{1,0:T(8,128)(2,1)S(1)} %copy-done, bf16[1024,1536]{1,0:T(8,128)(2,1)} %get-tuple-element.319.k_ref, bf16[1024,1536]{1,0:T(8,128)(2,1)} %get-tuple-element.320.v_ref, ...), custom_call_target="tpu_custom_call" | custom-call | flops 805306368 | bytes 150000 | tf_op jit(solution)/shard_map/pallas_call | solution.py:191
  502.0 11.4 %shard_map.247 = (bf16[512,384]{1,0:T(8,128)(2,1)S(1)}, bf16[1024,384]{1,0:T(8,128)(2,1)S(1)}, bf16[1024,384]{1,0:T(8,128)(2,1)S(1)}) custom-call(bf16[512,1536]{1,0:T(8,128)(2,1)S(1)} %copy-done, bf16[1024,1536]{1,0:T(8,128)(2,1)} %get-tuple-element.319.k_ref, bf16[1024,1536]{1,0:T(8,128)(2,1)} %get-tuple-element.320.v_ref, ...), custom_call_target="tpu_custom_call" | custom-call | flops 805306368 | bytes 150000 | tf_op jit(solution)/shard_map/pallas_call | solution.py:191
  529.5 13.7 %shard_map.248 = (bf16[1024,4608]{1,0:T(8,128)(2,1)}, f32[8,1536]{1,0:T(8,128)}) custom-call(bf16[512,384]{1,0:T(8,128)(2,1)} %copy-done.13, bf16[512,384]{1,0:T(8,128)(2,1)} %copy-done.14, bf16[512,384]{1,0:T(8,128)(2,1)} %copy-done.15, bf16[512,384]{1,0:T(8,128)(2,1)} %copy-done.16, bf16[1024,384]{1,0:T(8,128)(2,1)} %copy-done.5, ...), custom_call_target="tpu_custom_call" | custom-call | flops 4718592 | bytes 1500000 | tf_op jit(solution)/shard_map/pallas_call | solution.py:645
  543.2 16.6 %shard_map.249 = bf16[2,4608,384]{2,1,0:T(8,128)(2,1)} custom-call(s32[2]{0:T(128)} %pad_add_fusion.1.where_ref, bf16[1,1024,4608]{2,1,0:T(8,128)(2,1)} %bitcast.239, bf16[1024,1536]{1,0:T(8,128)(2,1)} %get-tuple-element.311.a_ref.refs_0_.refs_1_), custom_call_target="tpu_custom_call" | custom-call | flops 362387872 | bytes 707788 | tf_op jit(solution)/shard_map/pallas_call | solution.py:718
  559.8 16.5 %collective-permute-done.35 = bf16[2,2,2,512,128]{4,3,2,1,0:T(8,128)(2,1)S(1)} collective-permute-done((bf16[2,2,2,512,128]{4,3,2,1,0:T(8,128)(2,1)}, bf16[2,2,2,512,128]{4,3,2,1,0:T(8,128)(2,1)S(1)}, u32[]{:S(2)}, u32[]{:S(2)}) %collective-permute-start.35) | collective-permute-done | bytes 1048608 | tf_op jit(solution)/shard_map/ppermute | solution.py:819
  595.6 13.5 %shard_map.250 = (bf16[512,1536]{1,0:T(8,128)(2,1)}, f32[8,1536]{1,0:T(8,128)}) custom-call(bf16[1024,4608]{1,0:T(8,128)(2,1)} %get-tuple-element.467.dqkv_ref, bf16[512,1536]{1,0:T(8,128)(2,1)} %copy-done.22, bf16[1536,4608]{1,0:T(8,128)(2,1)} %get-tuple-element.450.w_ref, f32[6,1536]{1,0:T(8,128)} %get-tuple-element.611.gain_ref.refs_16_, ...), custom_call_target="tpu_custom_call" | custom-call | flops 362387872 | bytes 1500000 | tf_op jit(solution)/shard_map/pallas_call | solution.py:681
  620.7 16.1 %shard_map.252 = (bf16[512,1536]{1,0:T(8,128)(2,1)}, f32[8,1536]{1,0:T(8,128)}) custom-call(bf16[1024,4608]{1,0:T(8,128)(2,1)} %get-tuple-element.467.dqkv_ref, bf16[512,1536]{1,0:T(8,128)(2,1)} %bitcast.247, bf16[1536,4608]{1,0:T(8,128)(2,1)} %get-tuple-element.450.w_ref, f32[6,1536]{1,0:T(8,128)} %get-tuple-element.611.gain_ref.refs_16_, ...), custom_call_target="tpu_custom_call" | custom-call | flops 362387872 | bytes 1500000 | tf_op jit(solution)/shard_map/pallas_call | solution.py:681
  637.7 16.2 %shard_map.253 = (bf16[4608,128]{1,0:T(8,128)(2,1)}, bf16[4608,128]{1,0:T(8,128)(2,1)}, bf16[2,2304,128]{2,1,0:T(8,128)(2,1)}, bf16[2,2304,128]{2,1,0:T(8,128)(2...) custom-call(s32[4]{0:T(128)} %pad_add_fusion.2.where_ref, bf16[1,1024,4608]{2,1,0:T(8,128)(2,1)} %bitcast.240, ...), custom_call_target="tpu_custom_call" | custom-call | flops 362387872 | bytes 707788 | tf_op jit(solution)/shard_map/pallas_call | solution.py:794
  688.8 28.6 %collective-permute-done.51 = bf16[1,2,2,192,512]{4,3,2,1,0:T(8,128)(2,1)} collective-permute-done((bf16[1,2,2,192,512]{4,3,2,1,0:T(8,128)(2,1)}, bf16[1,2,2,192,512]{4,3,2,1,0:T(8,128)(2,1)}, u32[]{:S(2)}, u32[]{:S(2)}) %collective-permute-start.51) | collective-permute-done | bytes 786464 | tf_op jit(solution)/shard_map/ppermute | solution.py:819
  780.8 18.1 %collective-permute-done.64 = f32[16,1536]{1,0:T(8,128)S(1)} collective-permute-done((f32[16,1536]{1,0:T(8,128)S(1)}, f32[16,1536]{1,0:T(8,128)S(1)}, u32[]{:S(2)}, u32[]{:S(2)}) %collective-permute-start.64) | collective-permute-done | bytes 98336 | tf_op jit(solution)/shard_map/ppermute | solution.py:819
  (428 shorter events, 335.7 us)
Async XLA Ops:
  7.2 151.9 %all-gather.4.cloned.1.call-start = ((), (), s32[]{:S(2)}) async-start(), calls=%async_computation | async-start | bytes 14155776 | tf_op jit(solution)/shard_map/all_gather | solution.py:864
  69.0 142.1 %all-gather.6.cloned.1.call-start = ((), (), s32[]{:S(2)}) async-start(), calls=%async_computation.1 | async-start | bytes 2654208 | tf_op jit(solution)/shard_map/all_gather | solution.py:864
  116.1 43.1 %collective-permute-start.12 = (bf16[256,3072]{1,0:T(8,128)(2,1)}, bf16[256,3072]{1,0:T(8,128)(2,1)}, u32[]{:S(2)}, u32[]{:S(2)}) collective-permute-start(bf16[256,3072]{1,0:T(8,128)(2,1)} %get-tuple-element.312), channel_id=1, source_target_pairs={{0,1},{1,0},{2,3},{3,2},{4,5},{5,4},{6,7},{7,6},{8,9},{9,8},{10,11... | collective-permute-start | bytes 4718600 | tf_op jit(solution)/shard_map/ppermute | solution.py:819
  116.8 42.3 %collective-permute-start.13 = (bf16[96,1536]{1,0:T(8,128)(2,1)}, bf16[96,1536]{1,0:T(8,128)(2,1)}, u32[]{:S(2)}, u32[]{:S(2)}) collective-permute-start(bf16[96,1536]{1,0:T(8,128)(2,1)} %constant_dynamic-slice_fusion.44), channel_id=1, source_target_pairs={{0,1},{1,0},{2,3},{3,2},{4,5},{5,4},{6,7},{7,6},{8,9},{9,8},{10,11... | collective-permute-start | bytes 884744 | tf_op jit(solution)/shard_map/ppermute | solution.py:819
  159.2 91.0 %all-gather.8.cloned.1.call-start = ((), (), s32[]{:S(2)}) async-start(), calls=%async_computation.2 | async-start | bytes 7077888 | tf_op jit(solution)/shard_map/all_gather | solution.py:864
  161.6 48.8 %collective-permute-start.14 = (bf16[256,1536]{1,0:T(8,128)(2,1)}, bf16[256,1536]{1,0:T(8,128)(2,1)}, u32[]{:S(2)}, u32[]{:S(2)}) collective-permute-start(bf16[256,1536]{1,0:T(8,128)(2,1)} %constant_dynamic-slice_fusion.46), channel_id=1, source_target_pairs={{0,1},{1,0},{2,3},{3,2},{4,5},{5,4},{6,7},{7,6},{8,9},{9,8},{10,11... | collective-permute-start | bytes 2359304 | tf_op jit(solution)/shard_map/ppermute | solution.py:819
  342.9 38.2 %collective-permute-start.19 = (bf16[2,8192,384]{2,1,0:T(8,128)(2,1)}, bf16[2,8192,384]{2,1,0:T(8,128)(2,1)}, u32[]{:S(2)}, u32[]{:S(2)}) collective-permute-start(bf16[2,8192,384]{2,1,0:T(8,128)(2,1)} %shard_map.237), channel_id=1, source_target_pairs={{0,2},{2,0},{4,6},{6,4},{8,10},{10,8},{12,14},{14,12},{16,18},{18,... | collective-permute-start | bytes 37748744 | tf_op jit(solution)/shard_map/ppermute | solution.py:819
  457.1 56.3 %collective-permute-start.29 = (bf16[8192,128]{1,0:T(8,128)(2,1)}, bf16[8192,128]{1,0:T(8,128)(2,1)}, u32[]{:S(2)}, u32[]{:S(2)}) collective-permute-start(bf16[8192,128]{1,0:T(8,128)(2,1)} %get-tuple-element.408), channel_id=1, source_target_pairs={{0,1},{1,0},{2,3},{3,2},{4,5},{5,4},{6,7},{7,6},{8,9},{9,8},{10,11... | collective-permute-start | bytes 6291464 | tf_op jit(solution)/shard_map/ppermute | solution.py:819
  458.5 54.9 %collective-permute-start.30 = (bf16[2,4096,128]{2,1,0:T(8,128)(2,1)}, bf16[2,4096,128]{2,1,0:T(8,128)(2,1)}, u32[]{:S(2)}, u32[]{:S(2)}) collective-permute-start(bf16[2,4096,128]{2,1,0:T(8,128)(2,1)} %get-tuple-element.409), channel_id=1, source_target_pairs={{0,4},{2,6},{4,0},{6,2},{8,12},{10,14},{12,8},{14,10},{16,20},{18,... | collective-permute-start | bytes 6291464 | tf_op jit(solution)/shard_map/ppermute | solution.py:819
  460.0 53.4 %collective-permute-start.31 = (bf16[2,4096,128]{2,1,0:T(8,128)(2,1)}, bf16[2,4096,128]{2,1,0:T(8,128)(2,1)}, u32[]{:S(2)}, u32[]{:S(2)}) collective-permute-start(bf16[2,4096,128]{2,1,0:T(8,128)(2,1)} %get-tuple-element.410), channel_id=1, source_target_pairs={{0,8},{2,10},{4,12},{6,14},{8,0},{10,2},{12,4},{14,6},{16,24},{18,... | collective-permute-start | bytes 6291464 | tf_op jit(solution)/shard_map/ppermute | solution.py:819
  460.6 52.8 %collective-permute-start.32 = (bf16[96,1024]{1,0:T(8,128)(2,1)S(1)}, bf16[96,1024]{1,0:T(8,128)(2,1)S(1)}, u32[]{:S(2)}, u32[]{:S(2)}) collective-permute-start(bf16[96,1024]{1,0:T(8,128)(2,1)S(1)} %get-tuple-element.411), channel_id=1, source_target_pairs={{0,2},{2,0},{4,6},{6,4},{8,10},{10,8},{12,14},{14,12},{16,18},{18,... | collective-permute-start | bytes 589832 | tf_op jit(solution)/shard_map/ppermute | solution.py:819
  525.2 51.1 %collective-permute-start.33 = (bf16[1,3072,1024]{2,1,0:T(8,128)(2,1)}, bf16[1,3072,1024]{2,1,0:T(8,128)(2,1)}, u32[]{:S(2)}, u32[]{:S(2)}) collective-permute-start(bf16[1,3072,1024]{2,1,0:T(8,128)(2,1)} %shard_map.243), channel_id=1, source_target_pairs={{0,2},{2,0},{4,6},{6,4},{8,10},{10,8},{12,14},{14,12},{16,18},{18,... | collective-permute-start | bytes 18874376 | tf_op jit(solution)/shard_map/ppermute | solution.py:819
  525.7 50.6 %collective-permute-start.37 = (bf16[2,768,384]{2,1,0:T(8,128)(2,1)}, bf16[2,768,384]{2,1,0:T(8,128)(2,1)S(1)}, u32[]{:S(2)}, u32[]{:S(2)}) collective-permute-start(bf16[2,768,384]{2,1,0:T(8,128)(2,1)} %get-tuple-element.443), channel_id=1, source_target_pairs={{0,8},{2,10},{4,12},{6,14},{8,0},{10,2},{12,4},{14,6},{16,24},{18,... | collective-permute-start | bytes 3538952 | tf_op jit(solution)/shard_map/ppermute | solution.py:819
  527.8 48.6 %collective-permute-start.35 = (bf16[2,2,2,512,128]{4,3,2,1,0:T(8,128)(2,1)}, bf16[2,2,2,512,128]{4,3,2,1,0:T(8,128)(2,1)S(1)}, u32[]{:S(2)}, u32[]{:S(2)}) collective-permute-start(bf16[2,2,2,512,128]{4,3,2,1,0:T(8,128)(2,1)} %bitcast.68), channel_id=1, source_target_pairs={{0,8},{2,10},{4,12},{6,14},{8,0},{10,2},{12,4},{14,6},{16,24},{18,... | collective-permute-start | bytes 3145736 | tf_op jit(solution)/shard_map/ppermute | solution.py:819
  528.9 47.4 %collective-permute-start.36 = (bf16[1,2,2,2,512,128]{5,4,3,2,1,0:T(8,128)(2,1)}, bf16[1,2,2,2,512,128]{5,4,3,2,1,0:T(8,128)(2,1)}, u32[]{:S(2)}, u32[]{:S(2)}) collective-permute-start(bf16[1,2,2,2,512,128]{5,4,3,2,1,0:T(8,128)(2,1)} %slice_bitcast_fusion.1), channel_id=1, source_target_pairs={{0,1},{1,0},{2,3},{3,2},{4,5},{5,4},{6,7},{7,6},{8,9},{9,8},{10,11... | collective-permute-start | bytes 3145736 | tf_op jit(solution)/shard_map/ppermute | solution.py:819
  612.2 52.7 %collective-permute-start.43 = (bf16[512,1536]{1,0:T(8,128)(2,1)}, bf16[512,1536]{1,0:T(8,128)(2,1)}, u32[]{:S(2)}, u32[]{:S(2)}) collective-permute-start(bf16[512,1536]{1,0:T(8,128)(2,1)} %get-tuple-element.469), channel_id=1, source_target_pairs={{0,1},{1,0},{2,3},{3,2},{4,5},{5,4},{6,7},{7,6},{8,9},{9,8},{10,11... | collective-permute-start | bytes 4718600 | tf_op jit(solution)/shard_map/ppermute | solution.py:819
  612.7 52.1 %collective-permute-start.45 = (bf16[1,1536,512]{2,1,0:T(8,128)(2,1)}, bf16[1,1536,512]{2,1,0:T(8,128)(2,1)}, u32[]{:S(2)}, u32[]{:S(2)}) collective-permute-start(bf16[1,1536,512]{2,1,0:T(8,128)(2,1)} %get-tuple-element.471), channel_id=1, source_target_pairs={{0,4},{2,6},{4,0},{6,2},{8,12},{10,14},{12,8},{14,10},{16,20},{18,... | collective-permute-start | bytes 4718600 | tf_op jit(solution)/shard_map/ppermute | solution.py:819
  613.9 52.4 %collective-permute-start.46 = (bf16[1,1536,512]{2,1,0:T(8,128)(2,1)}, bf16[1,1536,512]{2,1,0:T(8,128)(2,1)S(1)}, u32[]{:S(2)}, u32[]{:S(2)}) collective-permute-start(bf16[1,1536,512]{2,1,0:T(8,128)(2,1)} %get-tuple-element.472), channel_id=1, source_target_pairs={{0,8},{2,10},{4,12},{6,14},{8,0},{10,2},{12,4},{14,6},{16,24},{18,... | collective-permute-start | bytes 4718600 | tf_op jit(solution)/shard_map/ppermute | solution.py:819
  614.8 50.1 %collective-permute-start.44 = (bf16[1,2,512,384]{3,2,1,0:T(8,128)(2,1)}, bf16[1,2,512,384]{3,2,1,0:T(8,128)(2,1)S(1)}, u32[]{:S(2)}, u32[]{:S(2)}) collective-permute-start(bf16[1,2,512,384]{3,2,1,0:T(8,128)(2,1)} %bitcast.89), channel_id=1, source_target_pairs={{0,16},{2,18},{4,20},{6,22},{8,24},{10,26},{12,28},{14,30},{16,0},... | collective-permute-start | bytes 2359304 | tf_op jit(solution)/shard_map/ppermute | solution.py:819
  671.3 46.0 %collective-permute-start.48 = (bf16[4608,128]{1,0:T(8,128)(2,1)}, bf16[4608,128]{1,0:T(8,128)(2,1)}, u32[]{:S(2)}, u32[]{:S(2)}) collective-permute-start(bf16[4608,128]{1,0:T(8,128)(2,1)} %get-tuple-element.487), channel_id=1, source_target_pairs={{0,1},{1,0},{2,3},{3,2},{4,5},{5,4},{6,7},{7,6},{8,9},{9,8},{10,11... | collective-permute-start | bytes 3538952 | tf_op jit(solution)/shard_map/ppermute | solution.py:819
  672.8 44.5 %collective-permute-start.49 = (bf16[2,2304,128]{2,1,0:T(8,128)(2,1)}, bf16[2,2304,128]{2,1,0:T(8,128)(2,1)S(1)}, u32[]{:S(2)}, u32[]{:S(2)}) collective-permute-start(bf16[2,2304,128]{2,1,0:T(8,128)(2,1)} %get-tuple-element.488), channel_id=1, source_target_pairs={{0,4},{2,6},{4,0},{6,2},{8,12},{10,14},{12,8},{14,10},{16,20},{18,... | collective-permute-start | bytes 3538952 | tf_op jit(solution)/shard_map/ppermute | solution.py:819
  673.7 43.6 %collective-permute-start.50 = (bf16[2,2304,128]{2,1,0:T(8,128)(2,1)}, bf16[2,2304,128]{2,1,0:T(8,128)(2,1)S(1)}, u32[]{:S(2)}, u32[]{:S(2)}) collective-permute-start(bf16[2,2304,128]{2,1,0:T(8,128)(2,1)} %get-tuple-element.489), channel_id=1, source_target_pairs={{0,8},{2,10},{4,12},{6,14},{8,0},{10,2},{12,4},{14,6},{16,24},{18,... | collective-permute-start | bytes 3538952 | tf_op jit(solution)/shard_map/ppermute | solution.py:819
  676.4 40.9 %collective-permute-start.51 = (bf16[1,2,2,192,512]{4,3,2,1,0:T(8,128)(2,1)}, bf16[1,2,2,192,512]{4,3,2,1,0:T(8,128)(2,1)}, u32[]{:S(2)}, u32[]{:S(2)}) collective-permute-start(bf16[1,2,2,192,512]{4,3,2,1,0:T(8,128)(2,1)} %bitcast.96), channel_id=1, source_target_pairs={{0,8},{2,10},{4,12},{6,14},{8,0},{10,2},{12,4},{14,6},{16,24},{18,... | collective-permute-start | bytes 2359304 | tf_op jit(solution)/shard_map/ppermute | solution.py:819
  676.4 40.9 %collective-permute-start.52 = (bf16[1,2,2,192,512]{4,3,2,1,0:T(8,128)(2,1)}, bf16[1,2,2,192,512]{4,3,2,1,0:T(8,128)(2,1)}, u32[]{:S(2)}, u32[]{:S(2)}) collective-permute-start(bf16[1,2,2,192,512]{4,3,2,1,0:T(8,128)(2,1)} %bitcast.98), channel_id=1, source_target_pairs={{0,4},{2,6},{4,0},{6,2},{8,12},{10,14},{12,8},{14,10},{16,20},{18,... | collective-permute-start | bytes 2359304 | tf_op jit(solution)/shard_map/ppermute | solution.py:819
  (110 other events, 1563.3 us)
Sparse Core Ops, SparseCore 0:
  69.1 75.7 all-gather.3
  159.3 22.4 all-gather.5
  210.6 39.5 all-gather.7

commit v4 on v3

--- a/solution.py
+++ b/solution.py
@@ -48,7 +48,7 @@
 def attend_kernel(q_ref, k_ref, v_ref, ck_ref, cv_ref, bias_ref, gate_ref, a_ref, o_ref, oy_ref, stat_ref):
     masks = head_masks(jnp.float32)
     rows = q_ref.shape[0]
-    step = min(rows, 256)
+    step = min(rows, 512)
     gate = gate_ref[...]
     for start in range(0, rows, step):
         where = pl.ds(start, step)
@@ -1283,15 +1283,15 @@
         grad_query, grad_key, grad_value, query_pre, key_pre, cosine, sine, gains
     )
     red_qkv = Reduction(grad_mixed[None], hm, portion_list(lanes_d, ORDERS), flow, 0.5)
-    grad_mixed, grad_cap_kv = flow.turn((red_qkv.partial,), (grad_mixed, grad_cap_kv))
+    dx_other, other_sums = project_back(
+        after(grad_mixed, red_qkv.partial), own_rows, own_rows, tokens_other, full_qkv, gains, mods
+    )
+    grad_mixed, grad_cap_kv = flow.turn((red_qkv.partial, other_sums), (grad_mixed, grad_cap_kv))
     done = red_caption.keep(grad_cap_kv[None])
-    dx_other, other_sums = project_back(
-        grad_mixed, own_rows, own_rows, tokens_other, full_qkv, gains, mods
-    )
     dx_got = []
     if nf == 2:
         flow.send(dx_other, "fsdp", 1, dx_got.append, 0)
-    (grad_mixed,) = flow.turn((done, other_sums), (grad_mixed,))
+    (grad_mixed,) = flow.turn((done,), (grad_mixed,))
     done = red_qkv.keep(grad_mixed[None])
     dx_own, own_sums = project_back(grad_mixed, 0, own_rows, tokens[0], full_qkv, gains, mods)
     project_sums = own_sums + other_sums if nf > 1 else own_sums

time: 827 us -> 812 us (0.982)
  Pallas kernels: 394 us -> 380 us
    pallas_call x1, Pallas kernels: 42.4 us -> 28.8 us  [attend(): pl.pallas_call(attend_kernel, grid=(pairs,), in_specs=[spec(rows), spec(k...]
  transfers between devices with their start and end apart: 75 -> 75, of which waited for: 28 -> 29; matrix products, arithmetic and copies ran while one was open for 7% -> 7% of each run, Pallas kernels for 41% -> 40%
where the time goes in v4:
time: 812 us; the launch traced here: 800 us
  Pallas kernels  380 us (47%)
  waiting for transfers between devices  213 us (26%)
  starting transfers between devices  71.2 us (9%)
  other arithmetic  51.9 us (6%)
  local copies, waits for them, and re-layouts  50.8 us (6%)
  matrix products  17.5 us (2%)
  between operations  15.3 us (2%)
    ppermute x72, waiting for transfers between devices, swap(): return lax.ppermute(value, axis, [(i, i ^ mask) for i in range(size)])  204 us
    ppermute x72, starting transfers between devices, swap(): return lax.ppermute(value, axis, [(i, i ^ mask) for i in range(size)])  71.1 us
    pallas_call x5, Pallas kernels, split_product(): pl.pallas_call(functools.partial(split_product_kernel, portions, count),...  59.2 us
    pallas_call x5, Pallas kernels, product(): pl.pallas_call(functools.partial(product_kernel, widths, received is not...  54.9 us
    pallas_call x4, Pallas kernels, self_back(): pl.pallas_call(self_back_kernel, grid=(count,), in_specs=[spec(rows), spe...  45 us
    pallas_call x1, Pallas kernels, project(): pl.pallas_call(functools.partial(project_kernel, len(pieces), own_rows),...  35.3 us
    pallas_call x1, Pallas kernels, ffn_back(): pl.pallas_call(ffn_back_kernel, grid_spec=pltpu.PrefetchScalarGridSpec(nu...  34.9 us
    pallas_call x2, Pallas kernels, project_back(): pl.pallas_call(functools.partial(project_back_kernel, first == 0), grid=(...  29.5 us
  transfers between devices with their start and end apart: 75, of which 29 were waited for; matrix products, arithmetic and copies ran while one was open for 7% of the time, Pallas kernels for 40%

profile of v4, /device:TPU:0, one launch (start us, length us, event | category | flops | bytes accessed | tf_op | source)
XLA Modules:
  0.0 800.2 jit_solution(14220123397848572487)
XLA Ops:
  16.6 16.6 %collective-permute-done.3 = s32[512,2]{0,1:T(2,128)S(1)} collective-permute-done((s32[512,2]{0,1:T(2,128)S(1)}, s32[512,2]{0,1:T(2,128)S(1)}, u32[]{:S(2)}, u32[]{:S(2)}) %collective-permute-start.3) | collective-permute-done | bytes 4128 | tf_op jit(solution)/shard_map/ppermute | solution.py:819
  47.7 21.3 %collective-permute-done.4 = bf16[96,8192]{1,0:T(8,128)(2,1)} collective-permute-done((bf16[96,8192]{1,0:T(8,128)(2,1)S(1)}, bf16[96,8192]{1,0:T(8,128)(2,1)}, u32[]{:S(2)}, u32[]{:S(2)}) %collective-permute-start.4) | collective-permute-done | bytes 1572896 | tf_op jit(solution)/shard_map/ppermute | solution.py:819
  78.2 25.6 %collective-permute-done.8 = bf16[2,48,4608]{2,1,0:T(8,128)(2,1)S(1)} collective-permute-done((bf16[2,48,4608]{2,1,0:T(8,128)(2,1)S(1)}, bf16[2,48,4608]{2,1,0:T(8,128)(2,1)S(1)}, u32[]{:S(2)}, u32[]{:S(2)}) %collective-permute-start.8) | collective-permute-done | bytes 884768 | tf_op jit(solution)/shard_map/ppermute | solution.py:819
  119.5 35.3 %shard_map.229 = (bf16[1024,1536]{1,0:T(8,128)(2,1)}, bf16[1536,4608]{1,0:T(8,128)(2,1)}, bf16[512,1536]{1,0:T(8,128)(2,1)}, bf16[1024,1536]{1,0:T(8,128)(2,1)},...) custom-call(s32[17]{0:T(128)} %stack.138.where_ref, ...), custom_call_target="tpu_custom_call" | custom-call | flops 603979776 | bytes 3000000 | tf_op jit(solution)/shard_map/pallas_call | solution.py:338
  165.6 28.8 %shard_map.230 = (bf16[512,1536]{1,0:T(8,128)(2,1)S(1)}, bf16[512,1536]{1,0:T(8,128)(2,1)S(1)}, bf16[512,1536]{1,0:T(8,128)(2,1)}, f32[12,8,512]{2,1,0:T(8,128)S(1)}) custom-call(bf16[512,1536]{1,0:T(8,128)(2,1)} %get-tuple-element.319.q_ref, bf16[1024,1536]{1,0:T(8,128)(2,1)} %get-tuple-element.320.k_ref, bf16[1024,1536]{1,0:T(8,128)(2,1)} %get-tuple-element.321.v_ref, ...), custom_call_target="tpu_custom_call" | custom-call | flops 805306368 | bytes 1000000 | tf_op jit(solution)/shard_map/pallas_call | solution.py:86
  206.0 21.2 %shard_map.232 = (bf16[512,4096]{1,0:T(8,128)(2,1)}, bf16[512,4096]{1,0:T(8,128)(2,1)}, bf16[512,4096]{1,0:T(8,128)(2,1)}) custom-call(s32[1]{0:T(128)} %bitcast.which_ref, bf16[512,1536]{1,0:T(8,128)(2,1)} %get-tuple-element.332.h_ref.a_ref.refs_0_.refs_1_, bf16[768,8192]{1,0:T(8,128)(2,1)} %u0_ref.3, ...), custom_call_target="tpu_custom_call" | custom-call | flops 644245120 | bytes 2000000 | tf_op jit(solution)/shard_map/pallas_call | solution.py:407
  236.6 18.2 %shard_map.233 = (bf16[512,1536]{1,0:T(8,128)(2,1)}, bf16[512,1536]{1,0:T(8,128)(2,1)}, f32[8,1536]{1,0:T(8,128)}) custom-call(s32[1]{0:T(128)} %bitcast.which_ref, bf16[512,4096]{1,0:T(8,128)(2,1)} %get-tuple-element.333.ff_ref.a_ref.refs_0_.refs_1_, bf16[2048,1536]{1,0:T(8,128)(2,1)} %d0_ref.1, ...), custom_call_target="tpu_custom_call" | custom-call | flops 322122560 | bytes 1200000 | tf_op jit(solution)/shard_map/pallas_call | solution.py:458
  265.6 17.4 %shard_map.235.d_ref.dgu_ref = bf16[2,512,4096]{2,1,0:T(8,128)(2,1)} custom-call(s32[1]{0:T(128)} %bitcast.which_ref, bf16[512,1536]{1,0:T(8,128)(2,1)} %get-tuple-element.345.df_ref, bf16[512,4096]{1,0:T(8,128)(2,1)} %get-tuple-element.340.ga_ref, bf16[512,4096]{1,0:T(8,128)(2,1)} %get-tuple-element.341.up_ref, bf16[2048,1536]{1,0:T(8,128)(2,1)} %d0_ref.1, ...), custom_call_target="tpu_custom_call" | custom-call | flops 322122560 | bytes 1500000 | tf_op jit(solution)/shard_map/pallas_call | solution.py:503
  296.6 17.2 %shard_map.237 = bf16[2,8192,384]{2,1,0:T(8,128)(2,1)} custom-call(s32[2]{0:T(128)} %pad_add_fusion.1.where_ref, bf16[2,512,4096]{2,1,0:T(8,128)(2,1)} %shard_map.235.d_ref.dgu_ref, bf16[512,1536]{1,0:T(8,128)(2,1)} %get-tuple-element.332.h_ref.a_ref.refs_0_.refs_1_), custom_call_target="tpu_custom_call" | custom-call | flops 322122560 | bytes 1258291 | tf_op jit(solution)/shard_map/pallas_call | solution.py:718
  332.1 34.9 %shard_map.238 = (f32[512,1536]{1,0:T(8,128)}, bf16[512,1536]{1,0:T(8,128)(2,1)}, bf16[512,1536]{1,0:T(8,128)(2,1)}, f32[8,1536]{1,0:T(8,128)}) custom-call(s32[1]{0:T(128)} %bitcast.which_ref, bf16[2,512,4096]{2,1,0:T(8,128)(2,1)} %shard_map.235.d_ref.dgu_ref, bf16[768,8192]{1,0:T(8,128)(2,1)} %u0_ref.3, ...), custom_call_target="tpu_custom_call" | custom-call | flops 765041024 | bytes 2750000 | tf_op jit(solution)/shard_map/pallas_call | solution.py:582
  372.8 13.7 %shard_map.239 = (bf16[512,1536]{1,0:T(8,128)(2,1)S(1)}, bf16[256,1536]{1,0:T(8,128)(2,1)S(1)}, bf16[256,1536]{1,0:T(8,128)(2,1)S(1)}, f32[1,1536]{1,0:T(1,128)S(1)}) custom-call(bf16[512,1536]{1,0:T(8,128)(2,1)} %get-tuple-element.319.q_ref, bf16[256,1536]{1,0:T(8,128)(2,1)S(1)} %multiply_convert_fusion.ck_ref, bf16[256,1536]{1,0:T(8,128)(2,1)S(1)} %slice.223.cv_ref, ...), custom_call_target="tpu_custom_call" | custom-call | flops 402653184 | bytes 450000 | tf_op jit(solution)/shard_map/pallas_call | solution.py:170
  407.9 17.4 %shard_map.241 = (bf16[8192,128]{1,0:T(8,128)(2,1)}, bf16[8192,128]{1,0:T(8,128)(2,1)}, bf16[2,4096,128]{2,1,0:T(8,128)(2,1)}, bf16[2,4096,128]{2,1,0:T(8,128)(2...) custom-call(s32[4]{0:T(128)} %pad_add_fusion.2.where_ref, ...), custom_call_target="tpu_custom_call" | custom-call | flops 322122560 | bytes 1258291 | tf_op jit(solution)/shard_map/pallas_call | solution.py:794
  425.4 11.1 %shard_map.242 = (bf16[512,384]{1,0:T(8,128)(2,1)S(1)}, bf16[1024,384]{1,0:T(8,128)(2,1)S(1)}, bf16[1024,384]{1,0:T(8,128)(2,1)S(1)}) custom-call(bf16[512,1536]{1,0:T(8,128)(2,1)S(1)} %copy-done, bf16[1024,1536]{1,0:T(8,128)(2,1)} %get-tuple-element.320.k_ref, bf16[1024,1536]{1,0:T(8,128)(2,1)} %get-tuple-element.321.v_ref, ...), custom_call_target="tpu_custom_call" | custom-call | flops 805306368 | bytes 150000 | tf_op jit(solution)/shard_map/pallas_call | solution.py:191
  462.0 11.1 %shard_map.245 = (bf16[512,384]{1,0:T(8,128)(2,1)S(1)}, bf16[1024,384]{1,0:T(8,128)(2,1)S(1)}, bf16[1024,384]{1,0:T(8,128)(2,1)S(1)}) custom-call(bf16[512,1536]{1,0:T(8,128)(2,1)S(1)} %copy-done, bf16[1024,1536]{1,0:T(8,128)(2,1)} %get-tuple-element.320.k_ref, bf16[1024,1536]{1,0:T(8,128)(2,1)} %get-tuple-element.321.v_ref, ...), custom_call_target="tpu_custom_call" | custom-call | flops 805306368 | bytes 150000 | tf_op jit(solution)/shard_map/pallas_call | solution.py:191
  474.7 11.4 %shard_map.246 = (bf16[512,384]{1,0:T(8,128)(2,1)S(1)}, bf16[1024,384]{1,0:T(8,128)(2,1)S(1)}, bf16[1024,384]{1,0:T(8,128)(2,1)S(1)}) custom-call(bf16[512,1536]{1,0:T(8,128)(2,1)S(1)} %copy-done, bf16[1024,1536]{1,0:T(8,128)(2,1)} %get-tuple-element.320.k_ref, bf16[1024,1536]{1,0:T(8,128)(2,1)} %get-tuple-element.321.v_ref, ...), custom_call_target="tpu_custom_call" | custom-call | flops 805306368 | bytes 150000 | tf_op jit(solution)/shard_map/pallas_call | solution.py:191
  487.7 11.4 %shard_map.247 = (bf16[512,384]{1,0:T(8,128)(2,1)S(1)}, bf16[1024,384]{1,0:T(8,128)(2,1)S(1)}, bf16[1024,384]{1,0:T(8,128)(2,1)S(1)}) custom-call(bf16[512,1536]{1,0:T(8,128)(2,1)S(1)} %copy-done, bf16[1024,1536]{1,0:T(8,128)(2,1)} %get-tuple-element.320.k_ref, bf16[1024,1536]{1,0:T(8,128)(2,1)} %get-tuple-element.321.v_ref, ...), custom_call_target="tpu_custom_call" | custom-call | flops 805306368 | bytes 150000 | tf_op jit(solution)/shard_map/pallas_call | solution.py:191
  515.6 13.7 %shard_map.248 = (bf16[1024,4608]{1,0:T(8,128)(2,1)}, f32[8,1536]{1,0:T(8,128)}) custom-call(bf16[512,384]{1,0:T(8,128)(2,1)} %copy-done.13, bf16[512,384]{1,0:T(8,128)(2,1)} %copy-done.14, bf16[512,384]{1,0:T(8,128)(2,1)} %copy-done.15, bf16[512,384]{1,0:T(8,128)(2,1)} %copy-done.16, bf16[1024,384]{1,0:T(8,128)(2,1)} %copy-done.5, ...), custom_call_target="tpu_custom_call" | custom-call | flops 4718592 | bytes 1500000 | tf_op jit(solution)/shard_map/pallas_call | solution.py:645
  529.3 16.7 %shard_map.249 = bf16[2,4608,384]{2,1,0:T(8,128)(2,1)} custom-call(s32[2]{0:T(128)} %pad_add_fusion.1.where_ref, bf16[1,1024,4608]{2,1,0:T(8,128)(2,1)} %bitcast.239, bf16[1024,1536]{1,0:T(8,128)(2,1)} %get-tuple-element.312.a_ref.refs_0_.refs_1_), custom_call_target="tpu_custom_call" | custom-call | flops 362387872 | bytes 707788 | tf_op jit(solution)/shard_map/pallas_call | solution.py:718
  546.0 13.4 %shard_map.250 = (bf16[512,1536]{1,0:T(8,128)(2,1)}, f32[8,1536]{1,0:T(8,128)}) custom-call(bf16[1024,4608]{1,0:T(8,128)(2,1)} %get-tuple-element.469.dqkv_ref, bf16[512,1536]{1,0:T(8,128)(2,1)} %copy-done.22, bf16[1536,4608]{1,0:T(8,128)(2,1)} %get-tuple-element.441.w_ref, f32[6,1536]{1,0:T(8,128)} %get-tuple-element.613.gain_ref.refs_16_, ...), custom_call_target="tpu_custom_call" | custom-call | flops 362387872 | bytes 1500000 | tf_op jit(solution)/shard_map/pallas_call | solution.py:681
  581.6 12.3 %collective-permute-done.40 = bf16[1,2,2,512,128]{4,3,2,1,0:T(8,128)(2,1)S(1)} collective-permute-done((bf16[1,2,2,512,128]{4,3,2,1,0:T(8,128)(2,1)S(1)}, bf16[1,2,2,512,128]{4,3,2,1,0:T(8,128)(2,1)S(1)}, u32[]{:S(2)}, u32[]{:S(2)}) %collective-permute-start.40) | collective-permute-done | bytes 524320 | tf_op jit(solution)/shard_map/ppermute | solution.py:819
  605.2 16.1 %shard_map.252 = (bf16[512,1536]{1,0:T(8,128)(2,1)}, f32[8,1536]{1,0:T(8,128)}) custom-call(bf16[1024,4608]{1,0:T(8,128)(2,1)} %get-tuple-element.469.dqkv_ref, bf16[512,1536]{1,0:T(8,128)(2,1)} %bitcast.247, bf16[1536,4608]{1,0:T(8,128)(2,1)} %get-tuple-element.441.w_ref, f32[6,1536]{1,0:T(8,128)} %get-tuple-element.613.gain_ref.refs_16_, ...), custom_call_target="tpu_custom_call" | custom-call | flops 362387872 | bytes 1500000 | tf_op jit(solution)/shard_map/pallas_call | solution.py:681
  622.2 16.2 %shard_map.253 = (bf16[4608,128]{1,0:T(8,128)(2,1)}, bf16[4608,128]{1,0:T(8,128)(2,1)}, bf16[2,2304,128]{2,1,0:T(8,128)(2,1)}, bf16[2,2304,128]{2,1,0:T(8,128)(2...) custom-call(s32[4]{0:T(128)} %pad_add_fusion.2.where_ref, bf16[1,1024,4608]{2,1,0:T(8,128)(2,1)} %bitcast.240, ...), custom_call_target="tpu_custom_call" | custom-call | flops 362387872 | bytes 707788 | tf_op jit(solution)/shard_map/pallas_call | solution.py:794
  673.2 28.6 %collective-permute-done.51 = bf16[1,2,2,192,512]{4,3,2,1,0:T(8,128)(2,1)} collective-permute-done((bf16[1,2,2,192,512]{4,3,2,1,0:T(8,128)(2,1)}, bf16[1,2,2,192,512]{4,3,2,1,0:T(8,128)(2,1)}, u32[]{:S(2)}, u32[]{:S(2)}) %collective-permute-start.51) | collective-permute-done | bytes 786464 | tf_op jit(solution)/shard_map/ppermute | solution.py:819
  765.3 18.1 %collective-permute-done.64 = f32[16,1536]{1,0:T(8,128)S(1)} collective-permute-done((f32[16,1536]{1,0:T(8,128)S(1)}, f32[16,1536]{1,0:T(8,128)S(1)}, u32[]{:S(2)}, u32[]{:S(2)}) %collective-permute-start.64) | collective-permute-done | bytes 98336 | tf_op jit(solution)/shard_map/ppermute | solution.py:819
  (428 shorter events, 337.4 us)
Async XLA Ops:
  7.2 151.9 %all-gather.4.cloned.1.call-start = ((), (), s32[]{:S(2)}) async-start(), calls=%async_computation | async-start | bytes 14155776 | tf_op jit(solution)/shard_map/all_gather | solution.py:864
  69.0 128.5 %all-gather.6.cloned.1.call-start = ((), (), s32[]{:S(2)}) async-start(), calls=%async_computation.1 | async-start | bytes 2654208 | tf_op jit(solution)/shard_map/all_gather | solution.py:864
  116.1 43.1 %collective-permute-start.12 = (bf16[256,3072]{1,0:T(8,128)(2,1)}, bf16[256,3072]{1,0:T(8,128)(2,1)}, u32[]{:S(2)}, u32[]{:S(2)}) collective-permute-start(bf16[256,3072]{1,0:T(8,128)(2,1)} %get-tuple-element.313), channel_id=1, source_target_pairs={{0,1},{1,0},{2,3},{3,2},{4,5},{5,4},{6,7},{7,6},{8,9},{9,8},{10,11... | collective-permute-start | bytes 4718600 | tf_op jit(solution)/shard_map/ppermute | solution.py:819
  116.8 42.3 %collective-permute-start.13 = (bf16[96,1536]{1,0:T(8,128)(2,1)}, bf16[96,1536]{1,0:T(8,128)(2,1)}, u32[]{:S(2)}, u32[]{:S(2)}) collective-permute-start(bf16[96,1536]{1,0:T(8,128)(2,1)} %constant_dynamic-slice_fusion.44), channel_id=1, source_target_pairs={{0,1},{1,0},{2,3},{3,2},{4,5},{5,4},{6,7},{7,6},{8,9},{9,8},{10,11... | collective-permute-start | bytes 884744 | tf_op jit(solution)/shard_map/ppermute | solution.py:819
  159.2 77.4 %all-gather.8.cloned.1.call-start = ((), (), s32[]{:S(2)}) async-start(), calls=%async_computation.2 | async-start | bytes 7077888 | tf_op jit(solution)/shard_map/all_gather | solution.py:864
  328.8 38.3 %collective-permute-start.19 = (bf16[2,8192,384]{2,1,0:T(8,128)(2,1)}, bf16[2,8192,384]{2,1,0:T(8,128)(2,1)}, u32[]{:S(2)}, u32[]{:S(2)}) collective-permute-start(bf16[2,8192,384]{2,1,0:T(8,128)(2,1)} %shard_map.237), channel_id=1, source_target_pairs={{0,2},{2,0},{4,6},{6,4},{8,10},{10,8},{12,14},{14,12},{16,18},{18,... | collective-permute-start | bytes 37748744 | tf_op jit(solution)/shard_map/ppermute | solution.py:819
  443.0 56.3 %collective-permute-start.29 = (bf16[8192,128]{1,0:T(8,128)(2,1)}, bf16[8192,128]{1,0:T(8,128)(2,1)}, u32[]{:S(2)}, u32[]{:S(2)}) collective-permute-start(bf16[8192,128]{1,0:T(8,128)(2,1)} %get-tuple-element.409), channel_id=1, source_target_pairs={{0,1},{1,0},{2,3},{3,2},{4,5},{5,4},{6,7},{7,6},{8,9},{9,8},{10,11... | collective-permute-start | bytes 6291464 | tf_op jit(solution)/shard_map/ppermute | solution.py:819
  444.4 54.8 %collective-permute-start.30 = (bf16[2,4096,128]{2,1,0:T(8,128)(2,1)}, bf16[2,4096,128]{2,1,0:T(8,128)(2,1)}, u32[]{:S(2)}, u32[]{:S(2)}) collective-permute-start(bf16[2,4096,128]{2,1,0:T(8,128)(2,1)} %get-tuple-element.410), channel_id=1, source_target_pairs={{0,4},{2,6},{4,0},{6,2},{8,12},{10,14},{12,8},{14,10},{16,20},{18,... | collective-permute-start | bytes 6291464 | tf_op jit(solution)/shard_map/ppermute | solution.py:819
  445.9 53.4 %collective-permute-start.31 = (bf16[2,4096,128]{2,1,0:T(8,128)(2,1)}, bf16[2,4096,128]{2,1,0:T(8,128)(2,1)}, u32[]{:S(2)}, u32[]{:S(2)}) collective-permute-start(bf16[2,4096,128]{2,1,0:T(8,128)(2,1)} %get-tuple-element.411), channel_id=1, source_target_pairs={{0,8},{2,10},{4,12},{6,14},{8,0},{10,2},{12,4},{14,6},{16,24},{18,... | collective-permute-start | bytes 6291464 | tf_op jit(solution)/shard_map/ppermute | solution.py:819
  446.5 52.7 %collective-permute-start.32 = (bf16[96,1024]{1,0:T(8,128)(2,1)S(1)}, bf16[96,1024]{1,0:T(8,128)(2,1)S(1)}, u32[]{:S(2)}, u32[]{:S(2)}) collective-permute-start(bf16[96,1024]{1,0:T(8,128)(2,1)S(1)} %get-tuple-element.412), channel_id=1, source_target_pairs={{0,2},{2,0},{4,6},{6,4},{8,10},{10,8},{12,14},{14,12},{16,18},{18,... | collective-permute-start | bytes 589832 | tf_op jit(solution)/shard_map/ppermute | solution.py:819
  511.4 51.1 %collective-permute-start.33 = (bf16[1,3072,1024]{2,1,0:T(8,128)(2,1)}, bf16[1,3072,1024]{2,1,0:T(8,128)(2,1)}, u32[]{:S(2)}, u32[]{:S(2)}) collective-permute-start(bf16[1,3072,1024]{2,1,0:T(8,128)(2,1)} %shard_map.243), channel_id=1, source_target_pairs={{0,2},{2,0},{4,6},{6,4},{8,10},{10,8},{12,14},{14,12},{16,18},{18,... | collective-permute-start | bytes 18874376 | tf_op jit(solution)/shard_map/ppermute | solution.py:819
  511.9 50.6 %collective-permute-start.37 = (bf16[2,768,384]{2,1,0:T(8,128)(2,1)}, bf16[2,768,384]{2,1,0:T(8,128)(2,1)S(1)}, u32[]{:S(2)}, u32[]{:S(2)}) collective-permute-start(bf16[2,768,384]{2,1,0:T(8,128)(2,1)} %get-tuple-element.447), channel_id=1, source_target_pairs={{0,8},{2,10},{4,12},{6,14},{8,0},{10,2},{12,4},{14,6},{16,24},{18,... | collective-permute-start | bytes 3538952 | tf_op jit(solution)/shard_map/ppermute | solution.py:819
  513.4 46.1 %collective-permute-start.34 = (bf16[1,2,2,2,512,128]{5,4,3,2,1,0:T(8,128)(2,1)}, bf16[1,2,2,2,512,128]{5,4,3,2,1,0:T(8,128)(2,1)S(1)}, u32[]{:S(2)}, u32[]{:S(2)}) collective-permute-start(bf16[1,2,2,2,512,128]{5,4,3,2,1,0:T(8,128)(2,1)} %bitcast.66), channel_id=1, source_target_pairs={{0,4},{2,6},{4,0},{6,2},{8,12},{10,14},{12,8},{14,10},{16,20},{18,... | collective-permute-start | bytes 3145736 | tf_op jit(solution)/shard_map/ppermute | solution.py:819
  513.9 48.6 %collective-permute-start.35 = (bf16[2,2,2,512,128]{4,3,2,1,0:T(8,128)(2,1)}, bf16[2,2,2,512,128]{4,3,2,1,0:T(8,128)(2,1)S(1)}, u32[]{:S(2)}, u32[]{:S(2)}) collective-permute-start(bf16[2,2,2,512,128]{4,3,2,1,0:T(8,128)(2,1)} %bitcast.68), channel_id=1, source_target_pairs={{0,8},{2,10},{4,12},{6,14},{8,0},{10,2},{12,4},{14,6},{16,24},{18,... | collective-permute-start | bytes 3145736 | tf_op jit(solution)/shard_map/ppermute | solution.py:819
  515.1 47.4 %collective-permute-start.36 = (bf16[1,2,2,2,512,128]{5,4,3,2,1,0:T(8,128)(2,1)}, bf16[1,2,2,2,512,128]{5,4,3,2,1,0:T(8,128)(2,1)}, u32[]{:S(2)}, u32[]{:S(2)}) collective-permute-start(bf16[1,2,2,2,512,128]{5,4,3,2,1,0:T(8,128)(2,1)} %slice_bitcast_fusion.1), channel_id=1, source_target_pairs={{0,1},{1,0},{2,3},{3,2},{4,5},{5,4},{6,7},{7,6},{8,9},{9,8},{10,11... | collective-permute-start | bytes 3145736 | tf_op jit(solution)/shard_map/ppermute | solution.py:819
  596.7 52.7 %collective-permute-start.43 = (bf16[512,1536]{1,0:T(8,128)(2,1)}, bf16[512,1536]{1,0:T(8,128)(2,1)}, u32[]{:S(2)}, u32[]{:S(2)}) collective-permute-start(bf16[512,1536]{1,0:T(8,128)(2,1)} %get-tuple-element.471), channel_id=1, source_target_pairs={{0,1},{1,0},{2,3},{3,2},{4,5},{5,4},{6,7},{7,6},{8,9},{9,8},{10,11... | collective-permute-start | bytes 4718600 | tf_op jit(solution)/shard_map/ppermute | solution.py:819
  597.3 52.1 %collective-permute-start.45 = (bf16[1,1536,512]{2,1,0:T(8,128)(2,1)}, bf16[1,1536,512]{2,1,0:T(8,128)(2,1)}, u32[]{:S(2)}, u32[]{:S(2)}) collective-permute-start(bf16[1,1536,512]{2,1,0:T(8,128)(2,1)} %get-tuple-element.473), channel_id=1, source_target_pairs={{0,4},{2,6},{4,0},{6,2},{8,12},{10,14},{12,8},{14,10},{16,20},{18,... | collective-permute-start | bytes 4718600 | tf_op jit(solution)/shard_map/ppermute | solution.py:819
  598.4 52.5 %collective-permute-start.46 = (bf16[1,1536,512]{2,1,0:T(8,128)(2,1)}, bf16[1,1536,512]{2,1,0:T(8,128)(2,1)S(1)}, u32[]{:S(2)}, u32[]{:S(2)}) collective-permute-start(bf16[1,1536,512]{2,1,0:T(8,128)(2,1)} %get-tuple-element.474), channel_id=1, source_target_pairs={{0,8},{2,10},{4,12},{6,14},{8,0},{10,2},{12,4},{14,6},{16,24},{18,... | collective-permute-start | bytes 4718600 | tf_op jit(solution)/shard_map/ppermute | solution.py:819
  599.3 50.1 %collective-permute-start.44 = (bf16[1,2,512,384]{3,2,1,0:T(8,128)(2,1)}, bf16[1,2,512,384]{3,2,1,0:T(8,128)(2,1)S(1)}, u32[]{:S(2)}, u32[]{:S(2)}) collective-permute-start(bf16[1,2,512,384]{3,2,1,0:T(8,128)(2,1)} %bitcast.89), channel_id=1, source_target_pairs={{0,16},{2,18},{4,20},{6,22},{8,24},{10,26},{12,28},{14,30},{16,0},... | collective-permute-start | bytes 2359304 | tf_op jit(solution)/shard_map/ppermute | solution.py:819
  655.8 46.0 %collective-permute-start.48 = (bf16[4608,128]{1,0:T(8,128)(2,1)}, bf16[4608,128]{1,0:T(8,128)(2,1)}, u32[]{:S(2)}, u32[]{:S(2)}) collective-permute-start(bf16[4608,128]{1,0:T(8,128)(2,1)} %get-tuple-element.489), channel_id=1, source_target_pairs={{0,1},{1,0},{2,3},{3,2},{4,5},{5,4},{6,7},{7,6},{8,9},{9,8},{10,11... | collective-permute-start | bytes 3538952 | tf_op jit(solution)/shard_map/ppermute | solution.py:819
  657.3 44.5 %collective-permute-start.49 = (bf16[2,2304,128]{2,1,0:T(8,128)(2,1)}, bf16[2,2304,128]{2,1,0:T(8,128)(2,1)S(1)}, u32[]{:S(2)}, u32[]{:S(2)}) collective-permute-start(bf16[2,2304,128]{2,1,0:T(8,128)(2,1)} %get-tuple-element.490), channel_id=1, source_target_pairs={{0,4},{2,6},{4,0},{6,2},{8,12},{10,14},{12,8},{14,10},{16,20},{18,... | collective-permute-start | bytes 3538952 | tf_op jit(solution)/shard_map/ppermute | solution.py:819
  658.2 43.6 %collective-permute-start.50 = (bf16[2,2304,128]{2,1,0:T(8,128)(2,1)}, bf16[2,2304,128]{2,1,0:T(8,128)(2,1)S(1)}, u32[]{:S(2)}, u32[]{:S(2)}) collective-permute-start(bf16[2,2304,128]{2,1,0:T(8,128)(2,1)} %get-tuple-element.491), channel_id=1, source_target_pairs={{0,8},{2,10},{4,12},{6,14},{8,0},{10,2},{12,4},{14,6},{16,24},{18,... | collective-permute-start | bytes 3538952 | tf_op jit(solution)/shard_map/ppermute | solution.py:819
  660.9 40.9 %collective-permute-start.51 = (bf16[1,2,2,192,512]{4,3,2,1,0:T(8,128)(2,1)}, bf16[1,2,2,192,512]{4,3,2,1,0:T(8,128)(2,1)}, u32[]{:S(2)}, u32[]{:S(2)}) collective-permute-start(bf16[1,2,2,192,512]{4,3,2,1,0:T(8,128)(2,1)} %bitcast.96), channel_id=1, source_target_pairs={{0,8},{2,10},{4,12},{6,14},{8,0},{10,2},{12,4},{14,6},{16,24},{18,... | collective-permute-start | bytes 2359304 | tf_op jit(solution)/shard_map/ppermute | solution.py:819
  660.9 40.9 %collective-permute-start.52 = (bf16[1,2,2,192,512]{4,3,2,1,0:T(8,128)(2,1)}, bf16[1,2,2,192,512]{4,3,2,1,0:T(8,128)(2,1)}, u32[]{:S(2)}, u32[]{:S(2)}) collective-permute-start(bf16[1,2,2,192,512]{4,3,2,1,0:T(8,128)(2,1)} %bitcast.98), channel_id=1, source_target_pairs={{0,4},{2,6},{4,0},{6,2},{8,12},{10,14},{12,8},{14,10},{16,20},{18,... | collective-permute-start | bytes 2359304 | tf_op jit(solution)/shard_map/ppermute | solution.py:819
  (110 other events, 1553.3 us)
Sparse Core Ops, SparseCore 0:
  69.1 75.7 all-gather.3
  159.3 22.4 all-gather.5
  196.9 39.5 all-gather.7
